TPU v7x, 128 devices: a whole 4x4x4 slice. The times are simulated.
128 devices in a mesh: inline: 16 (over z, x), crosslin: 8 (over y, core).
Axes of the slice: x: 4, y: 4, z: 4, core: 2. Of those that a mesh axis runs over, the one named last changes fastest.
Arguments:
- amplitudes: bfloat16 [16, 4096, 8192], P(None, 'inline', 'crosslin'), may hold values from -6 to 6
- pick_mask: int32 [4096, 8192], P('inline', 'crosslin'), may hold values 0 or 1
- pick_depth: int32 [4096, 8192], P('inline', 'crosslin'), may hold values from 0 to 15
- iterate: float32 [4096, 8192], P('inline', 'crosslin'), may hold values from -60 to 60
Outputs:
- new_iterate: float32 [4096, 8192], P('inline', 'crosslin')
- new_residual: float32 [4096, 8192], P('inline', 'crosslin')
- new_direction: float32 [4096, 8192], P('inline', 'crosslin')
All inputs are finite; a program needn't handle non-finite values. No bound on the sum of `pick_mask` on one device may be relied on, other than what follows from the above.
Results may differ from a plain program's by a relative error of at most 0.0022.
Values may be sent and summed in bfloat16 or wider, within the bound.
No kernel may reach another device: no remote copies, remote signals or barrier semaphores. Data moves between devices by JAX's collectives and lax.ppermute only.
A program may use at most 128 MiB of HBM per device.

v0:
```python
import functools

import jax
import jax.numpy as jnp
import ml_dtypes
import numpy as np
from jax import lax
from jax.experimental import pallas as pl
from jax.experimental.pallas import tpu as pltpu
from jax.sharding import PartitionSpec as P

K = 16
DEC = 8
CI = 32
COUPLING = 4.0
F32 = jnp.float32
BF16 = jnp.bfloat16
NPB = ml_dtypes.bfloat16
VMEM = pltpu.VMEM

RD = 256
CD = 1024
ER = RD + 32
EC = CD + 256
CR = RD // DEC
CC = CD // DEC
MSG = 64
LIMIT = 56 * 1024 * 1024


def dot(a, b):
    return jnp.dot(a, b, preferred_element_type=F32)


def parts2(x):
    hi = x.astype(BF16)
    return hi, (x - hi.astype(F32)).astype(BF16)


def parts3(x):
    hi = x.astype(BF16)
    rest = x - hi.astype(F32)
    mid = rest.astype(BF16)
    return hi, mid, (rest - mid.astype(F32)).astype(BF16)


def np2(x):
    hi = x.astype(np.float32).astype(NPB)
    return hi, (x - hi.astype(np.float64)).astype(np.float32).astype(NPB)


def line_tables():
    sel = np.zeros((2, 21, 128, 128), np.float32)
    for s in range(K):
        for k in range(3):
            sel[0, s, k, 3 * s + k] = 1
            sel[1, s, 125 + k, 3 * s + k] = 1
    for part in range(3):
        for l in range(2):
            sel[0, 16 + part, l, 48 + 3 * l + part] = 1
            sel[1, 16 + part, 126 + l, 48 + 3 * l + part] = 1
    for o in range(2):
        sel[0, 19 + o, 0, 54 + o] = 1
        sel[1, 19 + o, 127, 54 + o] = 1
    place = np.zeros((2, 128, 19 * 128), np.float32)
    for side in range(2):
        for s in range(K):
            place[side, :, s * 128 : s * 128 + 128] = sel[side, s].T
        place[side, :, 2048:2176] = sel[side, 16:19].sum(0).T
        place[side, :, 2176:2304] = sel[side, 19].T
        place[side, :, 2304:2432] = sel[side, 20].T
    rows = np.zeros((2, MSG, 256), np.float32)
    put = np.zeros((2, 304, MSG), np.float32)
    for s in range(K):
        for k in range(3):
            rows[0, 3 * s + k, 16 * s + k] = 1
            rows[1, 3 * s + k, 16 * s + 13 + k] = 1
    for side in range(2):
        put[side, :256] = rows[side].T
        for l in range(2):
            for part in range(3):
                put[side, 256 + (14 + l if side else l), 48 + 3 * l + part] = 1
        put[side, 272 + (15 if side else 0), 54] = 1
        put[side, 288 + (15 if side else 0), 55] = 1
    mix = np.zeros((2, 3, MSG, 128), np.float32)
    for k in range(3):
        for s in range(K):
            mix[:, k, 3 * s + k, 3 * s : 3 * s + 3] = 1
    for l in range(2):
        for part in range(3):
            for other in range(2):
                mix[0, l, 48 + 3 * l + part, 48 + 3 * other + part] = 1
                mix[1, l + 1, 48 + 3 * l + part, 48 + 3 * other + part] = 1
    for o in (54, 55):
        mix[0, 0, o, o] = 1
        mix[1, 2, o, o] = 1
    lanes = sel.sum(1).transpose(0, 2, 1)
    return tuple(t.astype(NPB) for t in (sel, place, rows, put, mix, lanes))


def coarse_tables(n_in, n_cr):
    n = CC * n_cr
    freq = np.arange(n, dtype=np.float64)
    norm = np.where(freq == 0, np.sqrt(1.0 / n), np.sqrt(2.0 / n))

    def cosines(cols):
        phase = (freq[:, None] * (2 * cols[None, :] + 1)) % (4 * n)
        return norm[:, None] * np.cos(np.pi * phase / (2 * n))

    forward = cosines(np.arange(n, dtype=np.float64)).T
    back = np.zeros((n_cr, n, 2 * CC))
    for j in range(n_cr):
        cols = np.zeros(2 * CC)
        cols[:CC] = j * CC + np.arange(CC)
        cols[CC] = j * CC - 1
        cols[CC + 1] = j * CC + CC
        back[j] = cosines(cols)
        back[j, :, CC + 2 :] = 0
    half = (2.0 - 2.0 * np.cos(np.pi * freq / n) + 1.0 / (CI * CI)) / 2.0
    kappa = np.log1p(half + np.sqrt(half * (half + 2.0)))
    scale = 1.0 / (COUPLING * 2.0 * np.sinh(kappa))
    steps = np.stack([np.exp(-kappa * d) for d in (1, 2, 4, 8, 16)] + [scale] + [scale * 0] * 2)
    at = np.arange(40)[:, None]
    grow = scale * np.exp(-kappa * at) * (at < 34)
    fall = scale * np.exp(-kappa * (33.0 - at)) * (at < 34)
    whole = CR * n_in
    blocks = np.stack(
        [
            np.exp(-kappa * CR),
            np.exp(-kappa * whole),
            1.0 / (1.0 - np.exp(-kappa * 2 * whole)),
            scale * np.exp(-kappa),
        ]
    ).reshape(4, n_cr, 128)
    spread = np.zeros((2 * CC, EC))
    for lane in range(EC):
        col = (lane - 128) // DEC
        if -1 <= col <= CC:
            spread[{-1: CC, CC: CC + 1}.get(col, col), lane] = 1
    group = np.zeros((CD, CC))
    group[np.arange(CD), np.arange(CD) // DEC] = 1
    f = np.float32
    return dict(
        forward=np2(forward), back=np2(back), steps=steps.astype(f), grow=grow.astype(f),
        fall=fall.astype(f), blocks=blocks.astype(f), spread=spread.astype(NPB), group=group.astype(NPB),
    )


def pack_columns_kernel(a0, a1, v0, v1, m0, m1, d0, d1, sel, out0, out1):
    for side, (a, v, m, d, out) in enumerate(((a0, v0, m0, d0, out0), (a1, v1, m1, d1, out1))):
        weight = m[...].astype(F32)
        source = weight * (d[...].astype(F32) - 0.5 * (K - 1))
        total = jnp.zeros((RD, 128), F32)
        for s in range(K):
            total += dot(a[s], sel[side, s])
        for i, part in enumerate(parts3(v[...]) + (weight.astype(BF16), source.astype(BF16))):
            total += dot(part, sel[side, 16 + i])
        out[...] = total.astype(BF16)


def pack_columns(amplitudes, iterate, mask, depth, sel):
    last = CD // 128 - 1
    cube = [pl.BlockSpec((K, RD, 128), lambda i, c=c: (0, 0, c)) for c in (0, last)]
    flat = [pl.BlockSpec((RD, 128), lambda i, c=c: (0, c)) for c in (0, last)]
    whole = pl.BlockSpec(sel.shape, lambda i: (0, 0, 0, 0))
    out = jax.ShapeDtypeStruct((RD, 128), BF16)
    return pl.pallas_call(
        pack_columns_kernel, grid=(1,), in_specs=cube + flat * 3 + [whole],
        out_specs=[pl.BlockSpec((RD, 128), lambda i: (0, 0))] * 2, out_shape=[out, out],
        compiler_params=pltpu.CompilerParams(vmem_limit_bytes=32 * 1024 * 1024),
        cost_estimate=pl.CostEstimate(flops=10**8, bytes_accessed=3 * 10**6, transcendentals=0),
        name="pack_columns",
    )(amplitudes, amplitudes, iterate, iterate, mask, mask, depth, depth, sel)


def pack_rows_kernel(a0, a1, v0, v1, m0, m1, d0, d1, left, right, rows, mix, lanes, out0, out1):
    at = lax.broadcasted_iota(jnp.int32, (MSG, CD), 0)
    for side, (a, v, m, d, out) in enumerate(((a0, v0, m0, d0, out0), (a1, v1, m1, d1, out1))):
        middle = dot(rows[side], a[...].reshape(K * 16, CD))
        split = [p.astype(F32) for p in parts3(v[...])]
        for l in range(2):
            row = 6 + l if side else l
            for part in range(3):
                middle = jnp.where(at == 48 + 3 * l + part, split[part][row : row + 1], middle)
        row = 7 if side else 0
        weight = m[row : row + 1].astype(F32)
        source = weight * (d[row : row + 1].astype(F32) - 0.5 * (K - 1))
        middle = jnp.where(at == 54, weight, jnp.where(at == 55, source, middle))
        out[:, 128 : 128 + CD] = middle.astype(BF16)
        for tile, halo, which in ((0, left, 1), (128 + CD, right, 0)):
            total = jnp.zeros((MSG, 128), F32)
            edge = halo[RD - 16 : RD].astype(F32)[13:16] if side else halo[0:16].astype(F32)[0:3]
            for k in range(3):
                term = mix[side, k].astype(F32) * edge[k : k + 1]
                total += dot(term.astype(BF16), lanes[which])
            out[:, tile : tile + 128] = total.astype(BF16)


def pack_rows(amplitudes, iterate, mask, depth, left, right, rows, mix, lanes):
    cube = [pl.BlockSpec((K, 16, CD), lambda i, c=c: (0, c, 0)) for c in (0, RD // 16 - 1)]
    flat = [pl.BlockSpec((8, CD), lambda i, c=c: (c, 0)) for c in (0, RD // 8 - 1)]
    full = [pl.BlockSpec(t.shape, lambda i, n=t.ndim: (0,) * n) for t in (left, right, rows, mix, lanes)]
    out = jax.ShapeDtypeStruct((MSG, EC), BF16)
    return pl.pallas_call(
        pack_rows_kernel, grid=(1,), in_specs=cube + flat * 3 + full,
        out_specs=[pl.BlockSpec((MSG, EC), lambda i: (0, 0))] * 2, out_shape=[out, out],
        compiler_params=pltpu.CompilerParams(vmem_limit_bytes=32 * 1024 * 1024),
        cost_estimate=pl.CostEstimate(flops=10**8, bytes_accessed=2 * 10**6, transcendentals=0),
        name="pack_rows",
    )(amplitudes, amplitudes, iterate, iterate, mask, mask, depth, depth, left, right, rows, mix, lanes)


def block_sums(rows, group):
    return sum(dot(part, group) for part in parts3(rows))


def tensor_kernel(
    n_in, n_cr, pos, amp, v_in, mask, depth, up, down, left, right, put, place, group,
    ta_o, tb_o, tc_o, z_o, r_o, rd_o, blocks_o, sums_o,
    ext, v_ext, w_ext, s_ext, fd, fr, rowsum, sems,
):
    inner = (slice(16, 16 + RD), slice(128, 128 + CD))
    copies = [
        pltpu.make_async_copy(amp, ext.at[:, 16 : 16 + RD, 128 : 128 + CD], sems.at[0]),
        pltpu.make_async_copy(v_in, v_ext.at[16 : 16 + RD, 128 : 128 + CD], sems.at[1]),
    ]
    for c in copies:
        c.start()
    weight = mask[...].astype(F32)
    w_ext[inner] = weight
    s_ext[inner] = weight * (depth[...].astype(F32) - 0.5 * (K - 1))
    for side, halo, lane in ((1, left, 0), (0, right, 128 + CD)):
        tile = dot(halo[...], place[side])
        for s in range(K):
            ext[s, 16 : 16 + RD, lane : lane + 128] = tile[:, s * 128 : s * 128 + 128].astype(BF16)
        v_ext[16 : 16 + RD, lane : lane + 128] = tile[:, 2048:2176]
        w_ext[16 : 16 + RD, lane : lane + 128] = tile[:, 2176:2304]
        s_ext[16 : 16 + RD, lane : lane + 128] = tile[:, 2304:2432]
    for side, halo, row in ((1, up, 0), (0, down, 16 + RD)):
        lines = dot(put[side], halo[...])
        for s in range(K):
            ext[s, row : row + 16, :] = lines[16 * s : 16 * s + 16].astype(BF16)
        v_ext[row : row + 16, :] = lines[256:272]
        w_ext[row : row + 16, :] = lines[272:288]
        s_ext[row : row + 16, :] = lines[288:304]
    for c in copies:
        c.wait()
    first_row = pos[0] * RD - 16
    col = pos[1] * CD - 128 + lax.broadcasted_iota(jnp.int32, (8, EC), 1)
    valid_right = ((col >= 0) & (col < n_cr * CD - 1)).astype(F32)
    row_iota = lax.broadcasted_iota(jnp.int32, (8, EC), 0)

    def left_of(x):
        return pltpu.roll(x, 1, 1)

    def right_of(x):
        return pltpu.roll(x, EC - 1, 1)

    def tensors(t, carry):
        for half in range(2):
            at = pl.multiple_of(16 * t + 8 + 8 * half, 8)
            sii = jnp.zeros((8, EC), F32)
            sic = jnp.zeros((8, EC), F32)
            scc = jnp.zeros((8, EC), F32)
            for s in range(K):
                x = ext[s, pl.ds(pl.multiple_of(16 * t, 16), 32), :].astype(F32)
                lo = 8 + 8 * half
                middle = x[lo : lo + 8]
                gi = x[lo + 1 : lo + 9] - x[lo - 1 : lo + 7]
                gc = right_of(middle) - left_of(middle)
                sii += gi * gi
                sic += gi * gc
                scc += gc * gc
            sii, sic, scc = 0.25 * sii, 0.25 * sic, 0.25 * scc
            inv = 1.0 / (sii + scc + 2.0)
            row = first_row + at + row_iota
            valid_down = ((row >= 0) & (row < n_in * RD - 1)).astype(F32)
            ta = valid_down * ((scc + 1.0) * inv)
            tb = (valid_down * valid_right) * (-sic * inv)
            tc = valid_right * ((sii + 1.0) * inv)
            value = v_ext[pl.ds(at, 16), :]
            here = value[0:8]
            dd = value[1:9] - here
            dr = right_of(here) - here
            ta_o[pl.ds(at, 8), :] = ta
            tb_o[pl.ds(at, 8), :] = tb
            tc_o[pl.ds(at, 8), :] = tc
            fd[pl.ds(at, 8), :] = ta * dd + tb * dr
            fr[pl.ds(at, 8), :] = tb * dd + tc * dr
        return carry

    lax.fori_loop(0, ER // 16 - 1, tensors, 0)

    def residuals(at):
        before = pl.ds(pl.multiple_of(at - 8, 8), 16)
        here = pl.ds(at, 8)
        fdw, taw = fd[before, :], ta_o[before, :]
        tc, right_flux, weight = tc_o[here, :], fr[here, :], w_ext[here, :]
        image = fdw[7:15] - fdw[8:16] + left_of(right_flux) - right_flux + weight * v_ext[here, :]
        r = s_ext[here, :] - image
        diag = taw[8:16] + 2.0 * tb_o[here, :] + tc + taw[7:15] + left_of(tc) + weight
        inv = jnp.where(diag != 0.0, 1.0 / diag, 0.0)
        z = r * inv
        z_o[here, :] = z
        return r, inv, z

    def own(e, total):
        at = pl.multiple_of(16 + 8 * e, 8)
        r, inv, z = residuals(at)
        r, inv, z = r[:, 128 : 128 + CD], inv[:, 128 : 128 + CD], z[:, 128 : 128 + CD]
        to = pl.ds(pl.multiple_of(8 * e, 8), 8)
        r_o[to, :] = r
        rd_o[to, :] = inv
        rowsum[pl.ds(e, 1), :] = jnp.sum(r, axis=0, keepdims=True)
        return total + r * z

    residuals(8)
    residuals(16 + RD)
    total = lax.fori_loop(0, CR, own, jnp.zeros((8, CD), F32))
    sums_o[...] = sum(total[:, k * 128 : k * 128 + 128] for k in range(CD // 128))
    sums = block_sums(rowsum[...], group[...])
    for j in range(n_cr):
        blocks_o[j] = sums


def tensor_stage(n_in, n_cr, pos, amp, v, mask, depth, up, down, left, right, put, place, group):
    vmem = pl.BlockSpec(memory_space=VMEM)
    anyw = pl.BlockSpec(memory_space=pl.ANY)
    ext = jax.ShapeDtypeStruct((ER, EC), F32)
    flat = jax.ShapeDtypeStruct((RD, CD), F32)
    return pl.pallas_call(
        functools.partial(tensor_kernel, n_in, n_cr),
        in_specs=[pl.BlockSpec(memory_space=pltpu.SMEM), anyw, anyw] + [vmem] * 9,
        out_specs=[vmem] * 8,
        out_shape=[
            ext, ext, ext, ext, flat, flat,
            jax.ShapeDtypeStruct((n_cr, CR, CC), F32),
            jax.ShapeDtypeStruct((8, 128), F32),
        ],
        scratch_shapes=[
            VMEM((K, ER, EC), BF16), VMEM((ER, EC), F32), VMEM((ER, EC), F32), VMEM((ER, EC), F32),
            VMEM((ER, EC), F32), VMEM((ER, EC), F32), VMEM((CR, CD), F32), pltpu.SemaphoreType.DMA((2,)),
        ],
        compiler_params=pltpu.CompilerParams(vmem_limit_bytes=LIMIT),
        cost_estimate=pl.CostEstimate(flops=10**8, bytes_accessed=2 * 10**7, transcendentals=0),
        name="tensor_stage",
    )(pos, amp, v, mask, depth, up, down, left, right, put, place, group)


def moments_kernel(n_in, n_cr, extra, blocks, fwd_hi, fwd_lo, steps, pay_o, own_o):
    x = jnp.concatenate([blocks[j, :CR] for j in range(n_cr)], axis=1)
    hi, lo = parts2(x)
    both = dot(jnp.concatenate([hi, lo], axis=0), fwd_hi[...])
    x = both[:CR] + both[CR:] + dot(hi, fwd_lo[...])
    width = x.shape[1]
    forth, back = x, x
    for i in range(5):
        d = 1 << i
        zero = jnp.zeros((d, width), F32)
        decay = steps[i : i + 1]
        forth = forth + decay * jnp.concatenate([zero, forth[:-d]], axis=0)
        back = back + decay * jnp.concatenate([back[d:], zero], axis=0)
    decay, scale = steps[0:1], steps[5:6]
    zero = jnp.zeros((1, width), F32)
    inside = forth + decay * jnp.concatenate([back[1:], zero], axis=0)
    inside = scale * inside
    own_o[...] = jnp.concatenate(
        [scale * decay * back[0:1], inside, scale * decay * forth[CR - 1 :], jnp.zeros((6, width), F32)],
        axis=0,
    )
    f = jnp.concatenate([forth[CR - 1 :, 128 * k : 128 * k + 128] for k in range(n_cr)], axis=0)
    b = jnp.concatenate([back[0:1, 128 * k : 128 * k + 128] for k in range(n_cr)], axis=0)
    for i in range(n_in):
        pay_o[i, 0:n_cr] = f
        pay_o[i, n_cr : 2 * n_cr] = b
    if extra:
        sums = sum(blocks[j, CR : CR + 8] for j in range(n_cr))
        energy = jnp.sum(x * inside, axis=0, keepdims=True)
        energy = sum(energy[:, 128 * k : 128 * k + 128] for k in range(n_cr))
        at = lax.broadcasted_iota(jnp.int32, (8, 128), 0)
        sums = jnp.where(at == 3, energy, sums)
        for i in range(n_in):
            pay_o[i, 2 * n_cr : 2 * n_cr + 8] = sums


def moments_stage(n_in, n_cr, extra, blocks, fwd_hi, fwd_lo, steps):
    vmem = pl.BlockSpec(memory_space=VMEM)
    return pl.pallas_call(
        functools.partial(moments_kernel, n_in, n_cr, extra),
        in_specs=[vmem] * 4, out_specs=[vmem] * 2,
        out_shape=[
            jax.ShapeDtypeStruct((n_in, 2 * n_cr + 8 * extra, 128), F32),
            jax.ShapeDtypeStruct((40, CC * n_cr), F32),
        ],
        compiler_params=pltpu.CompilerParams(vmem_limit_bytes=32 * 1024 * 1024),
        cost_estimate=pl.CostEstimate(flops=2 * 10**8, bytes_accessed=5 * 10**6, transcendentals=0),
        name="moments_stage",
    )(blocks, fwd_hi, fwd_lo, steps)


def coarse_values(n_in, n_cr, mine, moments, own, grow, fall, blocks, back_hi, back_lo, spread):
    r32, whole, series, link = (blocks[i] for i in range(4))
    f = [moments[i, 0:n_cr] for i in range(n_in)]
    b = [moments[i, n_cr : 2 * n_cr] for i in range(n_in)]
    hf, hb = f[0], b[n_in - 1]
    for i in range(1, n_in):
        hf = r32 * hf + f[i]
        hb = r32 * hb + b[n_in - 1 - i]
    above = (hb + whole * hf) * series
    below = (hf + whole * hb) * series
    mine_above, mine_below = jnp.zeros_like(above), jnp.zeros_like(below)
    energy = jnp.zeros_like(above)
    for i in range(n_in):
        k = n_in - 1 - i
        mine_above = jnp.where(mine == i, above, mine_above)
        mine_below = jnp.where(mine == k, below, mine_below)
        energy += above * b[i] + below * f[k]
        above = r32 * above + f[i]
        below = r32 * below + b[k]
    energy = energy * link
    a_row = jnp.concatenate([mine_above[k : k + 1] for k in range(n_cr)], axis=1)
    b_row = jnp.concatenate([mine_below[k : k + 1] for k in range(n_cr)], axis=1)
    u = own[...] + a_row * grow[...] + b_row * fall[...]
    hi, lo = parts2(u)
    both = dot(jnp.concatenate([hi, lo], axis=0), back_hi[0])
    values = both[:40] + both[40:] + dot(hi, back_lo[0])
    three = dot(jnp.concatenate(parts3(values), axis=0), spread[...])
    return values, three[:40] + three[40:80] + three[80:], energy


def image_kernel(
    n_in, n_cr, pos, moments, own, grow, fall, blocks, back_hi, back_lo, spread, group,
    ta, tb, tc, z, r, rd, mask, first_blocks, first_sums,
    p_o, q_o, blocks_o, p_ext, fd, fr, rowsum, cs,
):
    values, spread_rows, _ = coarse_values(
        n_in, n_cr, pos[0], moments, own, grow, fall, blocks, back_hi, back_lo, spread
    )
    cs[...] = spread_rows

    def fields(e, carry):
        at = pl.ds(pl.multiple_of(8 + 8 * e, 8), 8)
        p_ext[at, :] = z[at, :] + cs[pl.ds(e, 1), :]
        return carry

    lax.fori_loop(0, CR + 2, fields, 0)

    def fluxes(e, carry):
        at = pl.multiple_of(8 + 8 * e, 8)
        value = p_ext[pl.ds(at, 16), :]
        here = value[0:8]
        dd = value[1:9] - here
        dr = pltpu.roll(here, EC - 1, 1) - here
        at = pl.ds(at, 8)
        b = tb[at, :]
        fd[at, :] = ta[at, :] * dd + b * dr
        fr[at, :] = b * dd + tc[at, :] * dr
        return carry

    lax.fori_loop(0, CR + 1, fluxes, 0)

    def images(e, totals):
        at = pl.multiple_of(16 + 8 * e, 8)
        fdw = fd[pl.ds(pl.multiple_of(at - 8, 8), 16), :]
        side = fr[pl.ds(at, 8), :]
        flux = fdw[7:15] - fdw[8:16] + pltpu.roll(side, 1, 1) - side
        to = pl.ds(pl.multiple_of(8 * e, 8), 8)
        p = p_ext[pl.ds(at, 8), :][:, 128 : 128 + CD]
        q = flux[:, 128 : 128 + CD] + mask[to, :].astype(F32) * p
        p_o[to, :] = p
        q_o[to, :] = q
        rowsum[pl.ds(e, 1), :] = jnp.sum(q, axis=0, keepdims=True)
        return totals[0] + p * q, totals[1] + q * q * rd[to, :]

    zero = jnp.zeros((8, CD), F32)
    pq, qq = lax.fori_loop(0, CR, images, (zero, zero))

    def lanes(x):
        x = jnp.sum(x, axis=0, keepdims=True)
        return sum(x[:, k * 128 : k * 128 + 128] for k in range(CD // 128))

    rp = jnp.sum(first_sums[...], axis=0, keepdims=True)
    rp += jnp.sum(first_blocks[0] * values[1 : CR + 1, :CC], axis=0, keepdims=True)
    tail = jnp.concatenate([rp, lanes(pq), lanes(qq), jnp.zeros((5, 128), F32)], axis=0)
    sums = block_sums(rowsum[...], group[...])
    for j in range(n_cr):
        blocks_o[j, 0:CR] = sums
        blocks_o[j, CR : CR + 8] = tail


def final_kernel(
    n_in, n_cr, pos, moments, own, grow, fall, blocks, back_hi, back_lo, spread,
    p_in, q_in, r_in, rd, v_in, v_o, r_o, d_o, cs,
):
    _, spread_rows, energy = coarse_values(
        n_in, n_cr, pos[0], moments, own, grow, fall, blocks, back_hi, back_lo, spread
    )
    cs[...] = spread_rows
    sums = sum(moments[i, 2 * n_cr : 2 * n_cr + 8] for i in range(n_in))
    old = jnp.sum(sums[0:1], axis=1, keepdims=True)
    curvature = jnp.sum(sums[1:2], axis=1, keepdims=True)
    energy = jnp.sum(jnp.sum(energy, axis=0, keepdims=True), axis=1, keepdims=True)
    image = jnp.sum(sums[2:3] + sums[3:4], axis=1, keepdims=True) + energy
    step = old / curvature
    ratio = (step * step * image - old) / old
    more = 1.0 + ratio

    def body(e, carry):
        at = pl.ds(pl.multiple_of(8 * e, 8), 8)
        p, q = p_in[at, :], q_in[at, :]
        coarse = cs[pl.ds(e + 1, 1), 128 : 128 + CD]
        v_o[at, :] = v_in[at, :] + step * p
        r_o[at, :] = r_in[at, :] - step * q
        d_o[at, :] = more * p - step * (q * rd[at, :] + coarse)
        return carry

    lax.fori_loop(0, CR, body, 0)


def coarse_call(kernel, n_in, n_cr, name, out_shape, scratch, pos, moments, own, tables, rest, group=None):
    n = CC * n_cr

    def whole(t):
        return pl.BlockSpec(t.shape, lambda i, pos, n=t.ndim: (0,) * n)

    pick = pl.BlockSpec((1, n, 2 * CC), lambda i, pos: (pos[1], 0, 0))
    first = [moments, own, tables["grow"], tables["fall"], tables["blocks"]]
    last = [tables["spread"]] + ([group] if group is not None else []) + list(rest)
    return pl.pallas_call(
        functools.partial(kernel, n_in, n_cr),
        grid_spec=pltpu.PrefetchScalarGridSpec(
            num_scalar_prefetch=1, grid=(1,),
            in_specs=[whole(t) for t in first] + [pick, pick] + [whole(t) for t in last],
            out_specs=[whole(t) for t in out_shape], scratch_shapes=scratch,
        ),
        out_shape=out_shape,
        compiler_params=pltpu.CompilerParams(vmem_limit_bytes=LIMIT),
        cost_estimate=pl.CostEstimate(flops=10**8, bytes_accessed=10**7, transcendentals=0),
        name=name,
    )(pos, *first, *tables["back"], *last)


def neighbours(value_low, value_high, axis, count):
    ahead = [(i, i + 1) for i in range(count - 1)]
    behind = [(j, i) for i, j in ahead]
    return lax.ppermute(value_high, axis, ahead), lax.ppermute(value_low, axis, behind)


def per_device(n_in, n_cr, amplitudes, mask, depth, iterate):
    sel, place, rows, put, mix, lanes = (jnp.asarray(t) for t in line_tables())
    tables = coarse_tables(n_in, n_cr)
    pos = jnp.stack([lax.axis_index("inline"), lax.axis_index("crosslin")]).astype(jnp.int32)
    col_first, col_last = pack_columns(amplitudes, iterate, mask, depth, sel)
    left, right = neighbours(col_first, col_last, "crosslin", n_cr)
    row_first, row_last = pack_rows(amplitudes, iterate, mask, depth, left, right, rows, mix, lanes)
    up, down = neighbours(row_first, row_last, "inline", n_in)
    group = jnp.asarray(tables["group"])
    ta, tb, tc, z, r, rd, blocks, sums = tensor_stage(
        n_in, n_cr, pos, amplitudes, iterate, mask, depth, up, down, left, right, put, place, group
    )

    def moments_of(payload, extra):
        gathered = lax.all_to_all(payload, "crosslin", 0, 0, tiled=True)
        pay, own = moments_stage(n_in, n_cr, extra, gathered, *tables["forward"], tables["steps"])
        return lax.all_to_all(pay, "inline", 0, 0, tiled=True), own

    flat = jax.ShapeDtypeStruct((RD, CD), F32)
    ext = VMEM((ER, EC), F32)
    cs = VMEM((40, EC), F32)
    moments, own = moments_of(blocks, False)
    p, q, payload = coarse_call(
        image_kernel, n_in, n_cr, "image_stage",
        [flat, flat, jax.ShapeDtypeStruct((n_cr, CR + 8, CC), F32)],
        [ext, ext, ext, VMEM((CR, CD), F32), cs],
        pos, moments, own, tables, [ta, tb, tc, z, r, rd, mask, blocks, sums], group,
    )
    moments, own = moments_of(payload, True)
    return tuple(
        coarse_call(
            final_kernel, n_in, n_cr, "final_stage", [flat, flat, flat], [cs],
            pos, moments, own, tables, [p, q, r, rd, iterate],
        )
    )


def solution(mesh):
    n_in, n_cr = mesh.shape["inline"], mesh.shape["crosslin"]
    flat = P("inline", "crosslin")
    return jax.shard_map(
        functools.partial(per_device, n_in, n_cr), mesh=mesh,
        in_specs=(P(None, "inline", "crosslin"), flat, flat, flat),
        out_specs=(flat, flat, flat), check_vma=False,
    )
```

profile of v0, /device:TPU:0, one launch (start us, length us, event | category | flops | bytes accessed | tf_op | source)
XLA Modules:
  0.0 138.8 jit_solution(14339251883536659639)
XLA Ops:
  0.6 3.4 %copy-done = bf16[16,256,1024]{2,1,0:T(8,128)(2,1)S(1)} copy-done((bf16[16,256,1024]{2,1,0:T(8,128)(2,1)S(1)}, bf16[16,256,1024]{2,1,0:T(8,128)(2,1)}, u32[]{:S(2)}) %copy-start) | copy-done | bytes 8388632
  4.0 1.2 copy-done.1
  5.2 1.2 copy-done.2
  6.5 1.2 copy-done.3
  7.7 1.3 copy-done.6
  9.0 1.0 pack_columns.1
  10.1 1.3 collective-permute-start
  11.4 1.3 collective-permute-start.1
  12.7 3.7 %collective-permute-done.1.right = bf16[256,128]{1,0:T(8,128)(2,1)S(1)} collective-permute-done((bf16[256,128]{1,0:T(8,128)(2,1)S(1)}, bf16[256,128]{1,0:T(8,128)(2,1)S(1)}, u32[]{:S(2)}, u32[]{:S(2)}) %collective-permute-start.1) | collective-permute-done | bytes 65568 | tf_op jit(solution)/shard_map/ppermute | solution.py:546
  17.1 3.4 %collective-permute-start.2 = (bf16[64,1280]{1,0:T(8,128)(2,1)S(1)}, bf16[64,1280]{1,0:T(8,128)(2,1)S(1)}, u32[]{:S(2)}, u32[]{:S(2)}) collective-permute-start(bf16[64,1280]{1,0:T(8,128)(2,1)S(1)} %get-tuple-element.24), channel_id=1, source_target_pairs={{0,8},{8,16},{16,24},{24,32},{32,40},{40,48},{48,56},{56,64},{64,7... | collective-permute-start | bytes 491528 | tf_op jit(solution)/shard_map/ppermute | solution.py:546
  20.5 1.3 collective-permute-start.3
  22.3 0.9 collective-permute-done.2.up
  23.3 4.4 %collective-permute-done.3.down = bf16[64,1280]{1,0:T(8,128)(2,1)S(1)} collective-permute-done((bf16[64,1280]{1,0:T(8,128)(2,1)S(1)}, bf16[64,1280]{1,0:T(8,128)(2,1)S(1)}, u32[]{:S(2)}, u32[]{:S(2)}) %collective-permute-start.3) | collective-permute-done | bytes 163872 | tf_op jit(solution)/shard_map/ppermute | solution.py:546
  27.7 0.7 copy-done.16
  28.4 34.0 %tensor_stage.1 = (f32[288,1280]{1,0:T(8,128)}, f32[288,1280]{1,0:T(8,128)}, f32[288,1280]{1,0:T(8,128)}, f32[288,1280]{1,0:T(8,128)}, f32[256,1024]{1,0:T(8,128...) custom-call(s32[2]{0:T(128)} %pad_add_fusion.pos, bf16[16,256,1024]{2,1,0:T(8,128)(2,1)} %amp.1, ...), custom_call_target="tpu_custom_call" | custom-call | flops 100000000 | bytes 20000000 | tf_op jit(solution)/shard_map/tensor_stage/pallas_call | solution.py:331
  62.3 13.4 %all_to_all.20.blocks = f32[8,32,128]{2,1,0:T(8,128)S(1)} all-to-all(f32[8,32,128]{2,1,0:T(8,128)} %get-tuple-element.26.first_blocks), channel_id=1, replica_groups=mesh['inline'=16,'crosslin'=8] {'crosslin'}, dimensions={0} | all-to-all | bytes 262144 | tf_op jit(solution)/shard_map/all_to_all | solution.py:563
  75.7 1.0 moments_stage.2
  76.7 0.7 copy-done.9
  77.4 17.5 %all_to_all.21.moments = f32[16,16,128]{2,1,0:T(8,128)} all-to-all(f32[16,16,128]{2,1,0:T(8,128)S(1)} %get-tuple-element.27), channel_id=1, replica_groups=mesh['inline'=16,'crosslin'=8] {'inline'}, dimensions={0} | all-to-all | bytes 262144 | tf_op jit(solution)/shard_map/all_to_all | solution.py:565
  94.9 13.9 %image_stage.1 = (f32[256,1024]{1,0:T(8,128)}, f32[256,1024]{1,0:T(8,128)}, f32[8,40,128]{2,1,0:T(8,128)}) custom-call(s32[2]{0:T(128)} %pad_add_fusion.pos, f32[16,16,128]{2,1,0:T(8,128)} %all_to_all.21.moments, f32[40,1024]{1,0:T(8,128)} %copy-done.9, f32[40,1024]{1,0:T(8,128)} %constant.51.clone.grow, f32[40,1024]{1,0:T(8,128)} %constant.52.clone.fall, ...), custom_call_target="tpu_custom_call" | custom-call | flops 100000000 | bytes 10000000 | tf_op jit(solution)/shard_map/image_stage/pallas_call | solution.py:529
  108.8 9.8 %all_to_all.22.blocks = f32[8,40,128]{2,1,0:T(8,128)S(1)} all-to-all(f32[8,40,128]{2,1,0:T(8,128)} %get-tuple-element.36), channel_id=1, replica_groups=mesh['inline'=16,'crosslin'=8] {'crosslin'}, dimensions={0} | all-to-all | bytes 327680 | tf_op jit(solution)/shard_map/all_to_all | solution.py:563
  118.6 1.0 moments_stage.3
  119.6 11.6 %all_to_all.23.moments = f32[16,24,128]{2,1,0:T(8,128)} all-to-all(f32[16,24,128]{2,1,0:T(8,128)S(1)} %get-tuple-element.37), channel_id=1, replica_groups=mesh['inline'=16,'crosslin'=8] {'inline'}, dimensions={0} | all-to-all | bytes 393216 | tf_op jit(solution)/shard_map/all_to_all | solution.py:565
  131.2 7.6 %final_stage.1 = (f32[256,1024]{1,0:T(8,128)}, f32[256,1024]{1,0:T(8,128)}, f32[256,1024]{1,0:T(8,128)}) custom-call(s32[2]{0:T(128)} %pad_add_fusion.pos, f32[16,24,128]{2,1,0:T(8,128)} %all_to_all.23.moments, f32[40,1024]{1,0:T(8,128)} %copy-done.10, f32[40,1024]{1,0:T(8,128)} %constant.51.clone.grow, f32[40,1024]{1,0:T(8,128)} %constant.52.clone.fall, ...), custom_call_target="tpu_custom_call" | custom-call | flops 100000000 | bytes 10000000 | tf_op jit(solution)/shard_map/final_stage/pallas_call | solution.py:529
  (30 shorter events, 1.2 us)
Async XLA Ops:
  0.6 3.4 %copy-start = (bf16[16,256,1024]{2,1,0:T(8,128)(2,1)S(1)}, bf16[16,256,1024]{2,1,0:T(8,128)(2,1)}, u32[]{:S(2)}) copy-start(bf16[16,256,1024]{2,1,0:T(8,128)(2,1)} %amp.1) | copy-start | bytes 25165828
  4.0 1.2 copy-start.1
  5.2 1.2 copy-start.2
  6.5 1.2 copy-start.3
  7.7 1.3 copy-start.6
  9.0 7.4 %copy-start.12 = (bf16[2,3,64,128]{3,2,1,0:T(8,128)(2,1)S(1)}, bf16[2,3,64,128]{3,2,1,0:T(8,128)(2,1)}, u32[]{:S(2)}) copy-start(bf16[2,3,64,128]{3,2,1,0:T(8,128)(2,1)} %constant.45.clone.mix) | copy-start | bytes 294916
  9.0 7.4 %copy-start.13 = (bf16[2,128,128]{2,1,0:T(8,128)(2,1)S(1)}, bf16[2,128,128]{2,1,0:T(8,128)(2,1)}, u32[]{:S(2)}) copy-start(bf16[2,128,128]{2,1,0:T(8,128)(2,1)} %constant.46.clone.lanes) | copy-start | bytes 196612
  9.0 7.4 %copy-start.14 = (bf16[2,64,256]{2,1,0:T(8,128)(2,1)S(1)}, bf16[2,64,256]{2,1,0:T(8,128)(2,1)}, u32[]{:S(2)}) copy-start(bf16[2,64,256]{2,1,0:T(8,128)(2,1)} %constant.43.clone.rows) | copy-start | bytes 196612
  10.1 2.6 %collective-permute-start = (bf16[256,128]{1,0:T(8,128)(2,1)S(1)}, bf16[256,128]{1,0:T(8,128)(2,1)S(1)}, u32[]{:S(2)}, u32[]{:S(2)}) collective-permute-start(bf16[256,128]{1,0:T(8,128)(2,1)S(1)} %get-tuple-element.22), channel_id=1, source_target_pairs={{0,1},{1,2},{2,3},{3,4},{4,5},{5,6},{6,7},{8,9},{9,10},{10,11},{11... | collective-permute-start | bytes 196616 | tf_op jit(solution)/shard_map/ppermute | solution.py:546
  11.4 5.0 %collective-permute-start.1 = (bf16[256,128]{1,0:T(8,128)(2,1)S(1)}, bf16[256,128]{1,0:T(8,128)(2,1)S(1)}, u32[]{:S(2)}, u32[]{:S(2)}) collective-permute-start(bf16[256,128]{1,0:T(8,128)(2,1)S(1)} %get-tuple-element.23), channel_id=1, source_target_pairs={{1,0},{2,1},{3,2},{4,3},{5,4},{6,5},{7,6},{9,8},{10,9},{11,10},{12... | collective-permute-start | bytes 196616 | tf_op jit(solution)/shard_map/ppermute | solution.py:546
  12.7 4.2 %copy-start.7 = (bf16[256,128]{1,0:T(8,128)(2,1)}, bf16[256,128]{1,0:T(8,128)(2,1)S(1)}, u32[]{:S(2)}) copy-start(bf16[256,128]{1,0:T(8,128)(2,1)S(1)} %collective-permute-done.left) | copy-start | bytes 196612
  16.4 0.6 copy-start.8
  17.1 6.2 %collective-permute-start.2 = (bf16[64,1280]{1,0:T(8,128)(2,1)S(1)}, bf16[64,1280]{1,0:T(8,128)(2,1)S(1)}, u32[]{:S(2)}, u32[]{:S(2)}) collective-permute-start(bf16[64,1280]{1,0:T(8,128)(2,1)S(1)} %get-tuple-element.24), channel_id=1, source_target_pairs={{0,8},{8,16},{16,24},{24,32},{32,40},{40,48},{48,56},{56,64},{64,7... | collective-permute-start | bytes 491528 | tf_op jit(solution)/shard_map/ppermute | solution.py:546
  20.5 7.2 %collective-permute-start.3 = (bf16[64,1280]{1,0:T(8,128)(2,1)S(1)}, bf16[64,1280]{1,0:T(8,128)(2,1)S(1)}, u32[]{:S(2)}, u32[]{:S(2)}) collective-permute-start(bf16[64,1280]{1,0:T(8,128)(2,1)S(1)} %get-tuple-element.25), channel_id=1, source_target_pairs={{8,0},{16,8},{24,16},{32,24},{40,32},{48,40},{56,48},{64,56},{72,6... | collective-permute-start | bytes 491528 | tf_op jit(solution)/shard_map/ppermute | solution.py:546
  22.3 53.4 %copy-start.11 = (f32[8,1024]{1,0:T(8,128)S(1)}, f32[8,1024]{1,0:T(8,128)}, u32[]{:S(2)}) copy-start(f32[8,1024]{1,0:T(8,128)} %constant.50.clone.steps) | copy-start | bytes 98308
  23.3 4.4 %copy-start.15 = (bf16[64,1280]{1,0:T(8,128)(2,1)}, bf16[64,1280]{1,0:T(8,128)(2,1)S(1)}, u32[]{:S(2)}) copy-start(bf16[64,1280]{1,0:T(8,128)(2,1)S(1)} %collective-permute-done.2.up) | copy-start | bytes 491524
  27.7 0.7 copy-start.16
  28.4 47.3 %copy-start.4 = (bf16[1024,1024]{1,0:T(8,128)(2,1)S(1)}, bf16[1024,1024]{1,0:T(8,128)(2,1)}, u32[]{:S(2)}) copy-start(bf16[1024,1024]{1,0:T(8,128)(2,1)} %constant.49.clone.fwd_lo) | copy-start | bytes 6291460
  28.4 47.3 %copy-start.5 = (bf16[1024,1024]{1,0:T(8,128)(2,1)S(1)}, bf16[1024,1024]{1,0:T(8,128)(2,1)}, u32[]{:S(2)}) copy-start(bf16[1024,1024]{1,0:T(8,128)(2,1)} %constant.48.clone.fwd_hi) | copy-start | bytes 6291460
  76.7 0.7 copy-start.9
  119.6 11.6 %copy-start.10 = (f32[40,1024]{1,0:T(8,128)}, f32[40,1024]{1,0:T(8,128)S(1)}, u32[]{:S(2)}) copy-start(f32[40,1024]{1,0:T(8,128)S(1)} %get-tuple-element.38.own) | copy-start | bytes 491524
where the time goes:
time: 139 us
  Pallas kernels  59 us (42%)
  blocking collectives  52.2 us (38%)
  local copies, waits for them, and re-layouts  9.95 us (7%)
  waiting for transfers between devices  9.08 us (7%)
  starting transfers between devices  7.27 us (5%)
    pallas_call x1, Pallas kernels, tensor_stage(): pl.pallas_call(functools.partial(tensor_kernel, n_in, n_cr), in_specs=[pl...  34 us
    all_to_all x2, blocking collectives, moments_of(): return (lax.all_to_all(pay, 'inline', 0, 0, tiled=True), own)  29.1 us
    all_to_all x2, blocking collectives, moments_of(): gathered = lax.all_to_all(payload, 'crosslin', 0, 0, tiled=True)  23.1 us
    pallas_call x2, Pallas kernels, coarse_call(): pl.pallas_call(functools.partial(kernel, n_in, n_cr), grid_spec=pltpu.Pre...  21.5 us
    unnamed x34, local copies, waits for them, and re-layouts  9.95 us
    ppermute x2, waiting for transfers between devices, neighbours(): lax.ppermute(value_low, axis, behind)  8.13 us
    ppermute x2, starting transfers between devices, neighbours(): lax.ppermute(value_high, axis, ahead)  4.68 us
  transfers between devices with their start and end apart: 4, of which 3 were waited for; matrix products, arithmetic and copies ran while one was open for 0% of the time, Pallas kernels for 0%

commit v1 on v0

v1 whole, which is shorter than its diff:
```python
import functools

import jax
import jax.numpy as jnp
import ml_dtypes
import numpy as np
from jax import lax
from jax.experimental import pallas as pl
from jax.experimental.pallas import tpu as pltpu
from jax.sharding import PartitionSpec as P

K = 16
DEC = 8
CI = 32
COUPLING = 4.0
F32 = jnp.float32
BF16 = jnp.bfloat16
NPB = ml_dtypes.bfloat16
VMEM = pltpu.VMEM

RD = 256
CD = 1024
ER = RD + 32
EC = CD + 128
CR = RD // DEC
CC = CD // DEC
MSG = 64


def dot(a, b):
    return jnp.dot(a, b, preferred_element_type=F32)


def parts2(x):
    hi = x.astype(BF16)
    return hi, (x - hi.astype(F32)).astype(BF16)


def parts3(x):
    hi = x.astype(BF16)
    rest = x - hi.astype(F32)
    mid = rest.astype(BF16)
    return hi, mid, (rest - mid.astype(F32)).astype(BF16)


def np2(x):
    hi = x.astype(np.float32).astype(NPB)
    return hi, (x - hi.astype(np.float64)).astype(np.float32).astype(NPB)


def line_tables():
    rows = np.zeros((2, MSG, 256), np.float32)
    put = np.zeros((2, 304, MSG), np.float32)
    for s in range(K):
        for k in range(3):
            rows[0, 3 * s + k, 16 * s + k] = 1
            rows[1, 3 * s + k, 16 * s + 13 + k] = 1
    for side in range(2):
        put[side, :256] = rows[side].T
        for l in range(2):
            for part in range(3):
                put[side, 256 + (14 + l if side else l), 48 + 3 * l + part] = 1
        put[side, 272 + (15 if side else 0), 54] = 1
        put[side, 288 + (15 if side else 0), 55] = 1
    mix = np.zeros((2, 3, MSG, 128), np.float32)
    for k in range(3):
        for s in range(K):
            mix[:, k, 3 * s + k, 3 * s : 3 * s + 3] = 1
    for l in range(2):
        for part in range(3):
            for other in range(2):
                mix[0, l, 48 + 3 * l + part, 48 + 3 * other + part] = 1
                mix[1, l + 1, 48 + 3 * l + part, 48 + 3 * other + part] = 1
    for o in (54, 55):
        mix[0, 0, o, o] = 1
        mix[1, 2, o, o] = 1
    lanes = np.zeros((2, 128, 128), np.float32)
    for s in range(K):
        for k in range(3):
            lanes[0, 3 * s + k, k] = 1
            lanes[1, 3 * s + k, 125 + k] = 1
    for l in range(2):
        for part in range(3):
            lanes[0, 48 + 3 * l + part, l] = 1
            lanes[1, 48 + 3 * l + part, 126 + l] = 1
    for o in (54, 55):
        lanes[0, o, 0] = 1
        lanes[1, o, 127] = 1
    return tuple(t.astype(NPB) for t in (rows, put, mix, lanes))


def coarse_tables(n_in, n_cr):
    n = CC * n_cr
    freq = np.arange(n, dtype=np.float64)
    norm = np.where(freq == 0, np.sqrt(1.0 / n), np.sqrt(2.0 / n))

    def cosines(cols):
        phase = (freq[:, None] * (2 * cols[None, :] + 1)) % (4 * n)
        return norm[:, None] * np.cos(np.pi * phase / (2 * n))

    lead = np.arange(n + CC, dtype=np.float64) - 16
    forward = cosines(lead).T * (lead[:, None] >= -1) * (lead[:, None] <= n)
    half = (2.0 - 2.0 * np.cos(np.pi * freq / n) + 1.0 / (CI * CI)) / 2.0
    kappa = np.log1p(half + np.sqrt(half * (half + 2.0)))
    scale = 1.0 / (COUPLING * 2.0 * np.sinh(kappa))
    steps = np.stack([np.exp(-kappa * d) for d in (1, 2, 4, 8, 16)] + [scale] + [scale * 0] * 2)
    at = np.arange(40)[:, None]
    grow = scale * np.exp(-kappa * at) * (at < 34)
    fall = scale * np.exp(-kappa * (33.0 - at)) * (at < 34)
    whole = CR * n_in
    blocks = np.stack(
        [
            np.exp(-kappa * CR),
            np.exp(-kappa * whole),
            1.0 / (1.0 - np.exp(-kappa * 2 * whole)),
            scale * np.exp(-kappa),
        ]
    ).reshape(4, n_cr, 128)
    spread = np.zeros((2 * CC, EC))
    for lane in range(EC):
        col = ((lane if lane >= 64 else lane + EC) - 128) // DEC
        if -1 <= col <= CC:
            spread[16 + col, lane] = 1
    group = np.zeros((CD, CC))
    group[np.arange(CD), np.arange(CD) // DEC] = 1
    f = np.float32
    return dict(
        forward=np2(forward), steps=steps.astype(f), grow=grow.astype(f),
        fall=fall.astype(f), blocks=blocks.astype(f), spread=spread.astype(NPB), group=group.astype(NPB),
    )


def moved(x, lane, to):
    turn = (to - lane) % x.shape[1]
    return pltpu.roll(x, turn, 1) if turn else x


def pack_columns_kernel(amp, v_in, m_in, d_in, out0, out1, a, v, m, d, sems):
    copies = []
    for side, at in enumerate((0, CD - 128)):
        span = pl.ds(at, 128)
        copies.append(pltpu.make_async_copy(amp.at[:, :, span], a.at[side], sems.at[side, 0]))
        copies.append(pltpu.make_async_copy(v_in.at[:, span], v.at[side], sems.at[side, 1]))
        copies.append(pltpu.make_async_copy(m_in.at[:, span], m.at[side], sems.at[side, 2]))
        copies.append(pltpu.make_async_copy(d_in.at[:, span], d.at[side], sems.at[side, 3]))
    for c in copies:
        c.start()
    lane = lax.broadcasted_iota(jnp.int32, (RD, 128), 1)
    for c in copies:
        c.wait()
    for side, out in enumerate((out0, out1)):
        low = 125 if side else 0
        weight = m[side].astype(F32)
        source = weight * (d[side].astype(F32) - 0.5 * (K - 1))
        end = 127 if side else 0
        total = jnp.where(lane == 54, moved(weight, end, 54), moved(source, end, 55))
        for part, value in enumerate(parts3(v[side])):
            value = value.astype(F32)
            for l in range(2):
                to = 48 + 3 * l + part
                total = jnp.where(lane == to, moved(value, (126 if side else 0) + l, to), total)
        for s in range(K):
            total = jnp.where((lane >= 3 * s) & (lane < 3 * s + 3), moved(a[side, s].astype(F32), low, 3 * s), total)
        out[...] = jnp.where(lane < 56, total, 0.0).astype(BF16)


def pack_columns(amplitudes, iterate, mask, depth):
    hbm = pl.BlockSpec(memory_space=pltpu.HBM)
    out = jax.ShapeDtypeStruct((RD, 128), BF16)
    return pl.pallas_call(
        pack_columns_kernel, in_specs=[hbm] * 4,
        out_specs=[pl.BlockSpec(memory_space=VMEM)] * 2, out_shape=[out, out],
        scratch_shapes=[
            VMEM((2, K, RD, 128), BF16), VMEM((2, RD, 128), F32), VMEM((2, RD, 128), jnp.int32),
            VMEM((2, RD, 128), jnp.int32), pltpu.SemaphoreType.DMA((2, 4)),
        ],
        compiler_params=pltpu.CompilerParams(vmem_limit_bytes=60 * 1024 * 1024),
        cost_estimate=pl.CostEstimate(flops=10**7, bytes_accessed=3 * 10**6, transcendentals=0),
        name="pack_columns",
    )(amplitudes, iterate, mask, depth)


def pack_rows_kernel(
    amp, v_in, m_in, d_in, left, right, rows, mix, lanes, out0, out1, a, v, m, d, sems
):
    copies = []
    for side in range(2):
        copies.append(pltpu.make_async_copy(amp.at[:, pl.ds(side * (RD - 16), 16)], a.at[side], sems.at[side, 0]))
        for i, (source, to) in enumerate(((v_in, v), (m_in, m), (d_in, d))):
            copies.append(
                pltpu.make_async_copy(source.at[pl.ds(side * (RD - 8), 8)], to.at[side], sems.at[side, 1 + i])
            )
    for c in copies:
        c.start()
    for c in copies:
        c.wait()
    at = lax.broadcasted_iota(jnp.int32, (MSG, CD), 0)
    for side, out in enumerate((out0, out1)):
        middle = dot(rows[side], a[side].reshape(K * 16, CD))
        split = [p.astype(F32) for p in parts3(v[side])]
        for l in range(2):
            row = 6 + l if side else l
            for part in range(3):
                middle = jnp.where(at == 48 + 3 * l + part, split[part][row : row + 1], middle)
        row = 7 if side else 0
        weight = m[side, row : row + 1].astype(F32)
        source = weight * (d[side, row : row + 1].astype(F32) - 0.5 * (K - 1))
        middle = jnp.where(at == 54, weight, jnp.where(at == 55, source, middle))
        out[:, 128:] = middle.astype(BF16)
        total = jnp.zeros((MSG, 128), F32)
        for halo, which in ((left, 1), (right, 0)):
            edge = halo[RD - 16 : RD].astype(F32)[13:16] if side else halo[0:16].astype(F32)[0:3]
            for k in range(3):
                term = mix[side, k].astype(F32) * edge[k : k + 1]
                total += dot(term.astype(BF16), lanes[which])
        out[:, 0:128] = total.astype(BF16)


def pack_rows(amplitudes, iterate, mask, depth, left, right, rows, mix, lanes):
    hbm = pl.BlockSpec(memory_space=pltpu.HBM)
    vmem = pl.BlockSpec(memory_space=VMEM)
    out = jax.ShapeDtypeStruct((MSG, EC), BF16)
    return pl.pallas_call(
        pack_rows_kernel, in_specs=[hbm] * 4 + [vmem] * 5, out_specs=[vmem] * 2, out_shape=[out, out],
        scratch_shapes=[
            VMEM((2, K, 16, CD), BF16), VMEM((2, 8, CD), F32), VMEM((2, 8, CD), jnp.int32),
            VMEM((2, 8, CD), jnp.int32), pltpu.SemaphoreType.DMA((2, 4)),
        ],
        compiler_params=pltpu.CompilerParams(vmem_limit_bytes=58 * 1024 * 1024),
        cost_estimate=pl.CostEstimate(flops=10**7, bytes_accessed=2 * 10**6, transcendentals=0),
        name="pack_rows",
    )(amplitudes, iterate, mask, depth, left, right, rows, mix, lanes)


def gradient_sums(window, off, take):
    total = None
    for s in range(K):
        x = window(s).astype(F32)
        n = x.shape[1]
        middle = x[8:24]
        gc = (pltpu.roll(middle, n - 1, 1) - pltpu.roll(middle, 1, 1))[:, off : off + take]
        x = x[:, off : off + take]
        gi = pltpu.roll(x, 31, 0)[8:24] - pltpu.roll(x, 1, 0)[8:24]
        terms = (gi * gi, gi * gc, gc * gc)
        total = terms if total is None else tuple(t + u for t, u in zip(total, terms))
    return total


def inner_kernel(first, steps, amp, sii_o, sic_o, scc_o, edge_o, a, sems):
    rows = 16 * (steps + 1)
    half = 64
    bounds = [(r, min(half, rows - r)) for r in range(0, rows, half)]
    copies = [
        pltpu.make_async_copy(amp.at[:, pl.ds(16 * first + r, n)], a.at[:, pl.ds(r, n)], sems.at[i])
        for i, (r, n) in enumerate(bounds)
    ]
    for c in copies:
        c.start()
    lane = lax.broadcasted_iota(jnp.int32, (16, 128), 1)

    def step(t, carry):
        at = pl.multiple_of(16 * t, 16)
        for part in range(2):
            lanes = slice(0, 640) if part == 0 else slice(384, CD)
            off = 0 if part == 0 else 128
            sums = gradient_sums(lambda s: a[s, pl.ds(at, 32), lanes], off, 512)
            for o, value in zip((sii_o, sic_o, scc_o), sums):
                o[pl.ds(at, 16), 512 * part : 512 * part + 512] = value
        return carry

    def edges(t, carry):
        at = pl.ds(pl.multiple_of(16 * t, 16), 16)
        for s in range(K):
            low = moved(a[s, at, 0:128].astype(F32), 0, 35)
            high = moved(a[s, at, CD - 128 : CD].astype(F32), 125, 64)
            tile = jnp.where((lane >= 35) & (lane < 38), low, jnp.where((lane >= 64) & (lane < 67), high, 0.0))
            edge_o[s, at, :] = tile.astype(BF16)
        return carry

    done = 0
    for i, (r, n) in enumerate(bounds):
        copies[i].wait()
        until = min(steps, (r + n) // 16 - 1)
        lax.fori_loop(done, until, step, 0)
        done = until
    lax.fori_loop(0, steps + 1, edges, 0)


def inner_stage(first, steps, amplitudes):
    rows = 16 * (steps + 1)
    flat = jax.ShapeDtypeStruct((16 * steps, CD), F32)
    return pl.pallas_call(
        functools.partial(inner_kernel, first, steps),
        in_specs=[pl.BlockSpec(memory_space=pltpu.HBM)], out_specs=[pl.BlockSpec(memory_space=VMEM)] * 4,
        out_shape=[flat, flat, flat, jax.ShapeDtypeStruct((K, rows, 128), BF16)],
        scratch_shapes=[VMEM((K, rows, CD), BF16), pltpu.SemaphoreType.DMA((4,))],
        compiler_params=pltpu.CompilerParams(vmem_limit_bytes=57 * 1024 * 1024),
        cost_estimate=pl.CostEstimate(flops=10**8, bytes_accessed=6 * 10**6, transcendentals=0),
        name="inner_stage",
    )(amplitudes)


def block_sums(rows, group):
    return sum(dot(part, group) for part in parts3(rows))


def tensor_kernel(
    n_in, n_cr, cuts, pos, amp, v_in, mask, depth, up, down, left, right, put, group, *rest
):
    inner_refs, rest = rest[: 4 * len(cuts)], rest[4 * len(cuts) :]
    (ta_o, tb_o, tc_o, z_o, r_o, rd_o, blocks_o, sums_o,
     tops, rim, v_ext, w_ext, s_ext, fd, fr, rowsum, sems) = rest
    inner = (slice(16, 16 + RD), slice(128, EC))
    copies = [
        pltpu.make_async_copy(amp.at[:, 0:16], tops.at[0, :, 16:32, 128:EC], sems.at[0]),
        pltpu.make_async_copy(amp.at[:, RD - 16 : RD], tops.at[1, :, 0:16, 128:EC], sems.at[1]),
        pltpu.make_async_copy(v_in, v_ext.at[16 : 16 + RD, 128:EC], sems.at[2]),
    ]
    for c in copies:
        c.start()
    weight = mask[...].astype(F32)
    w_ext[inner] = weight
    s_ext[inner] = weight * (depth[...].astype(F32) - 0.5 * (K - 1))
    lane = lax.broadcasted_iota(jnp.int32, (RD, 128), 1)
    before, after = left[...].astype(F32), right[...].astype(F32)
    here = slice(16, 16 + RD)
    value = jnp.zeros((RD, 128), F32)
    for l in range(2):
        for halo, to in ((before, 126 + l), (after, l)):
            got = sum(moved(halo, 48 + 3 * l + part, to) for part in range(3))
            value = jnp.where(lane == to, got, value)
    v_ext[here, 0:128] = value
    for o, message in ((w_ext, 54), (s_ext, 55)):
        value = jnp.where(lane == 127, moved(before, message, 127), 0.0)
        o[here, 0:128] = jnp.where(lane == 0, moved(after, message, 0), value)
    for s in range(K):
        value = jnp.where(lane < 3, moved(after, 3 * s, 0), 0.0)
        value = jnp.where(lane >= 125, moved(before, 3 * s, 125), value).astype(BF16)
        tops[0, s, 16:32, 0:128] = value[0:16]
        tops[1, s, 0:16, 0:128] = value[RD - 16 : RD]
    for c, (first, steps) in enumerate(cuts):
        begin, rows = (0 if c == 0 else 16 * first + 16), 16 * (steps + 1)
        at = begin - 16 * first
        span, local = slice(begin, 16 * first + rows), slice(at, rows)
        turned, turned_after, tile = before[span], after[span], lane[span]
        for s in range(K):
            value = inner_refs[4 * c + 3][s, local, :].astype(F32)
            value = jnp.where((tile >= 32) & (tile < 35), moved(turned, 3 * s, 32), value)
            value = jnp.where((tile >= 67) & (tile < 70), moved(turned_after, 3 * s, 67), value)
            rim[s, span, :] = value.astype(BF16)
    for side, halo, row in ((1, up, 0), (0, down, 16 + RD)):
        lines = dot(put[side], halo[...])
        for s in range(K):
            tops[1 - side, s, 16 - 16 * side : 32 - 16 * side, :] = lines[16 * s : 16 * s + 16].astype(BF16)
        v_ext[row : row + 16, :] = lines[256:272]
        w_ext[row : row + 16, :] = lines[272:288]
        s_ext[row : row + 16, :] = lines[288:304]
    for c in copies:
        c.wait()
    at_lane = lax.broadcasted_iota(jnp.int32, (1, EC), 1)
    col = pos[1] * CD + jnp.where(at_lane < 64, at_lane + CD, at_lane - 128)
    valid_right = ((col >= 0) & (col < n_cr * CD - 1)).astype(F32)
    row_iota = lax.broadcasted_iota(jnp.int32, (16, 1), 0)
    tile_lane = lax.broadcasted_iota(jnp.int32, (16, 128), 1)

    def left_of(x):
        return pltpu.roll(x, 1, 1)

    def right_of(x):
        return pltpu.roll(x, EC - 1, 1)

    def finish(at, sums):
        sii, sic, scc = (0.25 * x for x in sums)
        inv = 1.0 / (sii + scc + 2.0)
        row = pos[0] * RD - 16 + at + row_iota
        valid_down = ((row >= 0) & (row < n_in * RD - 1)).astype(F32)
        ta = valid_down * ((scc + 1.0) * inv)
        tb = (valid_down * valid_right) * (-sic * inv)
        tc = valid_right * ((sii + 1.0) * inv)
        value = v_ext[pl.ds(at, 24), :]
        here = value[0:16]
        dd = value[1:17] - here
        dr = right_of(here) - here
        to = pl.ds(at, 16)
        ta_o[to, :] = ta
        tb_o[to, :] = tb
        tc_o[to, :] = tc
        fd[to, :] = ta * dd + tb * dr
        fr[to, :] = tb * dd + tc * dr

    for side in range(2):
        sums = gradient_sums(lambda s, side=side: tops[side, s], 0, EC)
        finish(8 + side * (RD), sums)

    for c, (first, steps) in enumerate(cuts):
        sii, sic, scc = inner_refs[4 * c : 4 * c + 3]

        def step(t, carry, sii=sii, sic=sic, scc=scc, first=first):
            local = pl.ds(pl.multiple_of(16 * (t - first), 16), 16)
            at = pl.multiple_of(16 * t, 16)
            edge = gradient_sums(lambda s: rim[s, pl.ds(at, 32), :], 0, 128)
            sums = []
            for ref, e in zip((sii, sic, scc), edge):
                low, high = pltpu.roll(e, 93, 1), pltpu.roll(e, 61, 1)
                x = ref[local, :]
                sums.append(
                    jnp.concatenate(
                        [
                            jnp.where(tile_lane < 64, high, low),
                            jnp.where(tile_lane == 0, low, x[:, 0:128]),
                            x[:, 128 : CD - 128],
                            jnp.where(tile_lane == 127, high, x[:, CD - 128 :]),
                        ],
                        axis=1,
                    )
                )
            finish(pl.multiple_of(24 + 16 * t, 8), sums)
            return carry

        lax.fori_loop(first, first + steps, step, 0)

    def residuals(at, n):
        before = pl.ds(pl.multiple_of(at - 8, 8), n + 8)
        here = pl.ds(at, n)
        fdw, taw = fd[before, :], ta_o[before, :]
        tc, right_flux, weight = tc_o[here, :], fr[here, :], w_ext[here, :]
        image = fdw[7 : n + 7] - fdw[8 : n + 8] + left_of(right_flux) - right_flux + weight * v_ext[here, :]
        r = s_ext[here, :] - image
        diag = taw[8 : n + 8] + 2.0 * tb_o[here, :] + tc + taw[7 : n + 7] + left_of(tc) + weight
        inv = jnp.where(diag != 0.0, 1.0 / diag, 0.0)
        z = r * inv
        z_o[here, :] = z
        return r, inv, z

    def own(e, total):
        at = pl.multiple_of(16 + 16 * e, 16)
        r, inv, z = (x[:, 128:] for x in residuals(at, 16))
        to = pl.ds(pl.multiple_of(16 * e, 16), 16)
        r_o[to, :] = r
        rd_o[to, :] = inv
        rowsum[pl.ds(2 * e, 1), :] = jnp.sum(r[0:8], axis=0, keepdims=True)
        rowsum[pl.ds(2 * e + 1, 1), :] = jnp.sum(r[8:16], axis=0, keepdims=True)
        rz = r * z
        rz = rz[0:8] + rz[8:16]
        return total + sum(rz[:, k * 128 : k * 128 + 128] for k in range(CD // 128))

    residuals(8, 8)
    residuals(16 + RD, 8)
    sums_o[...] = lax.fori_loop(0, RD // 16, own, jnp.zeros((8, 128), F32))
    sums = block_sums(rowsum[...], group[...])
    for j in range(n_cr):
        blocks_o[j] = sums


def tensor_stage(n_in, n_cr, cuts, pos, amp, v, mask, depth, up, down, left, right, put, group, sums):
    vmem = pl.BlockSpec(memory_space=VMEM)
    hbm = pl.BlockSpec(memory_space=pltpu.HBM)
    ext = jax.ShapeDtypeStruct((ER, EC), F32)
    flat = jax.ShapeDtypeStruct((RD, CD), F32)
    return pl.pallas_call(
        functools.partial(tensor_kernel, n_in, n_cr, cuts),
        in_specs=[pl.BlockSpec(memory_space=pltpu.SMEM), hbm, hbm] + [vmem] * (8 + len(sums)),
        out_specs=[vmem] * 8,
        out_shape=[
            ext, ext, ext, ext, flat, flat,
            jax.ShapeDtypeStruct((n_cr, CR, CC), F32),
            jax.ShapeDtypeStruct((8, 128), F32),
        ],
        scratch_shapes=[
            VMEM((2, K, 32, EC), BF16), VMEM((K, RD, 128), BF16), VMEM((ER, EC), F32), VMEM((ER, EC), F32),
            VMEM((ER, EC), F32), VMEM((ER, EC), F32), VMEM((ER, EC), F32), VMEM((CR, CD), F32),
            pltpu.SemaphoreType.DMA((3,)),
        ],
        compiler_params=pltpu.CompilerParams(vmem_limit_bytes=42 * 1024 * 1024),
        cost_estimate=pl.CostEstimate(flops=10**8, bytes_accessed=2 * 10**7, transcendentals=0),
        name="tensor_stage",
    )(pos, amp, v, mask, depth, up, down, left, right, put, group, *sums)


def moments_kernel(n_in, n_cr, extra, blocks, fwd_hi, fwd_lo, steps, pay_o, own_o):
    x = jnp.concatenate([blocks[j, :CR] for j in range(n_cr)], axis=1)
    hi, lo = parts2(x)
    span = slice(16, 16 + x.shape[1])
    both = dot(jnp.concatenate([hi, lo], axis=0), fwd_hi[span, :])
    x = both[:CR] + both[CR:] + dot(hi, fwd_lo[span, :])
    width = x.shape[1]
    forth, back = x, x
    for i in range(5):
        d = 1 << i
        zero = jnp.zeros((d, width), F32)
        decay = steps[i : i + 1]
        forth = forth + decay * jnp.concatenate([zero, forth[:-d]], axis=0)
        back = back + decay * jnp.concatenate([back[d:], zero], axis=0)
    decay, scale = steps[0:1], steps[5:6]
    zero = jnp.zeros((1, width), F32)
    inside = forth + decay * jnp.concatenate([back[1:], zero], axis=0)
    inside = scale * inside
    own_o[...] = jnp.concatenate(
        [scale * decay * back[0:1], inside, scale * decay * forth[CR - 1 :], jnp.zeros((6, width), F32)],
        axis=0,
    )
    f = jnp.concatenate([forth[CR - 1 :, 128 * k : 128 * k + 128] for k in range(n_cr)], axis=0)
    b = jnp.concatenate([back[0:1, 128 * k : 128 * k + 128] for k in range(n_cr)], axis=0)
    for i in range(n_in):
        pay_o[i, 0:n_cr] = f
        pay_o[i, n_cr : 2 * n_cr] = b
    if extra:
        sums = sum(blocks[j, CR : CR + 8] for j in range(n_cr))
        energy = jnp.sum(x * inside, axis=0, keepdims=True)
        energy = sum(energy[:, 128 * k : 128 * k + 128] for k in range(n_cr))
        at = lax.broadcasted_iota(jnp.int32, (8, 128), 0)
        sums = jnp.where(at == 3, energy, sums)
        for i in range(n_in):
            pay_o[i, 2 * n_cr : 2 * n_cr + 8] = sums


def moments_stage(n_in, n_cr, extra, blocks, fwd_hi, fwd_lo, steps):
    vmem = pl.BlockSpec(memory_space=VMEM)
    return pl.pallas_call(
        functools.partial(moments_kernel, n_in, n_cr, extra),
        in_specs=[vmem] * 4, out_specs=[vmem] * 2,
        out_shape=[
            jax.ShapeDtypeStruct((n_in, 2 * n_cr + 8 * extra, 128), F32),
            jax.ShapeDtypeStruct((40, CC * n_cr), F32),
        ],
        compiler_params=pltpu.CompilerParams(vmem_limit_bytes=32 * 1024 * 1024),
        cost_estimate=pl.CostEstimate(flops=2 * 10**8, bytes_accessed=5 * 10**6, transcendentals=0),
        name="moments_stage",
    )(blocks, fwd_hi, fwd_lo, steps)


def coarse_values(n_in, n_cr, pos, moments, own, grow, fall, blocks, fwd_hi, fwd_lo, spread):
    mine = pos[0]
    r32, whole, series, link = (blocks[i] for i in range(4))
    f = [moments[i, 0:n_cr] for i in range(n_in)]
    b = [moments[i, n_cr : 2 * n_cr] for i in range(n_in)]
    hf, hb = f[0], b[n_in - 1]
    for i in range(1, n_in):
        hf = r32 * hf + f[i]
        hb = r32 * hb + b[n_in - 1 - i]
    above = (hb + whole * hf) * series
    below = (hf + whole * hb) * series
    mine_above, mine_below = jnp.zeros_like(above), jnp.zeros_like(below)
    energy = jnp.zeros_like(above)
    for i in range(n_in):
        k = n_in - 1 - i
        mine_above = jnp.where(mine == i, above, mine_above)
        mine_below = jnp.where(mine == k, below, mine_below)
        energy += above * b[i] + below * f[k]
        above = r32 * above + f[i]
        below = r32 * below + b[k]
    energy = energy * link
    a_row = jnp.concatenate([mine_above[k : k + 1] for k in range(n_cr)], axis=1)
    b_row = jnp.concatenate([mine_below[k : k + 1] for k in range(n_cr)], axis=1)
    u = own[...] + a_row * grow[...] + b_row * fall[...]
    hi, lo = parts2(u)
    span = pl.ds(pl.multiple_of(pos[1] * CC, CC), 2 * CC)
    turned = (((1,), (1,)), ((), ()))
    both = lax.dot_general(jnp.concatenate([hi, lo], axis=0), fwd_hi[span, :], turned, preferred_element_type=F32)
    values = both[:40] + both[40:] + lax.dot_general(hi, fwd_lo[span, :], turned, preferred_element_type=F32)
    three = dot(jnp.concatenate(parts3(values), axis=0), spread[...])
    return values, three[:40] + three[40:80] + three[80:], energy


def image_kernel(
    n_in, n_cr, pos, moments, own, grow, fall, blocks, fwd_hi, fwd_lo, spread, group,
    ta, tb, tc, z, rd, mask, first_blocks, first_sums,
    p_o, q_o, blocks_o, rowsum, cs,
):
    values, spread_rows, _ = coarse_values(
        n_in, n_cr, pos, moments, own, grow, fall, blocks, fwd_hi, fwd_lo, spread
    )
    cs[...] = spread_rows

    def field(strip):
        at = pl.ds(pl.multiple_of(8 + 8 * strip, 8), 8)
        return z[at, :] + cs[pl.ds(strip, 1), :]

    def fluxes(at, n, value):
        here = value[0:n]
        dd = value[1 : n + 1] - here
        dr = pltpu.roll(here, EC - 1, 1) - here
        at = pl.ds(at, n)
        b = tb[at, :]
        return ta[at, :] * dd + b * dr, b * dd + tc[at, :] * dr

    def images(e, carry):
        pq, qq, strip, above = carry
        following = [field(2 * e + 2), field(2 * e + 3)]
        value = jnp.concatenate([strip] + following, axis=0)
        down, side = fluxes(pl.multiple_of(16 + 16 * e, 16), 16, value)
        flux = jnp.concatenate([above[7:8], down[0:15]], axis=0) - down + pltpu.roll(side, 1, 1) - side
        to = pl.ds(pl.multiple_of(16 * e, 16), 16)
        p = value[0:16, 128:]
        q = flux[:, 128:] + mask[to, :].astype(F32) * p
        p_o[to, :] = p
        q_o[to, :] = q
        rowsum[pl.ds(2 * e, 1), :] = jnp.sum(q[0:8], axis=0, keepdims=True)
        rowsum[pl.ds(2 * e + 1, 1), :] = jnp.sum(q[8:16], axis=0, keepdims=True)
        return pq + folded(p * q), qq + folded(q * q * rd[to, :]), following[1], down[8:16]

    def folded(x):
        x = x[0:8] + x[8:16]
        return sum(x[:, k * 128 : k * 128 + 128] for k in range(CD // 128))

    strip = field(1)
    above, _ = fluxes(8, 8, jnp.concatenate([field(0), strip], axis=0))
    zero = jnp.zeros((8, 128), F32)
    pq, qq, _, _ = lax.fori_loop(0, RD // 16, images, (zero, zero, strip, above))

    def lanes(x):
        return jnp.sum(x, axis=0, keepdims=True)

    rp = jnp.sum(first_sums[...], axis=0, keepdims=True)
    rp += jnp.sum(first_blocks[0] * pltpu.roll(values, 2 * CC - 16, 1)[1 : CR + 1, :CC], axis=0, keepdims=True)
    tail = jnp.concatenate([rp, lanes(pq), lanes(qq), jnp.zeros((5, 128), F32)], axis=0)
    sums = block_sums(rowsum[...], group[...])
    for j in range(n_cr):
        blocks_o[j, 0:CR] = sums
        blocks_o[j, CR : CR + 8] = tail


def final_kernel(
    n_in, n_cr, pos, moments, own, grow, fall, blocks, fwd_hi, fwd_lo, spread,
    p_in, q_in, r_in, rd, v_in, v_o, r_o, d_o, cs,
):
    _, spread_rows, energy = coarse_values(
        n_in, n_cr, pos, moments, own, grow, fall, blocks, fwd_hi, fwd_lo, spread
    )
    cs[...] = spread_rows
    sums = sum(moments[i, 2 * n_cr : 2 * n_cr + 8] for i in range(n_in))
    old = jnp.sum(sums[0:1], axis=1, keepdims=True)
    curvature = jnp.sum(sums[1:2], axis=1, keepdims=True)
    energy = jnp.sum(jnp.sum(energy, axis=0, keepdims=True), axis=1, keepdims=True)
    image = jnp.sum(sums[2:3] + sums[3:4], axis=1, keepdims=True) + energy
    step = old / curvature
    ratio = (step * step * image - old) / old
    more = 1.0 + ratio

    def body(e, carry):
        at = pl.ds(pl.multiple_of(16 * e, 16), 16)
        p, q = p_in[at, :], q_in[at, :]
        coarse = [jnp.broadcast_to(cs[pl.ds(2 * e + k, 1), 128:], (8, CD)) for k in (1, 2)]
        coarse = jnp.concatenate(coarse, axis=0)
        v_o[at, :] = v_in[at, :] + step * p
        r_o[at, :] = r_in[at, :] - step * q
        d_o[at, :] = more * p - step * (q * rd[at, :] + coarse)
        return carry

    lax.fori_loop(0, RD // 16, body, 0)


def coarse_call(kernel, n_in, n_cr, name, out_shape, scratch, pos, moments, own, tables, rest, group=None):
    vmem = pl.BlockSpec(memory_space=VMEM)
    args = [moments, own, tables["grow"], tables["fall"], tables["blocks"], *tables["forward"], tables["spread"]]
    args += ([group] if group is not None else []) + list(rest)
    return pl.pallas_call(
        functools.partial(kernel, n_in, n_cr),
        in_specs=[pl.BlockSpec(memory_space=pltpu.SMEM)] + [vmem] * len(args),
        out_specs=[vmem] * len(out_shape), out_shape=out_shape, scratch_shapes=scratch,
        compiler_params=pltpu.CompilerParams(vmem_limit_bytes=32 * 1024 * 1024),
        cost_estimate=pl.CostEstimate(flops=10**8, bytes_accessed=10**7, transcendentals=0),
        name=name,
    )(pos, *args)


def neighbours(value_low, value_high, axis, count):
    ahead = [(i, i + 1) for i in range(count - 1)]
    behind = [(j, i) for i, j in ahead]
    return lax.ppermute(value_high, axis, ahead), lax.ppermute(value_low, axis, behind)


def per_device(n_in, n_cr, amplitudes, mask, depth, iterate):
    rows, put, mix, lanes = (jnp.asarray(t) for t in line_tables())
    tables = coarse_tables(n_in, n_cr)
    pos = jnp.stack([lax.axis_index("inline"), lax.axis_index("crosslin")]).astype(jnp.int32)
    col_first, col_last = pack_columns(amplitudes, iterate, mask, depth)
    left, right = neighbours(col_first, col_last, "crosslin", n_cr)
    cuts = ((0, 7), (7, 8))
    inner = inner_stage(*cuts[0], amplitudes)
    (left, right), inner = lax.optimization_barrier(((left, right), inner))
    row_first, row_last = pack_rows(amplitudes, iterate, mask, depth, left, right, rows, mix, lanes)
    up, down = neighbours(row_first, row_last, "inline", n_in)
    inner = list(inner) + list(inner_stage(*cuts[1], amplitudes))
    group = jnp.asarray(tables["group"])
    ta, tb, tc, z, r, rd, blocks, sums = tensor_stage(
        n_in, n_cr, cuts, pos, amplitudes, iterate, mask, depth, up, down, left, right, put, group, inner
    )

    def moments_of(payload, extra):
        gathered = lax.all_to_all(payload, "crosslin", 0, 0, tiled=True)
        pay, own = moments_stage(n_in, n_cr, extra, gathered, *tables["forward"], tables["steps"])
        return lax.all_to_all(pay, "inline", 0, 0, tiled=True), own

    flat = jax.ShapeDtypeStruct((RD, CD), F32)
    cs = VMEM((40, EC), F32)
    moments, own = moments_of(blocks, False)
    p, q, payload = coarse_call(
        image_kernel, n_in, n_cr, "image_stage",
        [flat, flat, jax.ShapeDtypeStruct((n_cr, CR + 8, CC), F32)],
        [VMEM((CR, CD), F32), cs],
        pos, moments, own, tables, [ta, tb, tc, z, rd, mask, blocks, sums], group,
    )
    moments, own = moments_of(payload, True)
    return tuple(
        coarse_call(
            final_kernel, n_in, n_cr, "final_stage", [flat, flat, flat], [cs],
            pos, moments, own, tables, [p, q, r, rd, iterate],
        )
    )


def solution(mesh):
    n_in, n_cr = mesh.shape["inline"], mesh.shape["crosslin"]
    flat = P("inline", "crosslin")
    return jax.shard_map(
        functools.partial(per_device, n_in, n_cr), mesh=mesh,
        in_specs=(P(None, "inline", "crosslin"), flat, flat, flat),
        out_specs=(flat, flat, flat), check_vma=False,
    )
```

time: 139 us -> 111 us (0.80)
  Pallas kernels: 59 us -> 46.7 us
  waiting for transfers between devices: 9.08 us -> 0.01 us
  local copies, waits for them, and re-layouts: 9.95 us -> 4.92 us
  blocking collectives: 52.2 us -> 50.2 us
    pallas_call x5 -> x7, Pallas kernels: 56.9 us -> 44.7 us  [the longest x2 18.2 us: inner_stage(): pl.pallas_call(functools.partial(inner_kernel, first, steps), in_specs=[p...]
    ppermute x2, waiting for transfers between devices: 8.13 us -> 0.01 us  [neighbours(): lax.ppermute(value_low, axis, behind)]
    unnamed x34 -> x54, local copies, waits for them, and re-layouts: 9.95 us -> 4.92 us
  transfers between devices with their start and end apart: 4 -> 4, of which waited for: 3 -> 0; matrix products, arithmetic and copies ran while one was open for 0% -> 0% of each run, Pallas kernels for 0% -> 16%
where the time goes in v1:
time: 111 us
  blocking collectives  50.2 us (45%)
  Pallas kernels  46.7 us (42%)
  starting transfers between devices  7.81 us (7%)
  local copies, waits for them, and re-layouts  4.92 us (4%)
    all_to_all x2, blocking collectives, moments_of(): return (lax.all_to_all(pay, 'inline', 0, 0, tiled=True), own)  28.4 us
    all_to_all x2, blocking collectives, moments_of(): gathered = lax.all_to_all(payload, 'crosslin', 0, 0, tiled=True)  21.8 us
    pallas_call x2, Pallas kernels, inner_stage(): pl.pallas_call(functools.partial(inner_kernel, first, steps), in_specs=[p...  18.2 us
    pallas_call x1, Pallas kernels, tensor_stage(): pl.pallas_call(functools.partial(tensor_kernel, n_in, n_cr, cuts), in_spe...  11.3 us
    pallas_call x2, Pallas kernels, coarse_call(): pl.pallas_call(functools.partial(kernel, n_in, n_cr), in_specs=[pl.BlockS...  8.39 us
    ppermute x2, starting transfers between devices, neighbours(): lax.ppermute(value_high, axis, ahead)  5.23 us
    unnamed x54, local copies, waits for them, and re-layouts  4.92 us
    pallas_call x1, Pallas kernels, pack_columns(): pl.pallas_call(pack_columns_kernel, in_specs=[hbm] * 4, out_specs=[pl.Blo...  3.41 us
  transfers between devices with their start and end apart: 4, of which 0 were waited for; matrix products, arithmetic and copies ran while one was open for 0% of the time, Pallas kernels for 16%

profile of v1, /device:TPU:0, one launch (start us, length us, event | category | flops | bytes accessed | tf_op | source)
XLA Modules:
  0.0 110.8 jit_solution(10917015239650264031)
XLA Ops:
  0.6 3.4 %pack_columns.1 = (bf16[256,128]{1,0:T(8,128)(2,1)}, bf16[256,128]{1,0:T(8,128)(2,1)}) custom-call(bf16[16,256,1024]{2,1,0:T(8,128)(2,1)} %amp.9, f32[256,1024]{1,0:T(8,128)} %v_in.7, s32[256,1024]{1,0:T(8,128)} %mask.3, s32[256,1024]{1,0:T(8,128)} %depth.1), custom_call_target="tpu_custom_call" | custom-call | flops 10000000 | bytes 3000000 | tf_op jit(solution)/shard_map/pack_columns/pallas_call | solution.py:170
  4.0 1.3 %collective-permute-start = (bf16[256,128]{1,0:T(8,128)(2,1)}, bf16[256,128]{1,0:T(8,128)(2,1)S(1)}, u32[]{:S(2)}, u32[]{:S(2)}) collective-permute-start(bf16[256,128]{1,0:T(8,128)(2,1)} %get-tuple-element.36), channel_id=1, source_target_pairs={{0,1},{1,2},{2,3},{3,4},{4,5},{5,6},{6,7},{8,9},{9,10},{10,11},{11... | collective-permute-start | bytes 196616 | tf_op jit(solution)/shard_map/ppermute | solution.py:670
  5.4 1.3 %collective-permute-start.1 = (bf16[256,128]{1,0:T(8,128)(2,1)}, bf16[256,128]{1,0:T(8,128)(2,1)S(1)}, u32[]{:S(2)}, u32[]{:S(2)}) collective-permute-start(bf16[256,128]{1,0:T(8,128)(2,1)} %get-tuple-element.37), channel_id=1, source_target_pairs={{1,0},{2,1},{3,2},{4,3},{5,4},{6,5},{7,6},{9,8},{10,9},{11,10},{12... | collective-permute-start | bytes 196616 | tf_op jit(solution)/shard_map/ppermute | solution.py:670
  6.7 8.6 %inner_stage.2 = (f32[112,1024]{1,0:T(8,128)}, f32[112,1024]{1,0:T(8,128)}, f32[112,1024]{1,0:T(8,128)}, bf16[16,128,128]{2,1,0:T(8,128)(2,1)}) custom-call(bf16[16,256,1024]{2,1,0:T(8,128)(2,1)} %amp.9), custom_call_target="tpu_custom_call" | custom-call | flops 100000000 | bytes 6000000 | tf_op jit(solution)/shard_map/inner_stage/pallas_call | solution.py:292
  15.3 0.6 copy-done.20
  15.9 0.0 copy-done.22
  15.9 3.4 %pack_rows.1 = (bf16[64,1152]{1,0:T(8,128)(2,1)}, bf16[64,1152]{1,0:T(8,128)(2,1)}) custom-call(bf16[16,256,1024]{2,1,0:T(8,128)(2,1)} %amp.9, f32[256,1024]{1,0:T(8,128)} %v_in.7, s32[256,1024]{1,0:T(8,128)} %mask.3, s32[256,1024]{1,0:T(8,128)} %depth.1, bf16[256,128]{1,0:T(8,128)(2,1)} %copy-done.20, bf16[256,128]{1,0:T(8,128)(2,1)} %copy-done.22, ...), custom_call_target="tpu_custom_call" | custom-call | flops 10000000 | bytes 2000000 | tf_op jit(solution)/shard_map/pack_rows/pallas_call | solution.py:223
  19.3 3.9 %collective-permute-start.2 = (bf16[64,1152]{1,0:T(8,128)(2,1)}, bf16[64,1152]{1,0:T(8,128)(2,1)S(1)}, u32[]{:S(2)}, u32[]{:S(2)}) collective-permute-start(bf16[64,1152]{1,0:T(8,128)(2,1)} %get-tuple-element.44), channel_id=1, source_target_pairs={{0,8},{8,16},{16,24},{24,32},{32,40},{40,48},{48,56},{56,64},{64,7... | collective-permute-start | bytes 442376 | tf_op jit(solution)/shard_map/ppermute | solution.py:670
  23.3 1.3 %collective-permute-start.3 = (bf16[64,1152]{1,0:T(8,128)(2,1)}, bf16[64,1152]{1,0:T(8,128)(2,1)S(1)}, u32[]{:S(2)}, u32[]{:S(2)}) collective-permute-start(bf16[64,1152]{1,0:T(8,128)(2,1)} %get-tuple-element.45), channel_id=1, source_target_pairs={{8,0},{16,8},{24,16},{32,24},{40,32},{48,40},{56,48},{64,56},{72,6... | collective-permute-start | bytes 442376 | tf_op jit(solution)/shard_map/ppermute | solution.py:670
  24.7 9.6 %inner_stage.3 = (f32[128,1024]{1,0:T(8,128)}, f32[128,1024]{1,0:T(8,128)}, f32[128,1024]{1,0:T(8,128)}, bf16[16,144,128]{2,1,0:T(8,128)(2,1)}) custom-call(bf16[16,256,1024]{2,1,0:T(8,128)(2,1)} %amp.9), custom_call_target="tpu_custom_call" | custom-call | flops 100000000 | bytes 6000000 | tf_op jit(solution)/shard_map/inner_stage/pallas_call | solution.py:292
  34.3 0.1 pad_add_fusion.pos
  34.5 1.1 copy-done.12
  35.6 1.0 copy-done.14
  36.6 1.0 copy-done.15
  37.6 1.0 copy-done.16
  38.7 11.3 %tensor_stage.1 = (f32[288,1152]{1,0:T(8,128)S(1)}, f32[288,1152]{1,0:T(8,128)}, f32[288,1152]{1,0:T(8,128)}, f32[288,1152]{1,0:T(8,128)}, f32[256,1024]{1,0:T(8...) custom-call(s32[2]{0:T(128)S(1)} %pad_add_fusion.pos, ...), custom_call_target="tpu_custom_call" | custom-call | flops 100000000 | bytes 20000000 | tf_op jit(solution)/shard_map/tensor_stage/pallas_call | solution.py:460
  50.0 12.9 %all_to_all.20.blocks = f32[8,32,128]{2,1,0:T(8,128)S(1)} all-to-all(f32[8,32,128]{2,1,0:T(8,128)S(1)} %get-tuple-element.54.first_blocks), channel_id=1, replica_groups=mesh['inline'=16,'crosslin'=8] {'crosslin'}, dimensions={0} | all-to-all | bytes 262144 | tf_op jit(solution)/shard_map/all_to_all | solution.py:691
  63.0 1.0 moments_stage.2
  64.0 16.9 %all_to_all.21.moments = f32[16,16,128]{2,1,0:T(8,128)S(1)} all-to-all(f32[16,16,128]{2,1,0:T(8,128)S(1)} %get-tuple-element.55), channel_id=1, replica_groups=mesh['inline'=16,'crosslin'=8] {'inline'}, dimensions={0} | all-to-all | bytes 262144 | tf_op jit(solution)/shard_map/all_to_all | solution.py:693
  81.0 4.6 %image_stage.1 = (f32[256,1024]{1,0:T(8,128)S(1)}, f32[256,1024]{1,0:T(8,128)S(1)}, f32[8,40,128]{2,1,0:T(8,128)S(1)}) custom-call(s32[2]{0:T(128)S(1)} %pad_add_fusion.pos, f32[16,16,128]{2,1,0:T(8,128)S(1)} %all_to_all.21.moments, f32[40,1024]{1,0:T(8,128)S(1)} %get-tuple-element.56.own, f32[40,1024]{1,0:T(8,128)S(1)} %copy-done.11, ...), custom_call_target="tpu_custom_call" | custom-call | flops 100000000 | bytes 10000000 | tf_op jit(solution)/shard_map/image_stage/pallas_call | solution.py:657
  85.6 8.9 %all_to_all.22.blocks = f32[8,40,128]{2,1,0:T(8,128)S(1)} all-to-all(f32[8,40,128]{2,1,0:T(8,128)S(1)} %get-tuple-element.63), channel_id=1, replica_groups=mesh['inline'=16,'crosslin'=8] {'crosslin'}, dimensions={0} | all-to-all | bytes 327680 | tf_op jit(solution)/shard_map/all_to_all | solution.py:691
  94.5 1.0 moments_stage.3
  95.6 11.4 %all_to_all.23.moments = f32[16,24,128]{2,1,0:T(8,128)S(1)} all-to-all(f32[16,24,128]{2,1,0:T(8,128)S(1)} %get-tuple-element.64), channel_id=1, replica_groups=mesh['inline'=16,'crosslin'=8] {'inline'}, dimensions={0} | all-to-all | bytes 393216 | tf_op jit(solution)/shard_map/all_to_all | solution.py:693
  107.0 3.8 %final_stage.1 = (f32[256,1024]{1,0:T(8,128)}, f32[256,1024]{1,0:T(8,128)}, f32[256,1024]{1,0:T(8,128)}) custom-call(s32[2]{0:T(128)S(1)} %pad_add_fusion.pos, f32[16,24,128]{2,1,0:T(8,128)S(1)} %all_to_all.23.moments, f32[40,1024]{1,0:T(8,128)S(1)} %get-tuple-element.65.own, f32[40,1024]{1,0:T(8,128)S(1)} %copy-done.11, f32[40,1024]{1,0:T(8,128)S(1)} %copy-done.10, ...), custom_call_target="tpu_custom_call" | custom-call | flops 100000000 | bytes 10000000 | tf_op jit(solution)/shard_map/final_stage/pallas_call | solution.py:657
  (52 shorter events, 0.1 us)
Async XLA Ops:
  4.0 11.2 %collective-permute-start = (bf16[256,128]{1,0:T(8,128)(2,1)}, bf16[256,128]{1,0:T(8,128)(2,1)S(1)}, u32[]{:S(2)}, u32[]{:S(2)}) collective-permute-start(bf16[256,128]{1,0:T(8,128)(2,1)} %get-tuple-element.36), channel_id=1, source_target_pairs={{0,1},{1,2},{2,3},{3,4},{4,5},{5,6},{6,7},{8,9},{9,10},{10,11},{11... | collective-permute-start | bytes 196616 | tf_op jit(solution)/shard_map/ppermute | solution.py:670
  5.4 9.9 %collective-permute-start.1 = (bf16[256,128]{1,0:T(8,128)(2,1)}, bf16[256,128]{1,0:T(8,128)(2,1)S(1)}, u32[]{:S(2)}, u32[]{:S(2)}) collective-permute-start(bf16[256,128]{1,0:T(8,128)(2,1)} %get-tuple-element.37), channel_id=1, source_target_pairs={{1,0},{2,1},{3,2},{4,3},{5,4},{6,5},{7,6},{9,8},{10,9},{11,10},{12... | collective-permute-start | bytes 196616 | tf_op jit(solution)/shard_map/ppermute | solution.py:670
  19.3 15.1 %collective-permute-start.2 = (bf16[64,1152]{1,0:T(8,128)(2,1)}, bf16[64,1152]{1,0:T(8,128)(2,1)S(1)}, u32[]{:S(2)}, u32[]{:S(2)}) collective-permute-start(bf16[64,1152]{1,0:T(8,128)(2,1)} %get-tuple-element.44), channel_id=1, source_target_pairs={{0,8},{8,16},{16,24},{24,32},{32,40},{40,48},{48,56},{56,64},{64,7... | collective-permute-start | bytes 442376 | tf_op jit(solution)/shard_map/ppermute | solution.py:670
  23.3 11.1 %collective-permute-start.3 = (bf16[64,1152]{1,0:T(8,128)(2,1)}, bf16[64,1152]{1,0:T(8,128)(2,1)S(1)}, u32[]{:S(2)}, u32[]{:S(2)}) collective-permute-start(bf16[64,1152]{1,0:T(8,128)(2,1)} %get-tuple-element.45), channel_id=1, source_target_pairs={{8,0},{16,8},{24,16},{32,24},{40,32},{48,40},{56,48},{64,56},{72,6... | collective-permute-start | bytes 442376 | tf_op jit(solution)/shard_map/ppermute | solution.py:670
  24.6 9.8 %copy-start.2 = (s32[256,1024]{1,0:T(8,128)S(1)}, s32[256,1024]{1,0:T(8,128)}, u32[]{:S(2)}) copy-start(s32[256,1024]{1,0:T(8,128)} %mask.3) | copy-start | bytes 3145732
  24.6 9.8 %copy-start.3 = (f32[256,1024]{1,0:T(8,128)S(1)}, f32[256,1024]{1,0:T(8,128)}, u32[]{:S(2)}) copy-start(f32[256,1024]{1,0:T(8,128)} %v_in.7) | copy-start | bytes 3145732
  24.6 9.8 %copy-start.4 = (s32[256,1024]{1,0:T(8,128)S(1)}, s32[256,1024]{1,0:T(8,128)}, u32[]{:S(2)}) copy-start(s32[256,1024]{1,0:T(8,128)} %depth.1) | copy-start | bytes 3145732
  24.6 9.8 %copy-start.9 = (bf16[1024,128]{1,0:T(8,128)(2,1)S(1)}, bf16[1024,128]{1,0:T(8,128)(2,1)}, u32[]{:S(2)}) copy-start(bf16[1024,128]{1,0:T(8,128)(2,1)} %constant.37.clone.group) | copy-start | bytes 786436
  24.6 9.8 %copy-start.13 = (bf16[16,128,128]{2,1,0:T(8,128)(2,1)S(1)}, bf16[16,128,128]{2,1,0:T(8,128)(2,1)}, u32[]{:S(2)}) copy-start(bf16[16,128,128]{2,1,0:T(8,128)(2,1)} %get-tuple-element.49.rest_3_) | copy-start | bytes 1572868
  24.6 9.8 %copy-start.17 = (f32[112,1024]{1,0:T(8,128)S(1)}, f32[112,1024]{1,0:T(8,128)}, u32[]{:S(2)}) copy-start(f32[112,1024]{1,0:T(8,128)} %get-tuple-element.46.rest_0_) | copy-start | bytes 1376260
  24.6 9.8 %copy-start.18 = (f32[112,1024]{1,0:T(8,128)S(1)}, f32[112,1024]{1,0:T(8,128)}, u32[]{:S(2)}) copy-start(f32[112,1024]{1,0:T(8,128)} %get-tuple-element.47.rest_1_) | copy-start | bytes 1376260
  24.6 9.8 %copy-start.19 = (f32[112,1024]{1,0:T(8,128)S(1)}, f32[112,1024]{1,0:T(8,128)}, u32[]{:S(2)}) copy-start(f32[112,1024]{1,0:T(8,128)} %get-tuple-element.48.rest_2_) | copy-start | bytes 1376260
  24.6 9.8 %copy-start.21 = (bf16[256,128]{1,0:T(8,128)(2,1)S(1)}, bf16[256,128]{1,0:T(8,128)(2,1)}, u32[]{:S(2)}) copy-start(bf16[256,128]{1,0:T(8,128)(2,1)} %copy-done.20) | copy-start | bytes 196612
  24.7 9.8 %copy-start.23 = (bf16[256,128]{1,0:T(8,128)(2,1)S(1)}, bf16[256,128]{1,0:T(8,128)(2,1)}, u32[]{:S(2)}) copy-start(bf16[256,128]{1,0:T(8,128)(2,1)} %copy-done.22) | copy-start | bytes 196612
  38.7 24.2 %copy-start = (bf16[1152,1024]{1,0:T(8,128)(2,1)S(1)}, bf16[1152,1024]{1,0:T(8,128)(2,1)}, u32[]{:S(2)}) copy-start(bf16[1152,1024]{1,0:T(8,128)(2,1)} %constant.39.clone.fwd_lo) | copy-start | bytes 7077892
  38.7 24.2 %copy-start.1 = (bf16[1152,1024]{1,0:T(8,128)(2,1)S(1)}, bf16[1152,1024]{1,0:T(8,128)(2,1)}, u32[]{:S(2)}) copy-start(bf16[1152,1024]{1,0:T(8,128)(2,1)} %constant.38.clone.fwd_hi) | copy-start | bytes 7077892
  38.7 24.2 %copy-start.25 = (f32[8,1024]{1,0:T(8,128)S(1)}, f32[8,1024]{1,0:T(8,128)}, u32[]{:S(2)}) copy-start(f32[8,1024]{1,0:T(8,128)} %constant.40.clone.steps) | copy-start | bytes 98308
  62.9 18.0 %copy-start.5 = (bf16[256,1152]{1,0:T(8,128)(2,1)S(1)}, bf16[256,1152]{1,0:T(8,128)(2,1)}, u32[]{:S(2)}) copy-start(bf16[256,1152]{1,0:T(8,128)(2,1)} %constant.44.clone.spread) | copy-start | bytes 1769476
  62.9 18.0 %copy-start.6 = (f32[288,1152]{1,0:T(8,128)S(1)}, f32[288,1152]{1,0:T(8,128)}, u32[]{:S(2)}) copy-start(f32[288,1152]{1,0:T(8,128)} %get-tuple-element.58.tb) | copy-start | bytes 3981316
  63.0 18.0 %copy-start.7 = (f32[288,1152]{1,0:T(8,128)S(1)}, f32[288,1152]{1,0:T(8,128)}, u32[]{:S(2)}) copy-start(f32[288,1152]{1,0:T(8,128)} %get-tuple-element.59.tc) | copy-start | bytes 3981316
  63.0 18.0 %copy-start.8 = (f32[288,1152]{1,0:T(8,128)S(1)}, f32[288,1152]{1,0:T(8,128)}, u32[]{:S(2)}) copy-start(f32[288,1152]{1,0:T(8,128)} %get-tuple-element.60.z) | copy-start | bytes 3981316
  63.0 18.0 %copy-start.10 = (f32[40,1024]{1,0:T(8,128)S(1)}, f32[40,1024]{1,0:T(8,128)}, u32[]{:S(2)}) copy-start(f32[40,1024]{1,0:T(8,128)} %constant.42.clone.fall) | copy-start | bytes 491524
  63.0 18.0 %copy-start.11 = (f32[40,1024]{1,0:T(8,128)S(1)}, f32[40,1024]{1,0:T(8,128)}, u32[]{:S(2)}) copy-start(f32[40,1024]{1,0:T(8,128)} %constant.41.clone.grow) | copy-start | bytes 491524
  63.0 18.0 %copy-start.26 = (f32[4,8,128]{2,1,0:T(8,128)S(1)}, f32[4,8,128]{2,1,0:T(8,128)}, u32[]{:S(2)}) copy-start(f32[4,8,128]{2,1,0:T(8,128)} %constant.43.clone.blocks) | copy-start | bytes 49156
  (7 other events, 15.3 us)

commit v2 on v1

--- a/solution.py
+++ b/solution.py
@@ -180,33 +180,9 @@
     )(amplitudes, iterate, mask, depth)
 
 
-def pack_rows_kernel(
-    amp, v_in, m_in, d_in, left, right, rows, mix, lanes, out0, out1, a, v, m, d, sems
-):
-    copies = []
-    for side in range(2):
-        copies.append(pltpu.make_async_copy(amp.at[:, pl.ds(side * (RD - 16), 16)], a.at[side], sems.at[side, 0]))
-        for i, (source, to) in enumerate(((v_in, v), (m_in, m), (d_in, d))):
-            copies.append(
-                pltpu.make_async_copy(source.at[pl.ds(side * (RD - 8), 8)], to.at[side], sems.at[side, 1 + i])
-            )
-    for c in copies:
-        c.start()
-    for c in copies:
-        c.wait()
-    at = lax.broadcasted_iota(jnp.int32, (MSG, CD), 0)
+def pack_rows_kernel(lines, left, right, mix, lanes, out0, out1):
     for side, out in enumerate((out0, out1)):
-        middle = dot(rows[side], a[side].reshape(K * 16, CD))
-        split = [p.astype(F32) for p in parts3(v[side])]
-        for l in range(2):
-            row = 6 + l if side else l
-            for part in range(3):
-                middle = jnp.where(at == 48 + 3 * l + part, split[part][row : row + 1], middle)
-        row = 7 if side else 0
-        weight = m[side, row : row + 1].astype(F32)
-        source = weight * (d[side, row : row + 1].astype(F32) - 0.5 * (K - 1))
-        middle = jnp.where(at == 54, weight, jnp.where(at == 55, source, middle))
-        out[:, 128:] = middle.astype(BF16)
+        out[:, 128:] = lines[side]
         total = jnp.zeros((MSG, 128), F32)
         for halo, which in ((left, 1), (right, 0)):
             edge = halo[RD - 16 : RD].astype(F32)[13:16] if side else halo[0:16].astype(F32)[0:3]
@@ -216,63 +192,93 @@
         out[:, 0:128] = total.astype(BF16)
 
 
-def pack_rows(amplitudes, iterate, mask, depth, left, right, rows, mix, lanes):
-    hbm = pl.BlockSpec(memory_space=pltpu.HBM)
+def pack_rows(lines, left, right, mix, lanes):
     vmem = pl.BlockSpec(memory_space=VMEM)
     out = jax.ShapeDtypeStruct((MSG, EC), BF16)
     return pl.pallas_call(
-        pack_rows_kernel, in_specs=[hbm] * 4 + [vmem] * 5, out_specs=[vmem] * 2, out_shape=[out, out],
-        scratch_shapes=[
-            VMEM((2, K, 16, CD), BF16), VMEM((2, 8, CD), F32), VMEM((2, 8, CD), jnp.int32),
-            VMEM((2, 8, CD), jnp.int32), pltpu.SemaphoreType.DMA((2, 4)),
-        ],
-        compiler_params=pltpu.CompilerParams(vmem_limit_bytes=58 * 1024 * 1024),
-        cost_estimate=pl.CostEstimate(flops=10**7, bytes_accessed=2 * 10**6, transcendentals=0),
+        pack_rows_kernel, in_specs=[vmem] * 5, out_specs=[vmem] * 2, out_shape=[out, out],
+        compiler_params=pltpu.CompilerParams(vmem_limit_bytes=54 * 1024 * 1024),
+        cost_estimate=pl.CostEstimate(flops=10**7, bytes_accessed=10**6, transcendentals=0),
         name="pack_rows",
-    )(amplitudes, iterate, mask, depth, left, right, rows, mix, lanes)
-
-
-def gradient_sums(window, off, take):
+    )(lines, left, right, mix, lanes)
+
+
+def row_band(rows, window, lead):
+    at = lax.broadcasted_iota(jnp.int32, (rows, window), 0) + lead
+    to = lax.broadcasted_iota(jnp.int32, (rows, window), 1)
+    return jnp.where(to == at + 1, 1.0, jnp.where(to == at - 1, -1.0, 0.0)).astype(BF16)
+
+
+def gradient_sums(window, band, span, off, take):
     total = None
     for s in range(K):
-        x = window(s).astype(F32)
+        x = window(s)
         n = x.shape[1]
-        middle = x[8:24]
-        gc = (pltpu.roll(middle, n - 1, 1) - pltpu.roll(middle, 1, 1))[:, off : off + take]
-        x = x[:, off : off + take]
-        gi = pltpu.roll(x, 31, 0)[8:24] - pltpu.roll(x, 1, 0)[8:24]
+        middle = x[span]
+        gc = pltpu.roll(middle, n - 1, 1).astype(F32) - pltpu.roll(middle, 1, 1).astype(F32)
+        gc = gc[:, off : off + take]
+        gi = dot(band, x[:, off : off + take])
         terms = (gi * gi, gi * gc, gc * gc)
         total = terms if total is None else tuple(t + u for t, u in zip(total, terms))
     return total
 
 
-def inner_kernel(first, steps, amp, sii_o, sic_o, scc_o, edge_o, a, sems):
-    rows = 16 * (steps + 1)
-    half = 64
-    bounds = [(r, min(half, rows - r)) for r in range(0, rows, half)]
+def edge_lines(side, a, v, m, d, rows):
+    at = lax.broadcasted_iota(jnp.int32, (MSG, CD), 0)
+    middle = dot(rows[side], a.reshape(K * 16, CD))
+    split = [p.astype(F32) for p in parts3(v)]
+    for l in range(2):
+        row = 6 + l if side else l
+        for part in range(3):
+            middle = jnp.where(at == 48 + 3 * l + part, split[part][row : row + 1], middle)
+    row = 7 if side else 0
+    weight = m[row : row + 1].astype(F32)
+    source = weight * (d[row : row + 1].astype(F32) - 0.5 * (K - 1))
+    return jnp.where(at == 54, weight, jnp.where(at == 55, source, middle)).astype(BF16)
+
+
+def inner_kernel(first, steps, edge, amp, *rest):
+    if edge:
+        v_in, m_in, d_in, rows_t, sii_o, sic_o, scc_o, edge_o, lines_o, a, sems, ends, v, m, d, end_sems = rest
+    else:
+        sii_o, sic_o, scc_o, edge_o, a, sems = rest
+    base = 16 * (first - 1)
+    rows = 16 * (steps + 2)
+    bounds = [(0, 48), (48, 48), (96, rows - 96)]
     copies = [
-        pltpu.make_async_copy(amp.at[:, pl.ds(16 * first + r, n)], a.at[:, pl.ds(r, n)], sems.at[i])
+        pltpu.make_async_copy(amp.at[:, pl.ds(base + r, n)], a.at[:, pl.ds(r, n)], sems.at[i])
         for i, (r, n) in enumerate(bounds)
     ]
     for c in copies:
         c.start()
+    if edge:
+        more = [pltpu.make_async_copy(amp.at[:, pl.ds(RD - 16, 16)], ends, end_sems.at[0])]
+        for side in range(2):
+            for i, (source, to) in enumerate(((v_in, v), (m_in, m), (d_in, d))):
+                span = pl.ds(side * (RD - 8), 8)
+                more.append(pltpu.make_async_copy(source.at[span], to.at[side], end_sems.at[1 + 3 * side + i]))
+        for c in more:
+            c.start()
     lane = lax.broadcasted_iota(jnp.int32, (16, 128), 1)
+    band = row_band(16, 48, 16)
 
     def step(t, carry):
         at = pl.multiple_of(16 * t, 16)
         for part in range(2):
             lanes = slice(0, 640) if part == 0 else slice(384, CD)
             off = 0 if part == 0 else 128
-            sums = gradient_sums(lambda s: a[s, pl.ds(at, 32), lanes], off, 512)
+            sums = gradient_sums(lambda s: a[s, pl.ds(at, 48), lanes], band, slice(16, 32), off, 512)
             for o, value in zip((sii_o, sic_o, scc_o), sums):
                 o[pl.ds(at, 16), 512 * part : 512 * part + 512] = value
         return carry
 
     def edges(t, carry):
         at = pl.ds(pl.multiple_of(16 * t, 16), 16)
+        begin = 128 * (base > 0) - base
+        source = pl.ds(pl.multiple_of(16 * t + begin, 16), 16)
         for s in range(K):
-            low = moved(a[s, at, 0:128].astype(F32), 0, 35)
-            high = moved(a[s, at, CD - 128 : CD].astype(F32), 125, 64)
+            low = moved(a[s, source, 0:128].astype(F32), 0, 35)
+            high = moved(a[s, source, CD - 128 : CD].astype(F32), 125, 64)
             tile = jnp.where((lane >= 35) & (lane < 38), low, jnp.where((lane >= 64) & (lane < 67), high, 0.0))
             edge_o[s, at, :] = tile.astype(BF16)
         return carry
@@ -280,24 +286,38 @@
     done = 0
     for i, (r, n) in enumerate(bounds):
         copies[i].wait()
-        until = min(steps, (r + n) // 16 - 1)
+        until = min(steps, (r + n) // 16 - 2)
         lax.fori_loop(done, until, step, 0)
         done = until
-    lax.fori_loop(0, steps + 1, edges, 0)
-
-
-def inner_stage(first, steps, amplitudes):
-    rows = 16 * (steps + 1)
+    lax.fori_loop(0, 8, edges, 0)
+    if edge:
+        for c in more:
+            c.wait()
+        lines_o[0] = edge_lines(0, a[:, 0:16, :], v[0], m[0], d[0], rows_t)
+        lines_o[1] = edge_lines(1, ends[...], v[1], m[1], d[1], rows_t)
+
+
+def inner_stage(first, steps, amplitudes, more=()):
+    rows = 16 * (steps + 2)
+    hbm, vmem = pl.BlockSpec(memory_space=pltpu.HBM), pl.BlockSpec(memory_space=VMEM)
     flat = jax.ShapeDtypeStruct((16 * steps, CD), F32)
+    out_shape = [flat, flat, flat, jax.ShapeDtypeStruct((K, 128, 128), BF16)]
+    scratch = [VMEM((K, rows, CD), BF16), pltpu.SemaphoreType.DMA((3,))]
+    in_specs = [hbm]
+    if more:
+        out_shape += [jax.ShapeDtypeStruct((2, MSG, CD), BF16)]
+        scratch += [
+            VMEM((K, 16, CD), BF16), VMEM((2, 8, CD), F32), VMEM((2, 8, CD), jnp.int32),
+            VMEM((2, 8, CD), jnp.int32), pltpu.SemaphoreType.DMA((7,)),
+        ]
+        in_specs += [hbm, hbm, hbm, vmem]
     return pl.pallas_call(
-        functools.partial(inner_kernel, first, steps),
-        in_specs=[pl.BlockSpec(memory_space=pltpu.HBM)], out_specs=[pl.BlockSpec(memory_space=VMEM)] * 4,
-        out_shape=[flat, flat, flat, jax.ShapeDtypeStruct((K, rows, 128), BF16)],
-        scratch_shapes=[VMEM((K, rows, CD), BF16), pltpu.SemaphoreType.DMA((4,))],
-        compiler_params=pltpu.CompilerParams(vmem_limit_bytes=57 * 1024 * 1024),
+        functools.partial(inner_kernel, first, steps, bool(more)),
+        in_specs=in_specs, out_specs=[vmem] * len(out_shape), out_shape=out_shape, scratch_shapes=scratch,
+        compiler_params=pltpu.CompilerParams(vmem_limit_bytes=(57 if more else 55) * 1024 * 1024),
         cost_estimate=pl.CostEstimate(flops=10**8, bytes_accessed=6 * 10**6, transcendentals=0),
         name="inner_stage",
-    )(amplitudes)
+    )(amplitudes, *more)
 
 
 def block_sums(rows, group):
@@ -312,8 +332,8 @@
      tops, rim, v_ext, w_ext, s_ext, fd, fr, rowsum, sems) = rest
     inner = (slice(16, 16 + RD), slice(128, EC))
     copies = [
-        pltpu.make_async_copy(amp.at[:, 0:16], tops.at[0, :, 16:32, 128:EC], sems.at[0]),
-        pltpu.make_async_copy(amp.at[:, RD - 16 : RD], tops.at[1, :, 0:16, 128:EC], sems.at[1]),
+        pltpu.make_async_copy(amp.at[:, 0:32], tops.at[0, :, 16:48, 128:EC], sems.at[0]),
+        pltpu.make_async_copy(amp.at[:, RD - 32 : RD], tops.at[1, :, 0:32, 128:EC], sems.at[1]),
         pltpu.make_async_copy(v_in, v_ext.at[16 : 16 + RD, 128:EC], sems.at[2]),
     ]
     for c in copies:
@@ -336,22 +356,20 @@
     for s in range(K):
         value = jnp.where(lane < 3, moved(after, 3 * s, 0), 0.0)
         value = jnp.where(lane >= 125, moved(before, 3 * s, 125), value).astype(BF16)
-        tops[0, s, 16:32, 0:128] = value[0:16]
-        tops[1, s, 0:16, 0:128] = value[RD - 16 : RD]
-    for c, (first, steps) in enumerate(cuts):
-        begin, rows = (0 if c == 0 else 16 * first + 16), 16 * (steps + 1)
-        at = begin - 16 * first
-        span, local = slice(begin, 16 * first + rows), slice(at, rows)
+        tops[0, s, 16:48, 0:128] = value[0:32]
+        tops[1, s, 0:32, 0:128] = value[RD - 32 : RD]
+    for c in range(2):
+        span = slice(128 * c, 128 * c + 128)
         turned, turned_after, tile = before[span], after[span], lane[span]
         for s in range(K):
-            value = inner_refs[4 * c + 3][s, local, :].astype(F32)
+            value = inner_refs[4 * c + 3][s].astype(F32)
             value = jnp.where((tile >= 32) & (tile < 35), moved(turned, 3 * s, 32), value)
             value = jnp.where((tile >= 67) & (tile < 70), moved(turned_after, 3 * s, 67), value)
             rim[s, span, :] = value.astype(BF16)
     for side, halo, row in ((1, up, 0), (0, down, 16 + RD)):
         lines = dot(put[side], halo[...])
         for s in range(K):
-            tops[1 - side, s, 16 - 16 * side : 32 - 16 * side, :] = lines[16 * s : 16 * s + 16].astype(BF16)
+            tops[1 - side, s, 32 - 32 * side : 48 - 32 * side, :] = lines[16 * s : 16 * s + 16].astype(BF16)
         v_ext[row : row + 16, :] = lines[256:272]
         w_ext[row : row + 16, :] = lines[272:288]
         s_ext[row : row + 16, :] = lines[288:304]
@@ -389,16 +407,21 @@
         fr[to, :] = tb * dd + tc * dr
 
     for side in range(2):
-        sums = gradient_sums(lambda s, side=side: tops[side, s], 0, EC)
-        finish(8 + side * (RD), sums)
-
+        for half in range(2):
+            lead = 16 * (side + half)
+            sums = gradient_sums(
+                lambda s, side=side: tops[side, s], row_band(16, 48, lead), slice(lead, lead + 16), 0, EC
+            )
+            finish((RD if side else 0) + 16 * half, sums)
+
+    band = row_band(16, 48, 16)
     for c, (first, steps) in enumerate(cuts):
         sii, sic, scc = inner_refs[4 * c : 4 * c + 3]
 
         def step(t, carry, sii=sii, sic=sic, scc=scc, first=first):
             local = pl.ds(pl.multiple_of(16 * (t - first), 16), 16)
-            at = pl.multiple_of(16 * t, 16)
-            edge = gradient_sums(lambda s: rim[s, pl.ds(at, 32), :], 0, 128)
+            at = pl.multiple_of(16 * t - 16, 16)
+            edge = gradient_sums(lambda s: rim[s, pl.ds(at, 48), :], band, slice(16, 32), 0, 128)
             sums = []
             for ref, e in zip((sii, sic, scc), edge):
                 low, high = pltpu.roll(e, 93, 1), pltpu.roll(e, 61, 1)
@@ -414,7 +437,7 @@
                         axis=1,
                     )
                 )
-            finish(pl.multiple_of(24 + 16 * t, 8), sums)
+            finish(pl.multiple_of(16 * t + 16, 16), sums)
             return carry
 
         lax.fori_loop(first, first + steps, step, 0)
@@ -467,11 +490,11 @@
             jax.ShapeDtypeStruct((8, 128), F32),
         ],
         scratch_shapes=[
-            VMEM((2, K, 32, EC), BF16), VMEM((K, RD, 128), BF16), VMEM((ER, EC), F32), VMEM((ER, EC), F32),
+            VMEM((2, K, 48, EC), BF16), VMEM((K, RD, 128), BF16), VMEM((ER + 8, EC), F32), VMEM((ER, EC), F32),
             VMEM((ER, EC), F32), VMEM((ER, EC), F32), VMEM((ER, EC), F32), VMEM((CR, CD), F32),
             pltpu.SemaphoreType.DMA((3,)),
         ],
-        compiler_params=pltpu.CompilerParams(vmem_limit_bytes=42 * 1024 * 1024),
+        compiler_params=pltpu.CompilerParams(vmem_limit_bytes=36 * 1024 * 1024),
         cost_estimate=pl.CostEstimate(flops=10**8, bytes_accessed=2 * 10**7, transcendentals=0),
         name="tensor_stage",
     )(pos, amp, v, mask, depth, up, down, left, right, put, group, *sums)
@@ -676,12 +699,12 @@
     pos = jnp.stack([lax.axis_index("inline"), lax.axis_index("crosslin")]).astype(jnp.int32)
     col_first, col_last = pack_columns(amplitudes, iterate, mask, depth)
     left, right = neighbours(col_first, col_last, "crosslin", n_cr)
-    cuts = ((0, 7), (7, 8))
-    inner = inner_stage(*cuts[0], amplitudes)
-    (left, right), inner = lax.optimization_barrier(((left, right), inner))
-    row_first, row_last = pack_rows(amplitudes, iterate, mask, depth, left, right, rows, mix, lanes)
+    cuts = ((1, 7), (8, 7))
+    *inner, lines = inner_stage(*cuts[0], amplitudes, (iterate, mask, depth, rows))
+    (left, right), lines = lax.optimization_barrier(((left, right), lines))
+    row_first, row_last = pack_rows(lines, left, right, mix, lanes)
     up, down = neighbours(row_first, row_last, "inline", n_in)
-    inner = list(inner) + list(inner_stage(*cuts[1], amplitudes))
+    inner += inner_stage(*cuts[1], amplitudes)
     group = jnp.asarray(tables["group"])
     ta, tb, tc, z, r, rd, blocks, sums = tensor_stage(
         n_in, n_cr, cuts, pos, amplitudes, iterate, mask, depth, up, down, left, right, put, group, inner

time: 111 us -> 112 us (level)
  local copies, waits for them, and re-layouts: 4.92 us -> 8.97 us
  Pallas kernels: 46.7 us -> 43.1 us
    unnamed x54 -> x56, local copies, waits for them, and re-layouts: 4.92 us -> 8.97 us
    pallas_call x3, Pallas kernels: 21.6 us -> 17.7 us  [the longest x2 15.7 us: inner_stage(): pl.pallas_call(functools.partial(inner_kernel, first, steps, bool(more)),...]
  transfers between devices with their start and end apart: 4 -> 4, of which waited for: 0 -> 0; matrix products, arithmetic and copies ran while one was open for 0% -> 0% of each run, Pallas kernels for 16% -> 14%
where the time goes in v2:
time: 112 us; the launch traced here: 111 us
  blocking collectives  50 us (45%)
  Pallas kernels  43.1 us (38%)
  local copies, waits for them, and re-layouts  8.97 us (8%)
  starting transfers between devices  7.79 us (7%)
    all_to_all x2, blocking collectives, moments_of(): return (lax.all_to_all(pay, 'inline', 0, 0, tiled=True), own)  28.2 us
    all_to_all x2, blocking collectives, moments_of(): gathered = lax.all_to_all(payload, 'crosslin', 0, 0, tiled=True)  21.8 us
    pallas_call x2, Pallas kernels, inner_stage(): pl.pallas_call(functools.partial(inner_kernel, first, steps, bool(more)),...  15.7 us
    pallas_call x1, Pallas kernels, tensor_stage(): pl.pallas_call(functools.partial(tensor_kernel, n_in, n_cr, cuts), in_spe...  11.5 us
    unnamed x56, local copies, waits for them, and re-layouts  8.97 us
    pallas_call x2, Pallas kernels, coarse_call(): pl.pallas_call(functools.partial(kernel, n_in, n_cr), in_specs=[pl.BlockS...  8.41 us
    ppermute x2, starting transfers between devices, neighbours(): lax.ppermute(value_high, axis, ahead)  5.21 us
    pallas_call x1, Pallas kernels, pack_columns(): pl.pallas_call(pack_columns_kernel, in_specs=[hbm] * 4, out_specs=[pl.Blo...  3.4 us
  transfers between devices with their start and end apart: 4, of which 0 were waited for; matrix products, arithmetic and copies ran while one was open for 0% of the time, Pallas kernels for 14%

profile of v2, /device:TPU:0, one launch (start us, length us, event | category | flops | bytes accessed | tf_op | source)
XLA Modules:
  0.0 110.9 jit_solution(15313578820628291240)
XLA Ops:
  0.6 3.4 %pack_columns.1 = (bf16[256,128]{1,0:T(8,128)(2,1)}, bf16[256,128]{1,0:T(8,128)(2,1)}) custom-call(bf16[16,256,1024]{2,1,0:T(8,128)(2,1)} %amp.7, f32[256,1024]{1,0:T(8,128)} %v_in.5, s32[256,1024]{1,0:T(8,128)} %mask.3, s32[256,1024]{1,0:T(8,128)} %depth.1), custom_call_target="tpu_custom_call" | custom-call | flops 10000000 | bytes 3000000 | tf_op jit(solution)/shard_map/pack_columns/pallas_call | solution.py:170
  4.0 1.3 %collective-permute-start = (bf16[256,128]{1,0:T(8,128)(2,1)}, bf16[256,128]{1,0:T(8,128)(2,1)S(1)}, u32[]{:S(2)}, u32[]{:S(2)}) collective-permute-start(bf16[256,128]{1,0:T(8,128)(2,1)} %get-tuple-element.34), channel_id=1, source_target_pairs={{0,1},{1,2},{2,3},{3,4},{4,5},{5,6},{6,7},{8,9},{9,10},{10,11},{11... | collective-permute-start | bytes 196616 | tf_op jit(solution)/shard_map/ppermute | solution.py:693
  5.3 1.3 %collective-permute-start.1 = (bf16[256,128]{1,0:T(8,128)(2,1)}, bf16[256,128]{1,0:T(8,128)(2,1)S(1)}, u32[]{:S(2)}, u32[]{:S(2)}) collective-permute-start(bf16[256,128]{1,0:T(8,128)(2,1)} %get-tuple-element.35), channel_id=1, source_target_pairs={{1,0},{2,1},{3,2},{4,3},{5,4},{6,5},{7,6},{9,8},{10,9},{11,10},{12... | collective-permute-start | bytes 196616 | tf_op jit(solution)/shard_map/ppermute | solution.py:693
  6.6 8.5 %inner_stage.2 = (f32[112,1024]{1,0:T(8,128)}, f32[112,1024]{1,0:T(8,128)}, f32[112,1024]{1,0:T(8,128)}, bf16[16,128,128]{2,1,0:T(8,128)(2,1)}, bf16[2,64,1024]{2,1,0:T(8,128)(2,1)}) custom-call(bf16[16,256,1024]{2,1,0:T(8,128)(2,1)} %amp.7, f32[256,1024]{1,0:T(8,128)} %v_in.5, s32[256,1024]{1,0:T(8,128)} %mask.3, s32[256,1024]{1,0:T(8,128)} %depth.1, ...), custom_call_target="tpu_custom_call" | custom-call | flops 100000000 | bytes 6000000 | tf_op jit(solution)/shard_map/inner_stage/pallas_call | solution.py:314
  15.8 2.0 %pack_rows.1 = (bf16[64,1152]{1,0:T(8,128)(2,1)}, bf16[64,1152]{1,0:T(8,128)(2,1)}) custom-call(bf16[2,64,1024]{2,1,0:T(8,128)(2,1)} %get-tuple-element.37.lines, bf16[256,128]{1,0:T(8,128)(2,1)} %copy-done.17, bf16[256,128]{1,0:T(8,128)(2,1)} %copy-done.19, bf16[2,3,64,128]{3,2,1,0:T(8,128)(2,1)} %constant.35.clone.mix, ...), custom_call_target="tpu_custom_call" | custom-call | flops 10000000 | bytes 1000000 | tf_op jit(solution)/shard_map/pack_rows/pallas_call | solution.py:198
  17.8 3.9 %collective-permute-start.2 = (bf16[64,1152]{1,0:T(8,128)(2,1)}, bf16[64,1152]{1,0:T(8,128)(2,1)S(1)}, u32[]{:S(2)}, u32[]{:S(2)}) collective-permute-start(bf16[64,1152]{1,0:T(8,128)(2,1)} %get-tuple-element.40), channel_id=1, source_target_pairs={{0,8},{8,16},{16,24},{24,32},{32,40},{40,48},{48,56},{56,64},{64,7... | collective-permute-start | bytes 442376 | tf_op jit(solution)/shard_map/ppermute | solution.py:693
  21.7 1.3 %collective-permute-start.3 = (bf16[64,1152]{1,0:T(8,128)(2,1)}, bf16[64,1152]{1,0:T(8,128)(2,1)S(1)}, u32[]{:S(2)}, u32[]{:S(2)}) collective-permute-start(bf16[64,1152]{1,0:T(8,128)(2,1)} %get-tuple-element.41), channel_id=1, source_target_pairs={{8,0},{16,8},{24,16},{32,24},{40,32},{48,40},{56,48},{64,56},{72,6... | collective-permute-start | bytes 442376 | tf_op jit(solution)/shard_map/ppermute | solution.py:693
  23.1 7.3 %inner_stage.3 = (f32[112,1024]{1,0:T(8,128)}, f32[112,1024]{1,0:T(8,128)}, f32[112,1024]{1,0:T(8,128)}, bf16[16,128,128]{2,1,0:T(8,128)(2,1)}) custom-call(bf16[16,256,1024]{2,1,0:T(8,128)(2,1)} %amp.7), custom_call_target="tpu_custom_call" | custom-call | flops 100000000 | bytes 6000000 | tf_op jit(solution)/shard_map/inner_stage/pallas_call | solution.py:314
  31.9 1.0 copy-done.10
  32.9 1.0 copy-done.13
  33.9 1.0 copy-done.14
  34.9 1.0 copy-done.15
  36.0 1.0 copy-done.16
  37.0 0.9 copy-done.23
  37.9 0.9 copy-done.25
  38.8 11.5 %tensor_stage.1 = (f32[288,1152]{1,0:T(8,128)S(1)}, f32[288,1152]{1,0:T(8,128)S(1)}, f32[288,1152]{1,0:T(8,128)S(1)}, f32[288,1152]{1,0:T(8,128)S(1)}, f32[256,1...) custom-call(s32[2]{0:T(128)S(1)} %pad_add_fusion.pos, ...), custom_call_target="tpu_custom_call" | custom-call | flops 100000000 | bytes 20000000 | tf_op jit(solution)/shard_map/tensor_stage/pallas_call | solution.py:483
  50.4 12.9 %all_to_all.20.blocks = f32[8,32,128]{2,1,0:T(8,128)S(1)} all-to-all(f32[8,32,128]{2,1,0:T(8,128)S(1)} %get-tuple-element.50.first_blocks), channel_id=1, replica_groups=mesh['inline'=16,'crosslin'=8] {'crosslin'}, dimensions={0} | all-to-all | bytes 262144 | tf_op jit(solution)/shard_map/all_to_all | solution.py:714
  63.3 1.0 moments_stage.2
  64.4 16.8 %all_to_all.21.moments = f32[16,16,128]{2,1,0:T(8,128)S(1)} all-to-all(f32[16,16,128]{2,1,0:T(8,128)S(1)} %get-tuple-element.51), channel_id=1, replica_groups=mesh['inline'=16,'crosslin'=8] {'inline'}, dimensions={0} | all-to-all | bytes 262144 | tf_op jit(solution)/shard_map/all_to_all | solution.py:716
  81.2 4.6 %image_stage.1 = (f32[256,1024]{1,0:T(8,128)S(1)}, f32[256,1024]{1,0:T(8,128)S(1)}, f32[8,40,128]{2,1,0:T(8,128)S(1)}) custom-call(s32[2]{0:T(128)S(1)} %pad_add_fusion.pos, f32[16,16,128]{2,1,0:T(8,128)S(1)} %all_to_all.21.moments, f32[40,1024]{1,0:T(8,128)S(1)} %get-tuple-element.52.own, f32[40,1024]{1,0:T(8,128)S(1)} %copy-done.8, ...), custom_call_target="tpu_custom_call" | custom-call | flops 100000000 | bytes 10000000 | tf_op jit(solution)/shard_map/image_stage/pallas_call | solution.py:680
  85.8 8.9 %all_to_all.22.blocks = f32[8,40,128]{2,1,0:T(8,128)S(1)} all-to-all(f32[8,40,128]{2,1,0:T(8,128)S(1)} %get-tuple-element.59), channel_id=1, replica_groups=mesh['inline'=16,'crosslin'=8] {'crosslin'}, dimensions={0} | all-to-all | bytes 327680 | tf_op jit(solution)/shard_map/all_to_all | solution.py:714
  94.7 1.0 moments_stage.3
  95.7 11.4 %all_to_all.23.moments = f32[16,24,128]{2,1,0:T(8,128)S(1)} all-to-all(f32[16,24,128]{2,1,0:T(8,128)S(1)} %get-tuple-element.60), channel_id=1, replica_groups=mesh['inline'=16,'crosslin'=8] {'inline'}, dimensions={0} | all-to-all | bytes 393216 | tf_op jit(solution)/shard_map/all_to_all | solution.py:716
  107.2 3.8 %final_stage.1 = (f32[256,1024]{1,0:T(8,128)}, f32[256,1024]{1,0:T(8,128)}, f32[256,1024]{1,0:T(8,128)}) custom-call(s32[2]{0:T(128)S(1)} %pad_add_fusion.pos, f32[16,24,128]{2,1,0:T(8,128)S(1)} %all_to_all.23.moments, f32[40,1024]{1,0:T(8,128)S(1)} %get-tuple-element.61.own, f32[40,1024]{1,0:T(8,128)S(1)} %copy-done.8, f32[40,1024]{1,0:T(8,128)S(1)} %copy-done.7, ...), custom_call_target="tpu_custom_call" | custom-call | flops 100000000 | bytes 10000000 | tf_op jit(solution)/shard_map/final_stage/pallas_call | solution.py:680
  (54 shorter events, 2.1 us)
Async XLA Ops:
  4.0 11.1 %collective-permute-start = (bf16[256,128]{1,0:T(8,128)(2,1)}, bf16[256,128]{1,0:T(8,128)(2,1)S(1)}, u32[]{:S(2)}, u32[]{:S(2)}) collective-permute-start(bf16[256,128]{1,0:T(8,128)(2,1)} %get-tuple-element.34), channel_id=1, source_target_pairs={{0,1},{1,2},{2,3},{3,4},{4,5},{5,6},{6,7},{8,9},{9,10},{10,11},{11... | collective-permute-start | bytes 196616 | tf_op jit(solution)/shard_map/ppermute | solution.py:693
  5.3 9.8 %collective-permute-start.1 = (bf16[256,128]{1,0:T(8,128)(2,1)}, bf16[256,128]{1,0:T(8,128)(2,1)S(1)}, u32[]{:S(2)}, u32[]{:S(2)}) collective-permute-start(bf16[256,128]{1,0:T(8,128)(2,1)} %get-tuple-element.35), channel_id=1, source_target_pairs={{1,0},{2,1},{3,2},{4,3},{5,4},{6,5},{7,6},{9,8},{10,9},{11,10},{12... | collective-permute-start | bytes 196616 | tf_op jit(solution)/shard_map/ppermute | solution.py:693
  17.8 12.7 %collective-permute-start.2 = (bf16[64,1152]{1,0:T(8,128)(2,1)}, bf16[64,1152]{1,0:T(8,128)(2,1)S(1)}, u32[]{:S(2)}, u32[]{:S(2)}) collective-permute-start(bf16[64,1152]{1,0:T(8,128)(2,1)} %get-tuple-element.40), channel_id=1, source_target_pairs={{0,8},{8,16},{16,24},{24,32},{32,40},{40,48},{48,56},{56,64},{64,7... | collective-permute-start | bytes 442376 | tf_op jit(solution)/shard_map/ppermute | solution.py:693
  21.7 9.4 %collective-permute-start.3 = (bf16[64,1152]{1,0:T(8,128)(2,1)}, bf16[64,1152]{1,0:T(8,128)(2,1)S(1)}, u32[]{:S(2)}, u32[]{:S(2)}) collective-permute-start(bf16[64,1152]{1,0:T(8,128)(2,1)} %get-tuple-element.41), channel_id=1, source_target_pairs={{8,0},{16,8},{24,16},{32,24},{40,32},{48,40},{56,48},{64,56},{72,6... | collective-permute-start | bytes 442376 | tf_op jit(solution)/shard_map/ppermute | solution.py:693
  23.0 8.8 %copy-start.2 = (s32[256,1024]{1,0:T(8,128)S(1)}, s32[256,1024]{1,0:T(8,128)}, u32[]{:S(2)}) copy-start(s32[256,1024]{1,0:T(8,128)} %mask.3) | copy-start | bytes 3145732
  23.0 8.8 %copy-start.3 = (f32[256,1024]{1,0:T(8,128)S(1)}, f32[256,1024]{1,0:T(8,128)}, u32[]{:S(2)}) copy-start(f32[256,1024]{1,0:T(8,128)} %v_in.5) | copy-start | bytes 3145732
  23.0 8.8 %copy-start.4 = (s32[256,1024]{1,0:T(8,128)S(1)}, s32[256,1024]{1,0:T(8,128)}, u32[]{:S(2)}) copy-start(s32[256,1024]{1,0:T(8,128)} %depth.1) | copy-start | bytes 3145732
  23.0 8.8 %copy-start.6 = (bf16[1024,128]{1,0:T(8,128)(2,1)S(1)}, bf16[1024,128]{1,0:T(8,128)(2,1)}, u32[]{:S(2)}) copy-start(bf16[1024,128]{1,0:T(8,128)(2,1)} %constant.37.clone.group) | copy-start | bytes 786436
  23.1 8.8 %copy-start.9 = (bf16[16,128,128]{2,1,0:T(8,128)(2,1)S(1)}, bf16[16,128,128]{2,1,0:T(8,128)(2,1)}, u32[]{:S(2)}) copy-start(bf16[16,128,128]{2,1,0:T(8,128)(2,1)} %get-tuple-element.45.rest_3_) | copy-start | bytes 1572868
  23.1 8.7 %copy-start.11 = (f32[112,1024]{1,0:T(8,128)S(1)}, f32[112,1024]{1,0:T(8,128)}, u32[]{:S(2)}) copy-start(f32[112,1024]{1,0:T(8,128)} %get-tuple-element.42.rest_0_) | copy-start | bytes 1376260
  23.1 8.7 %copy-start.12 = (f32[112,1024]{1,0:T(8,128)S(1)}, f32[112,1024]{1,0:T(8,128)}, u32[]{:S(2)}) copy-start(f32[112,1024]{1,0:T(8,128)} %get-tuple-element.43.rest_1_) | copy-start | bytes 1376260
  23.1 8.7 %copy-start.18 = (bf16[256,128]{1,0:T(8,128)(2,1)S(1)}, bf16[256,128]{1,0:T(8,128)(2,1)}, u32[]{:S(2)}) copy-start(bf16[256,128]{1,0:T(8,128)(2,1)} %copy-done.17) | copy-start | bytes 196612
  23.1 8.7 %copy-start.20 = (bf16[256,128]{1,0:T(8,128)(2,1)S(1)}, bf16[256,128]{1,0:T(8,128)(2,1)}, u32[]{:S(2)}) copy-start(bf16[256,128]{1,0:T(8,128)(2,1)} %copy-done.19) | copy-start | bytes 196612
  23.1 8.7 %copy-start.21 = (bf16[2,304,64]{2,1,0:T(8,128)(2,1)S(1)}, bf16[2,304,64]{2,1,0:T(8,128)(2,1)}, u32[]{:S(2)}) copy-start(bf16[2,304,64]{2,1,0:T(8,128)(2,1)} %constant.34.clone.put) | copy-start | bytes 233476
  31.9 1.0 copy-start.10
  32.9 1.0 copy-start.13
  33.9 1.0 copy-start.14
  38.8 24.5 %copy-start = (bf16[1152,1024]{1,0:T(8,128)(2,1)S(1)}, bf16[1152,1024]{1,0:T(8,128)(2,1)}, u32[]{:S(2)}) copy-start(bf16[1152,1024]{1,0:T(8,128)(2,1)} %constant.39.clone.fwd_lo) | copy-start | bytes 7077892
  38.8 24.5 %copy-start.1 = (bf16[1152,1024]{1,0:T(8,128)(2,1)S(1)}, bf16[1152,1024]{1,0:T(8,128)(2,1)}, u32[]{:S(2)}) copy-start(bf16[1152,1024]{1,0:T(8,128)(2,1)} %constant.38.clone.fwd_hi) | copy-start | bytes 7077892
  38.8 24.5 %copy-start.26 = (f32[8,1024]{1,0:T(8,128)S(1)}, f32[8,1024]{1,0:T(8,128)}, u32[]{:S(2)}) copy-start(f32[8,1024]{1,0:T(8,128)} %constant.40.clone.steps) | copy-start | bytes 98308
  63.3 17.9 %copy-start.5 = (bf16[256,1152]{1,0:T(8,128)(2,1)S(1)}, bf16[256,1152]{1,0:T(8,128)(2,1)}, u32[]{:S(2)}) copy-start(bf16[256,1152]{1,0:T(8,128)(2,1)} %constant.44.clone.spread) | copy-start | bytes 1769476
  63.3 17.9 %copy-start.7 = (f32[40,1024]{1,0:T(8,128)S(1)}, f32[40,1024]{1,0:T(8,128)}, u32[]{:S(2)}) copy-start(f32[40,1024]{1,0:T(8,128)} %constant.42.clone.fall) | copy-start | bytes 491524
  63.3 17.9 %copy-start.8 = (f32[40,1024]{1,0:T(8,128)S(1)}, f32[40,1024]{1,0:T(8,128)}, u32[]{:S(2)}) copy-start(f32[40,1024]{1,0:T(8,128)} %constant.41.clone.grow) | copy-start | bytes 491524
  63.3 17.9 %copy-start.27 = (f32[4,8,128]{2,1,0:T(8,128)S(1)}, f32[4,8,128]{2,1,0:T(8,128)}, u32[]{:S(2)}) copy-start(f32[4,8,128]{2,1,0:T(8,128)} %constant.43.clone.blocks) | copy-start | bytes 49156
  (8 other events, 6.4 us)

commit v3 on v2

--- a/solution.py
+++ b/solution.py
@@ -25,6 +25,10 @@
 CR = RD // DEC
 CC = CD // DEC
 MSG = 64
+
+
+def in_hbm(x):
+    return pltpu.with_memory_space_constraint(x, pltpu.HBM)
 
 
 def dot(a, b):
@@ -174,10 +178,10 @@
             VMEM((2, K, RD, 128), BF16), VMEM((2, RD, 128), F32), VMEM((2, RD, 128), jnp.int32),
             VMEM((2, RD, 128), jnp.int32), pltpu.SemaphoreType.DMA((2, 4)),
         ],
-        compiler_params=pltpu.CompilerParams(vmem_limit_bytes=60 * 1024 * 1024),
+        compiler_params=pltpu.CompilerParams(vmem_limit_bytes=32 * 1024 * 1024),
         cost_estimate=pl.CostEstimate(flops=10**7, bytes_accessed=3 * 10**6, transcendentals=0),
         name="pack_columns",
-    )(amplitudes, iterate, mask, depth)
+    )(*(in_hbm(x) for x in (amplitudes, iterate, mask, depth)))
 
 
 def pack_rows_kernel(lines, left, right, mix, lanes, out0, out1):
@@ -197,7 +201,7 @@
     out = jax.ShapeDtypeStruct((MSG, EC), BF16)
     return pl.pallas_call(
         pack_rows_kernel, in_specs=[vmem] * 5, out_specs=[vmem] * 2, out_shape=[out, out],
-        compiler_params=pltpu.CompilerParams(vmem_limit_bytes=54 * 1024 * 1024),
+        compiler_params=pltpu.CompilerParams(vmem_limit_bytes=32 * 1024 * 1024),
         cost_estimate=pl.CostEstimate(flops=10**7, bytes_accessed=10**6, transcendentals=0),
         name="pack_rows",
     )(lines, left, right, mix, lanes)
@@ -314,10 +318,10 @@
     return pl.pallas_call(
         functools.partial(inner_kernel, first, steps, bool(more)),
         in_specs=in_specs, out_specs=[vmem] * len(out_shape), out_shape=out_shape, scratch_shapes=scratch,
-        compiler_params=pltpu.CompilerParams(vmem_limit_bytes=(57 if more else 55) * 1024 * 1024),
+        compiler_params=pltpu.CompilerParams(vmem_limit_bytes=32 * 1024 * 1024),
         cost_estimate=pl.CostEstimate(flops=10**8, bytes_accessed=6 * 10**6, transcendentals=0),
         name="inner_stage",
-    )(amplitudes, *more)
+    )(in_hbm(amplitudes), *(in_hbm(x) for x in more[:3]), *more[3:])
 
 
 def block_sums(rows, group):
@@ -494,10 +498,10 @@
             VMEM((ER, EC), F32), VMEM((ER, EC), F32), VMEM((ER, EC), F32), VMEM((CR, CD), F32),
             pltpu.SemaphoreType.DMA((3,)),
         ],
-        compiler_params=pltpu.CompilerParams(vmem_limit_bytes=36 * 1024 * 1024),
+        compiler_params=pltpu.CompilerParams(vmem_limit_bytes=32 * 1024 * 1024),
         cost_estimate=pl.CostEstimate(flops=10**8, bytes_accessed=2 * 10**7, transcendentals=0),
         name="tensor_stage",
-    )(pos, amp, v, mask, depth, up, down, left, right, put, group, *sums)
+    )(pos, in_hbm(amp), in_hbm(v), mask, depth, up, down, left, right, put, group, *sums)
 
 
 def moments_kernel(n_in, n_cr, extra, blocks, fwd_hi, fwd_lo, steps, pay_o, own_o):

time: 112 us -> 97.7 us (0.87)
  local copies, waits for them, and re-layouts: 8.97 us -> 0.1 us
  Pallas kernels: 43.1 us -> 38.2 us
    unnamed x56 -> x30, local copies, waits for them, and re-layouts: 8.97 us -> 0.1 us
    pallas_call x2, Pallas kernels: 15.7 us -> 12.7 us  [inner_stage(): pl.pallas_call(functools.partial(inner_kernel, first, steps, bool(more)),...]
    pallas_call x1, Pallas kernels: 2.01 us -> 0.24 us  [pack_rows(): pl.pallas_call(pack_rows_kernel, in_specs=[vmem] * 5, out_specs=[vmem] *...]
  transfers between devices with their start and end apart: 4 -> 4, of which waited for: 0 -> 0; matrix products, arithmetic and copies ran while one was open for 0% -> 0% of each run, Pallas kernels for 14% -> 13%
where the time goes in v3:
time: 97.7 us; the launch traced here: 97.3 us
  blocking collectives  50.1 us (51%)
  Pallas kernels  38.2 us (39%)
  starting transfers between devices  7.95 us (8%)
    all_to_all x2, blocking collectives, moments_of(): return (lax.all_to_all(pay, 'inline', 0, 0, tiled=True), own)  28.3 us
    all_to_all x2, blocking collectives, moments_of(): gathered = lax.all_to_all(payload, 'crosslin', 0, 0, tiled=True)  21.8 us
    pallas_call x2, Pallas kernels, inner_stage(): pl.pallas_call(functools.partial(inner_kernel, first, steps, bool(more)),...  12.7 us
    pallas_call x1, Pallas kernels, tensor_stage(): pl.pallas_call(functools.partial(tensor_kernel, n_in, n_cr, cuts), in_spe...  12 us
    pallas_call x2, Pallas kernels, coarse_call(): pl.pallas_call(functools.partial(kernel, n_in, n_cr), in_specs=[pl.BlockS...  8.38 us
    ppermute x2, starting transfers between devices, neighbours(): lax.ppermute(value_high, axis, ahead)  5.23 us
    pallas_call x1, Pallas kernels, pack_columns(): pl.pallas_call(pack_columns_kernel, in_specs=[hbm] * 4, out_specs=[pl.Blo...  2.82 us
    ppermute x2, starting transfers between devices, neighbours(): lax.ppermute(value_low, axis, behind)  2.72 us
  transfers between devices with their start and end apart: 4, of which 0 were waited for; matrix products, arithmetic and copies ran while one was open for 0% of the time, Pallas kernels for 13%

profile of v3, /device:TPU:0, one launch (start us, length us, event | category | flops | bytes accessed | tf_op | source)
XLA Modules:
  0.0 97.3 jit_solution(15136484488243464468)
XLA Ops:
  0.6 0.0 copy-start.12
  0.6 2.8 %pack_columns.1 = (bf16[256,128]{1,0:T(8,128)(2,1)S(1)}, bf16[256,128]{1,0:T(8,128)(2,1)S(1)}) custom-call(bf16[16,256,1024]{2,1,0:T(8,128)(2,1)} %amp.7, f32[256,1024]{1,0:T(8,128)} %v_in.5, s32[256,1024]{1,0:T(8,128)} %mask.3, s32[256,1024]{1,0:T(8,128)} %depth.1), custom_call_target="tpu_custom_call" | custom-call | flops 10000000 | bytes 3000000 | tf_op jit(solution)/shard_map/pack_columns/pallas_call | solution.py:174
  3.5 1.3 %collective-permute-start = (bf16[256,128]{1,0:T(8,128)(2,1)S(1)}, bf16[256,128]{1,0:T(8,128)(2,1)S(1)}, u32[]{:S(2)}, u32[]{:S(2)}) collective-permute-start(bf16[256,128]{1,0:T(8,128)(2,1)S(1)} %get-tuple-element.34), channel_id=1, source_target_pairs={{0,1},{1,2},{2,3},{3,4},{4,5},{5,6},{6,7},{8,9},{9,10},{10,11},{11... | collective-permute-start | bytes 196616 | tf_op jit(solution)/shard_map/ppermute | solution.py:697
  4.8 0.0 copy-start.11
  4.8 1.4 %collective-permute-start.1 = (bf16[256,128]{1,0:T(8,128)(2,1)S(1)}, bf16[256,128]{1,0:T(8,128)(2,1)S(1)}, u32[]{:S(2)}, u32[]{:S(2)}) collective-permute-start(bf16[256,128]{1,0:T(8,128)(2,1)S(1)} %get-tuple-element.35), channel_id=1, source_target_pairs={{1,0},{2,1},{3,2},{4,3},{5,4},{6,5},{7,6},{9,8},{10,9},{11,10},{12... | collective-permute-start | bytes 196616 | tf_op jit(solution)/shard_map/ppermute | solution.py:697
  6.2 6.6 %inner_stage.2 = (f32[112,1024]{1,0:T(8,128)S(1)}, f32[112,1024]{1,0:T(8,128)S(1)}, f32[112,1024]{1,0:T(8,128)S(1)}, bf16[16,128,128]{2,1,0:T(8,128)(2,1)S(1)}, bf16[2,64,1024]{2,1,0:T(8,128)(2,1)S(1)}) custom-call(bf16[16,256,1024]{2,1,0:T(8,128)(2,1)} %amp.7, f32[256,1024]{1,0:T(8,128)} %v_in.5, s32[256,1024]{1,0:T(8,128)} %mask.3, s32[256,1024]{1,0:T(8,128)} %depth.1, ...), custom_call_target="tpu_custom_call" | custom-call | flops 100000000 | bytes 6000000 | tf_op jit(solution)/shard_map/inner_stage/pallas_call | solution.py:318
  12.9 0.2 pack_rows.1
  13.1 3.9 %collective-permute-start.2 = (bf16[64,1152]{1,0:T(8,128)(2,1)S(1)}, bf16[64,1152]{1,0:T(8,128)(2,1)S(1)}, u32[]{:S(2)}, u32[]{:S(2)}) collective-permute-start(bf16[64,1152]{1,0:T(8,128)(2,1)S(1)} %get-tuple-element.40), channel_id=1, source_target_pairs={{0,8},{8,16},{16,24},{24,32},{32,40},{40,48},{48,56},{56,64},{64,7... | collective-permute-start | bytes 442376 | tf_op jit(solution)/shard_map/ppermute | solution.py:697
  17.1 1.3 %collective-permute-start.3 = (bf16[64,1152]{1,0:T(8,128)(2,1)S(1)}, bf16[64,1152]{1,0:T(8,128)(2,1)S(1)}, u32[]{:S(2)}, u32[]{:S(2)}) collective-permute-start(bf16[64,1152]{1,0:T(8,128)(2,1)S(1)} %get-tuple-element.41), channel_id=1, source_target_pairs={{8,0},{16,8},{24,16},{32,24},{40,32},{48,40},{56,48},{64,56},{72,6... | collective-permute-start | bytes 442376 | tf_op jit(solution)/shard_map/ppermute | solution.py:697
  18.4 0.0 copy-start.6
  18.4 0.0 copy-start.9
  18.4 6.1 %inner_stage.3 = (f32[112,1024]{1,0:T(8,128)S(1)}, f32[112,1024]{1,0:T(8,128)S(1)}, f32[112,1024]{1,0:T(8,128)S(1)}, bf16[16,128,128]{2,1,0:T(8,128)(2,1)S(1)}) custom-call(bf16[16,256,1024]{2,1,0:T(8,128)(2,1)} %amp.7), custom_call_target="tpu_custom_call" | custom-call | flops 100000000 | bytes 6000000 | tf_op jit(solution)/shard_map/inner_stage/pallas_call | solution.py:318
  24.5 0.1 pad_add_fusion.pos
  24.7 0.0 copy-start
  24.7 0.0 copy-start.1
  24.7 12.0 %tensor_stage.1 = (f32[288,1152]{1,0:T(8,128)S(1)}, f32[288,1152]{1,0:T(8,128)S(1)}, f32[288,1152]{1,0:T(8,128)S(1)}, f32[288,1152]{1,0:T(8,128)S(1)}, f32[256,1...) custom-call(s32[2]{0:T(128)S(1)} %pad_add_fusion.pos, ...), custom_call_target="tpu_custom_call" | custom-call | flops 100000000 | bytes 20000000 | tf_op jit(solution)/shard_map/tensor_stage/pallas_call | solution.py:487
  36.7 12.9 %all_to_all.20.blocks = f32[8,32,128]{2,1,0:T(8,128)S(1)} all-to-all(f32[8,32,128]{2,1,0:T(8,128)S(1)} %get-tuple-element.50.first_blocks), channel_id=1, replica_groups=mesh['inline'=16,'crosslin'=8] {'crosslin'}, dimensions={0} | all-to-all | bytes 262144 | tf_op jit(solution)/shard_map/all_to_all | solution.py:718
  49.7 1.0 %moments_stage.2 = (f32[16,16,128]{2,1,0:T(8,128)S(1)}, f32[40,1024]{1,0:T(8,128)S(1)}) custom-call(f32[8,32,128]{2,1,0:T(8,128)S(1)} %all_to_all.20.blocks, bf16[1152,1024]{1,0:T(8,128)(2,1)S(1)} %copy-done.1, bf16[1152,1024]{1,0:T(8,128)(2,1)S(1)} %copy-done, f32[8,1024]{1,0:T(8,128)S(1)} %copy-done.10), custom_call_target="tpu_custom_call" | custom-call | flops 200000000 | bytes 5000000 | tf_op jit(solution)/shard_map/moments_stage/pallas_call | solution.py:546
  50.7 16.9 %all_to_all.21.moments = f32[16,16,128]{2,1,0:T(8,128)S(1)} all-to-all(f32[16,16,128]{2,1,0:T(8,128)S(1)} %get-tuple-element.51), channel_id=1, replica_groups=mesh['inline'=16,'crosslin'=8] {'inline'}, dimensions={0} | all-to-all | bytes 262144 | tf_op jit(solution)/shard_map/all_to_all | solution.py:720
  67.6 4.6 %image_stage.1 = (f32[256,1024]{1,0:T(8,128)S(1)}, f32[256,1024]{1,0:T(8,128)S(1)}, f32[8,40,128]{2,1,0:T(8,128)S(1)}) custom-call(s32[2]{0:T(128)S(1)} %pad_add_fusion.pos, f32[16,16,128]{2,1,0:T(8,128)S(1)} %all_to_all.21.moments, f32[40,1024]{1,0:T(8,128)S(1)} %get-tuple-element.52.own, f32[40,1024]{1,0:T(8,128)S(1)} %copy-done.8, ...), custom_call_target="tpu_custom_call" | custom-call | flops 100000000 | bytes 10000000 | tf_op jit(solution)/shard_map/image_stage/pallas_call | solution.py:684
  72.2 8.9 %all_to_all.22.blocks = f32[8,40,128]{2,1,0:T(8,128)S(1)} all-to-all(f32[8,40,128]{2,1,0:T(8,128)S(1)} %get-tuple-element.59), channel_id=1, replica_groups=mesh['inline'=16,'crosslin'=8] {'crosslin'}, dimensions={0} | all-to-all | bytes 327680 | tf_op jit(solution)/shard_map/all_to_all | solution.py:718
  81.1 1.0 %moments_stage.3 = (f32[16,24,128]{2,1,0:T(8,128)S(1)}, f32[40,1024]{1,0:T(8,128)S(1)}) custom-call(f32[8,40,128]{2,1,0:T(8,128)S(1)} %all_to_all.22.blocks, bf16[1152,1024]{1,0:T(8,128)(2,1)S(1)} %copy-done.1, bf16[1152,1024]{1,0:T(8,128)(2,1)S(1)} %copy-done, f32[8,1024]{1,0:T(8,128)S(1)} %copy-done.10), custom_call_target="tpu_custom_call" | custom-call | flops 200000000 | bytes 5000000 | tf_op jit(solution)/shard_map/moments_stage/pallas_call | solution.py:546
  82.1 11.4 %all_to_all.23.moments = f32[16,24,128]{2,1,0:T(8,128)S(1)} all-to-all(f32[16,24,128]{2,1,0:T(8,128)S(1)} %get-tuple-element.60), channel_id=1, replica_groups=mesh['inline'=16,'crosslin'=8] {'inline'}, dimensions={0} | all-to-all | bytes 393216 | tf_op jit(solution)/shard_map/all_to_all | solution.py:720
  93.5 3.8 %final_stage.1 = (f32[256,1024]{1,0:T(8,128)}, f32[256,1024]{1,0:T(8,128)}, f32[256,1024]{1,0:T(8,128)}) custom-call(s32[2]{0:T(128)S(1)} %pad_add_fusion.pos, f32[16,24,128]{2,1,0:T(8,128)S(1)} %all_to_all.23.moments, f32[40,1024]{1,0:T(8,128)S(1)} %get-tuple-element.61.own, f32[40,1024]{1,0:T(8,128)S(1)} %copy-done.8, f32[40,1024]{1,0:T(8,128)S(1)} %copy-done.7, ...), custom_call_target="tpu_custom_call" | custom-call | flops 100000000 | bytes 10000000 | tf_op jit(solution)/shard_map/final_stage/pallas_call | solution.py:684
  (28 shorter events, 0.1 us)
Async XLA Ops:
  0.6 5.6 %copy-start.12 = (bf16[2,64,256]{2,1,0:T(8,128)(2,1)S(1)}, bf16[2,64,256]{2,1,0:T(8,128)(2,1)}, u32[]{:S(2)}) copy-start(bf16[2,64,256]{2,1,0:T(8,128)(2,1)} %constant.33.clone.rest_3_) | copy-start | bytes 196612
  3.5 9.4 %collective-permute-start = (bf16[256,128]{1,0:T(8,128)(2,1)S(1)}, bf16[256,128]{1,0:T(8,128)(2,1)S(1)}, u32[]{:S(2)}, u32[]{:S(2)}) collective-permute-start(bf16[256,128]{1,0:T(8,128)(2,1)S(1)} %get-tuple-element.34), channel_id=1, source_target_pairs={{0,1},{1,2},{2,3},{3,4},{4,5},{5,6},{6,7},{8,9},{9,10},{10,11},{11... | collective-permute-start | bytes 196616 | tf_op jit(solution)/shard_map/ppermute | solution.py:697
  4.8 8.1 %copy-start.11 = (bf16[2,3,64,128]{3,2,1,0:T(8,128)(2,1)S(1)}, bf16[2,3,64,128]{3,2,1,0:T(8,128)(2,1)}, u32[]{:S(2)}) copy-start(bf16[2,3,64,128]{3,2,1,0:T(8,128)(2,1)} %constant.35.clone.mix) | copy-start | bytes 294916
  4.8 8.1 %copy-start.14 = (bf16[2,128,128]{2,1,0:T(8,128)(2,1)S(1)}, bf16[2,128,128]{2,1,0:T(8,128)(2,1)}, u32[]{:S(2)}) copy-start(bf16[2,128,128]{2,1,0:T(8,128)(2,1)} %constant.36.clone.lanes) | copy-start | bytes 196612
  4.8 8.1 %collective-permute-start.1 = (bf16[256,128]{1,0:T(8,128)(2,1)S(1)}, bf16[256,128]{1,0:T(8,128)(2,1)S(1)}, u32[]{:S(2)}, u32[]{:S(2)}) collective-permute-start(bf16[256,128]{1,0:T(8,128)(2,1)S(1)} %get-tuple-element.35), channel_id=1, source_target_pairs={{1,0},{2,1},{3,2},{4,3},{5,4},{6,5},{7,6},{9,8},{10,9},{11,10},{12... | collective-permute-start | bytes 196616 | tf_op jit(solution)/shard_map/ppermute | solution.py:697
  13.1 11.5 %collective-permute-start.2 = (bf16[64,1152]{1,0:T(8,128)(2,1)S(1)}, bf16[64,1152]{1,0:T(8,128)(2,1)S(1)}, u32[]{:S(2)}, u32[]{:S(2)}) collective-permute-start(bf16[64,1152]{1,0:T(8,128)(2,1)S(1)} %get-tuple-element.40), channel_id=1, source_target_pairs={{0,8},{8,16},{16,24},{24,32},{32,40},{40,48},{48,56},{56,64},{64,7... | collective-permute-start | bytes 442376 | tf_op jit(solution)/shard_map/ppermute | solution.py:697
  17.1 7.6 %collective-permute-start.3 = (bf16[64,1152]{1,0:T(8,128)(2,1)S(1)}, bf16[64,1152]{1,0:T(8,128)(2,1)S(1)}, u32[]{:S(2)}, u32[]{:S(2)}) collective-permute-start(bf16[64,1152]{1,0:T(8,128)(2,1)S(1)} %get-tuple-element.41), channel_id=1, source_target_pairs={{8,0},{16,8},{24,16},{32,24},{40,32},{48,40},{56,48},{64,56},{72,6... | collective-permute-start | bytes 442376 | tf_op jit(solution)/shard_map/ppermute | solution.py:697
  18.4 6.3 %copy-start.2 = (s32[256,1024]{1,0:T(8,128)S(1)}, s32[256,1024]{1,0:T(8,128)}, u32[]{:S(2)}) copy-start(s32[256,1024]{1,0:T(8,128)} %mask.3) | copy-start | bytes 3145732
  18.4 6.2 %copy-start.4 = (s32[256,1024]{1,0:T(8,128)S(1)}, s32[256,1024]{1,0:T(8,128)}, u32[]{:S(2)}) copy-start(s32[256,1024]{1,0:T(8,128)} %depth.1) | copy-start | bytes 3145732
  18.4 6.2 %copy-start.6 = (bf16[1024,128]{1,0:T(8,128)(2,1)S(1)}, bf16[1024,128]{1,0:T(8,128)(2,1)}, u32[]{:S(2)}) copy-start(bf16[1024,128]{1,0:T(8,128)(2,1)} %constant.37.clone.group) | copy-start | bytes 786436
  18.4 6.2 %copy-start.9 = (bf16[2,304,64]{2,1,0:T(8,128)(2,1)S(1)}, bf16[2,304,64]{2,1,0:T(8,128)(2,1)}, u32[]{:S(2)}) copy-start(bf16[2,304,64]{2,1,0:T(8,128)(2,1)} %constant.34.clone.put) | copy-start | bytes 233476
  24.7 25.0 %copy-start = (bf16[1152,1024]{1,0:T(8,128)(2,1)S(1)}, bf16[1152,1024]{1,0:T(8,128)(2,1)}, u32[]{:S(2)}) copy-start(bf16[1152,1024]{1,0:T(8,128)(2,1)} %constant.39.clone.fwd_lo) | copy-start | bytes 7077892
  24.7 25.0 %copy-start.1 = (bf16[1152,1024]{1,0:T(8,128)(2,1)S(1)}, bf16[1152,1024]{1,0:T(8,128)(2,1)}, u32[]{:S(2)}) copy-start(bf16[1152,1024]{1,0:T(8,128)(2,1)} %constant.38.clone.fwd_hi) | copy-start | bytes 7077892
  24.7 24.9 %copy-start.10 = (f32[8,1024]{1,0:T(8,128)S(1)}, f32[8,1024]{1,0:T(8,128)}, u32[]{:S(2)}) copy-start(f32[8,1024]{1,0:T(8,128)} %constant.40.clone.steps) | copy-start | bytes 98308
  49.6 17.9 %copy-start.5 = (bf16[256,1152]{1,0:T(8,128)(2,1)S(1)}, bf16[256,1152]{1,0:T(8,128)(2,1)}, u32[]{:S(2)}) copy-start(bf16[256,1152]{1,0:T(8,128)(2,1)} %constant.44.clone.spread) | copy-start | bytes 1769476
  49.6 17.9 %copy-start.7 = (f32[40,1024]{1,0:T(8,128)S(1)}, f32[40,1024]{1,0:T(8,128)}, u32[]{:S(2)}) copy-start(f32[40,1024]{1,0:T(8,128)} %constant.42.clone.fall) | copy-start | bytes 491524
  49.7 17.9 %copy-start.8 = (f32[40,1024]{1,0:T(8,128)S(1)}, f32[40,1024]{1,0:T(8,128)}, u32[]{:S(2)}) copy-start(f32[40,1024]{1,0:T(8,128)} %constant.41.clone.grow) | copy-start | bytes 491524
  49.7 17.9 %copy-start.13 = (f32[4,8,128]{2,1,0:T(8,128)S(1)}, f32[4,8,128]{2,1,0:T(8,128)}, u32[]{:S(2)}) copy-start(f32[4,8,128]{2,1,0:T(8,128)} %constant.43.clone.blocks) | copy-start | bytes 49156
  81.1 12.5 %copy-start.3 = (f32[256,1024]{1,0:T(8,128)S(1)}, f32[256,1024]{1,0:T(8,128)}, u32[]{:S(2)}) copy-start(f32[256,1024]{1,0:T(8,128)} %v_in.5) | copy-start | bytes 3145732

commit v4 on v3

--- a/solution.py
+++ b/solution.py
@@ -139,21 +139,28 @@
     return pltpu.roll(x, turn, 1) if turn else x
 
 
-def pack_columns_kernel(amp, v_in, m_in, d_in, out0, out1, a, v, m, d, sems):
+def pack_columns_kernel(amp, v_in, m_in, d_in, out0, out1, amp_o, v, m, d, sems, rest_sem):
     copies = []
     for side, at in enumerate((0, CD - 128)):
         span = pl.ds(at, 128)
-        copies.append(pltpu.make_async_copy(amp.at[:, :, span], a.at[side], sems.at[side, 0]))
+        copies.append(pltpu.make_async_copy(amp.at[:, :, span], amp_o.at[:, :, span], sems.at[side, 0]))
         copies.append(pltpu.make_async_copy(v_in.at[:, span], v.at[side], sems.at[side, 1]))
         copies.append(pltpu.make_async_copy(m_in.at[:, span], m.at[side], sems.at[side, 2]))
         copies.append(pltpu.make_async_copy(d_in.at[:, span], d.at[side], sems.at[side, 3]))
+    middle = pl.ds(128, CD - 256)
+    rest = pltpu.make_async_copy(amp.at[:, :, middle], amp_o.at[:, :, middle], rest_sem)
     for c in copies:
         c.start()
+    rest.start()
     lane = lax.broadcasted_iota(jnp.int32, (RD, 128), 1)
     for c in copies:
         c.wait()
     for side, out in enumerate((out0, out1)):
         low = 125 if side else 0
+
+        def edge(s, side=side):
+            return amp_o[s, :, CD - 128 :] if side else amp_o[s, :, 0:128]
+
         weight = m[side].astype(F32)
         source = weight * (d[side].astype(F32) - 0.5 * (K - 1))
         end = 127 if side else 0
@@ -164,8 +171,9 @@
                 to = 48 + 3 * l + part
                 total = jnp.where(lane == to, moved(value, (126 if side else 0) + l, to), total)
         for s in range(K):
-            total = jnp.where((lane >= 3 * s) & (lane < 3 * s + 3), moved(a[side, s].astype(F32), low, 3 * s), total)
+            total = jnp.where((lane >= 3 * s) & (lane < 3 * s + 3), moved(edge(s).astype(F32), low, 3 * s), total)
         out[...] = jnp.where(lane < 56, total, 0.0).astype(BF16)
+    rest.wait()
 
 
 def pack_columns(amplitudes, iterate, mask, depth):
@@ -173,12 +181,13 @@
     out = jax.ShapeDtypeStruct((RD, 128), BF16)
     return pl.pallas_call(
         pack_columns_kernel, in_specs=[hbm] * 4,
-        out_specs=[pl.BlockSpec(memory_space=VMEM)] * 2, out_shape=[out, out],
+        out_specs=[pl.BlockSpec(memory_space=VMEM)] * 3,
+        out_shape=[out, out, jax.ShapeDtypeStruct((K, RD, CD), BF16)],
         scratch_shapes=[
-            VMEM((2, K, RD, 128), BF16), VMEM((2, RD, 128), F32), VMEM((2, RD, 128), jnp.int32),
-            VMEM((2, RD, 128), jnp.int32), pltpu.SemaphoreType.DMA((2, 4)),
+            VMEM((2, RD, 128), F32), VMEM((2, RD, 128), jnp.int32),
+            VMEM((2, RD, 128), jnp.int32), pltpu.SemaphoreType.DMA((2, 4)), pltpu.SemaphoreType.DMA,
         ],
-        compiler_params=pltpu.CompilerParams(vmem_limit_bytes=32 * 1024 * 1024),
+        compiler_params=pltpu.CompilerParams(vmem_limit_bytes=12 * 1024 * 1024),
         cost_estimate=pl.CostEstimate(flops=10**7, bytes_accessed=3 * 10**6, transcendentals=0),
         name="pack_columns",
     )(*(in_hbm(x) for x in (amplitudes, iterate, mask, depth)))
@@ -201,7 +210,7 @@
     out = jax.ShapeDtypeStruct((MSG, EC), BF16)
     return pl.pallas_call(
         pack_rows_kernel, in_specs=[vmem] * 5, out_specs=[vmem] * 2, out_shape=[out, out],
-        compiler_params=pltpu.CompilerParams(vmem_limit_bytes=32 * 1024 * 1024),
+        compiler_params=pltpu.CompilerParams(vmem_limit_bytes=12 * 1024 * 1024),
         cost_estimate=pl.CostEstimate(flops=10**7, bytes_accessed=10**6, transcendentals=0),
         name="pack_rows",
     )(lines, left, right, mix, lanes)
@@ -243,24 +252,16 @@
 
 def inner_kernel(first, steps, edge, amp, *rest):
     if edge:
-        v_in, m_in, d_in, rows_t, sii_o, sic_o, scc_o, edge_o, lines_o, a, sems, ends, v, m, d, end_sems = rest
+        v_in, m_in, d_in, rows_t, sii_o, sic_o, scc_o, edge_o, lines_o, v, m, d, end_sems = rest
     else:
-        sii_o, sic_o, scc_o, edge_o, a, sems = rest
+        sii_o, sic_o, scc_o, edge_o = rest
     base = 16 * (first - 1)
-    rows = 16 * (steps + 2)
-    bounds = [(0, 48), (48, 48), (96, rows - 96)]
-    copies = [
-        pltpu.make_async_copy(amp.at[:, pl.ds(base + r, n)], a.at[:, pl.ds(r, n)], sems.at[i])
-        for i, (r, n) in enumerate(bounds)
-    ]
-    for c in copies:
-        c.start()
     if edge:
-        more = [pltpu.make_async_copy(amp.at[:, pl.ds(RD - 16, 16)], ends, end_sems.at[0])]
+        more = []
         for side in range(2):
             for i, (source, to) in enumerate(((v_in, v), (m_in, m), (d_in, d))):
                 span = pl.ds(side * (RD - 8), 8)
-                more.append(pltpu.make_async_copy(source.at[span], to.at[side], end_sems.at[1 + 3 * side + i]))
+                more.append(pltpu.make_async_copy(source.at[span], to.at[side], end_sems.at[3 * side + i]))
         for c in more:
             c.start()
     lane = lax.broadcasted_iota(jnp.int32, (16, 128), 1)
@@ -268,60 +269,54 @@
 
     def step(t, carry):
         at = pl.multiple_of(16 * t, 16)
+        window = pl.ds(pl.multiple_of(base + 16 * t, 16), 48)
         for part in range(2):
             lanes = slice(0, 640) if part == 0 else slice(384, CD)
             off = 0 if part == 0 else 128
-            sums = gradient_sums(lambda s: a[s, pl.ds(at, 48), lanes], band, slice(16, 32), off, 512)
+            sums = gradient_sums(lambda s: amp[s, window, lanes], band, slice(16, 32), off, 512)
             for o, value in zip((sii_o, sic_o, scc_o), sums):
                 o[pl.ds(at, 16), 512 * part : 512 * part + 512] = value
         return carry
 
     def edges(t, carry):
         at = pl.ds(pl.multiple_of(16 * t, 16), 16)
-        begin = 128 * (base > 0) - base
-        source = pl.ds(pl.multiple_of(16 * t + begin, 16), 16)
+        source = pl.ds(pl.multiple_of(16 * t + 128 * (base > 0), 16), 16)
         for s in range(K):
-            low = moved(a[s, source, 0:128].astype(F32), 0, 35)
-            high = moved(a[s, source, CD - 128 : CD].astype(F32), 125, 64)
+            low = moved(amp[s, source, 0:128].astype(F32), 0, 35)
+            high = moved(amp[s, source, CD - 128 : CD].astype(F32), 125, 64)
             tile = jnp.where((lane >= 35) & (lane < 38), low, jnp.where((lane >= 64) & (lane < 67), high, 0.0))
             edge_o[s, at, :] = tile.astype(BF16)
         return carry
 
-    done = 0
-    for i, (r, n) in enumerate(bounds):
-        copies[i].wait()
-        until = min(steps, (r + n) // 16 - 2)
-        lax.fori_loop(done, until, step, 0)
-        done = until
+    lax.fori_loop(0, steps, step, 0)
     lax.fori_loop(0, 8, edges, 0)
     if edge:
         for c in more:
             c.wait()
-        lines_o[0] = edge_lines(0, a[:, 0:16, :], v[0], m[0], d[0], rows_t)
-        lines_o[1] = edge_lines(1, ends[...], v[1], m[1], d[1], rows_t)
+        lines_o[0] = edge_lines(0, amp[:, 0:16, :], v[0], m[0], d[0], rows_t)
+        lines_o[1] = edge_lines(1, amp[:, RD - 16 :, :], v[1], m[1], d[1], rows_t)
 
 
 def inner_stage(first, steps, amplitudes, more=()):
-    rows = 16 * (steps + 2)
     hbm, vmem = pl.BlockSpec(memory_space=pltpu.HBM), pl.BlockSpec(memory_space=VMEM)
     flat = jax.ShapeDtypeStruct((16 * steps, CD), F32)
     out_shape = [flat, flat, flat, jax.ShapeDtypeStruct((K, 128, 128), BF16)]
-    scratch = [VMEM((K, rows, CD), BF16), pltpu.SemaphoreType.DMA((3,))]
-    in_specs = [hbm]
+    scratch = []
+    in_specs = [vmem]
     if more:
         out_shape += [jax.ShapeDtypeStruct((2, MSG, CD), BF16)]
         scratch += [
-            VMEM((K, 16, CD), BF16), VMEM((2, 8, CD), F32), VMEM((2, 8, CD), jnp.int32),
-            VMEM((2, 8, CD), jnp.int32), pltpu.SemaphoreType.DMA((7,)),
+            VMEM((2, 8, CD), F32), VMEM((2, 8, CD), jnp.int32), VMEM((2, 8, CD), jnp.int32),
+            pltpu.SemaphoreType.DMA((6,)),
         ]
         in_specs += [hbm, hbm, hbm, vmem]
     return pl.pallas_call(
         functools.partial(inner_kernel, first, steps, bool(more)),
         in_specs=in_specs, out_specs=[vmem] * len(out_shape), out_shape=out_shape, scratch_shapes=scratch,
-        compiler_params=pltpu.CompilerParams(vmem_limit_bytes=32 * 1024 * 1024),
+        compiler_params=pltpu.CompilerParams(vmem_limit_bytes=14 * 1024 * 1024),
         cost_estimate=pl.CostEstimate(flops=10**8, bytes_accessed=6 * 10**6, transcendentals=0),
         name="inner_stage",
-    )(in_hbm(amplitudes), *(in_hbm(x) for x in more[:3]), *more[3:])
+    )(amplitudes, *(in_hbm(x) for x in more[:3]), *more[3:])
 
 
 def block_sums(rows, group):
@@ -333,7 +328,7 @@
 ):
     inner_refs, rest = rest[: 4 * len(cuts)], rest[4 * len(cuts) :]
     (ta_o, tb_o, tc_o, z_o, r_o, rd_o, blocks_o, sums_o,
-     tops, rim, v_ext, w_ext, s_ext, fd, fr, rowsum, sems) = rest
+     tops, rim, rim_sums, v_ext, w_ext, s_ext, fd, fr, rowsum, sems) = rest
     inner = (slice(16, 16 + RD), slice(128, EC))
     copies = [
         pltpu.make_async_copy(amp.at[:, 0:32], tops.at[0, :, 16:48, 128:EC], sems.at[0]),
@@ -418,16 +413,25 @@
             )
             finish((RD if side else 0) + 16 * half, sums)
 
-    band = row_band(16, 48, 16)
+    wide = row_band(32, 64, 16)
+
+    def rim_step(t, carry):
+        at = pl.multiple_of(32 * t, 32)
+        edge = gradient_sums(lambda s: rim[s, pl.ds(at, 64), :], wide, slice(16, 48), 0, 128)
+        for i, e in enumerate(edge):
+            rim_sums[i, pl.ds(pl.multiple_of(at + 16, 16), 32), :] = e
+        return carry
+
+    lax.fori_loop(0, RD // 32 - 1, rim_step, 0)
+
     for c, (first, steps) in enumerate(cuts):
         sii, sic, scc = inner_refs[4 * c : 4 * c + 3]
 
         def step(t, carry, sii=sii, sic=sic, scc=scc, first=first):
             local = pl.ds(pl.multiple_of(16 * (t - first), 16), 16)
-            at = pl.multiple_of(16 * t - 16, 16)
-            edge = gradient_sums(lambda s: rim[s, pl.ds(at, 48), :], band, slice(16, 32), 0, 128)
+            at = pl.ds(pl.multiple_of(16 * t, 16), 16)
             sums = []
-            for ref, e in zip((sii, sic, scc), edge):
+            for ref, e in zip((sii, sic, scc), (rim_sums[i, at, :] for i in range(3))):
                 low, high = pltpu.roll(e, 93, 1), pltpu.roll(e, 61, 1)
                 x = ref[local, :]
                 sums.append(
@@ -486,7 +490,7 @@
     flat = jax.ShapeDtypeStruct((RD, CD), F32)
     return pl.pallas_call(
         functools.partial(tensor_kernel, n_in, n_cr, cuts),
-        in_specs=[pl.BlockSpec(memory_space=pltpu.SMEM), hbm, hbm] + [vmem] * (8 + len(sums)),
+        in_specs=[pl.BlockSpec(memory_space=pltpu.SMEM), pl.BlockSpec(memory_space=pl.ANY), hbm] + [vmem] * (8 + len(sums)),
         out_specs=[vmem] * 8,
         out_shape=[
             ext, ext, ext, ext, flat, flat,
@@ -494,14 +498,14 @@
             jax.ShapeDtypeStruct((8, 128), F32),
         ],
         scratch_shapes=[
-            VMEM((2, K, 48, EC), BF16), VMEM((K, RD, 128), BF16), VMEM((ER + 8, EC), F32), VMEM((ER, EC), F32),
+            VMEM((2, K, 48, EC), BF16), VMEM((K, RD, 128), BF16), VMEM((3, RD, 128), F32), VMEM((ER + 8, EC), F32), VMEM((ER, EC), F32),
             VMEM((ER, EC), F32), VMEM((ER, EC), F32), VMEM((ER, EC), F32), VMEM((CR, CD), F32),
             pltpu.SemaphoreType.DMA((3,)),
         ],
-        compiler_params=pltpu.CompilerParams(vmem_limit_bytes=32 * 1024 * 1024),
+        compiler_params=pltpu.CompilerParams(vmem_limit_bytes=28 * 1024 * 1024),
         cost_estimate=pl.CostEstimate(flops=10**8, bytes_accessed=2 * 10**7, transcendentals=0),
         name="tensor_stage",
-    )(pos, in_hbm(amp), in_hbm(v), mask, depth, up, down, left, right, put, group, *sums)
+    )(pos, amp, in_hbm(v), mask, depth, up, down, left, right, put, group, *sums)
 
 
 def moments_kernel(n_in, n_cr, extra, blocks, fwd_hi, fwd_lo, steps, pay_o, own_o):
@@ -550,7 +554,7 @@
             jax.ShapeDtypeStruct((n_in, 2 * n_cr + 8 * extra, 128), F32),
             jax.ShapeDtypeStruct((40, CC * n_cr), F32),
         ],
-        compiler_params=pltpu.CompilerParams(vmem_limit_bytes=32 * 1024 * 1024),
+        compiler_params=pltpu.CompilerParams(vmem_limit_bytes=12 * 1024 * 1024),
         cost_estimate=pl.CostEstimate(flops=2 * 10**8, bytes_accessed=5 * 10**6, transcendentals=0),
         name="moments_stage",
     )(blocks, fwd_hi, fwd_lo, steps)
@@ -685,7 +689,7 @@
         functools.partial(kernel, n_in, n_cr),
         in_specs=[pl.BlockSpec(memory_space=pltpu.SMEM)] + [vmem] * len(args),
         out_specs=[vmem] * len(out_shape), out_shape=out_shape, scratch_shapes=scratch,
-        compiler_params=pltpu.CompilerParams(vmem_limit_bytes=32 * 1024 * 1024),
+        compiler_params=pltpu.CompilerParams(vmem_limit_bytes=22 * 1024 * 1024),
         cost_estimate=pl.CostEstimate(flops=10**8, bytes_accessed=10**7, transcendentals=0),
         name=name,
     )(pos, *args)
@@ -701,17 +705,17 @@
     rows, put, mix, lanes = (jnp.asarray(t) for t in line_tables())
     tables = coarse_tables(n_in, n_cr)
     pos = jnp.stack([lax.axis_index("inline"), lax.axis_index("crosslin")]).astype(jnp.int32)
-    col_first, col_last = pack_columns(amplitudes, iterate, mask, depth)
+    col_first, col_last, local = pack_columns(amplitudes, iterate, mask, depth)
     left, right = neighbours(col_first, col_last, "crosslin", n_cr)
     cuts = ((1, 7), (8, 7))
-    *inner, lines = inner_stage(*cuts[0], amplitudes, (iterate, mask, depth, rows))
+    *inner, lines = inner_stage(*cuts[0], local, (iterate, mask, depth, rows))
     (left, right), lines = lax.optimization_barrier(((left, right), lines))
     row_first, row_last = pack_rows(lines, left, right, mix, lanes)
     up, down = neighbours(row_first, row_last, "inline", n_in)
-    inner += inner_stage(*cuts[1], amplitudes)
+    inner += inner_stage(*cuts[1], local)
     group = jnp.asarray(tables["group"])
     ta, tb, tc, z, r, rd, blocks, sums = tensor_stage(
-        n_in, n_cr, cuts, pos, amplitudes, iterate, mask, depth, up, down, left, right, put, group, inner
+        n_in, n_cr, cuts, pos, local, iterate, mask, depth, up, down, left, right, put, group, inner
     )
 
     def moments_of(payload, extra):

time: 97.7 us -> 103 us (1.054)
  local copies, waits for them, and re-layouts: 0.1 us -> 7.94 us
  Pallas kernels: 38.2 us -> 35.8 us
    unnamed x30 -> x44, local copies, waits for them, and re-layouts: 0.1 us -> 7.94 us
    pallas_call x2, Pallas kernels: 12.7 us -> 9.6 us  [inner_stage(): pl.pallas_call(functools.partial(inner_kernel, first, steps, bool(more)),...]
  transfers between devices with their start and end apart: 4 -> 4, of which waited for: 0 -> 0; matrix products, arithmetic and copies ran while one was open for 0% -> 0% of each run, Pallas kernels for 13% -> 9%
where the time goes in v4:
time: 103 us
  blocking collectives  49.8 us (48%)
  Pallas kernels  35.8 us (35%)
  starting transfers between devices  8.42 us (8%)
  local copies, waits for them, and re-layouts  7.94 us (8%)
    all_to_all x2, blocking collectives, moments_of(): return (lax.all_to_all(pay, 'inline', 0, 0, tiled=True), own)  28 us
    all_to_all x2, blocking collectives, moments_of(): gathered = lax.all_to_all(payload, 'crosslin', 0, 0, tiled=True)  21.8 us
    pallas_call x1, Pallas kernels, tensor_stage(): pl.pallas_call(functools.partial(tensor_kernel, n_in, n_cr, cuts), in_spe...  11 us
    pallas_call x2, Pallas kernels, inner_stage(): pl.pallas_call(functools.partial(inner_kernel, first, steps, bool(more)),...  9.6 us
    pallas_call x2, Pallas kernels, coarse_call(): pl.pallas_call(functools.partial(kernel, n_in, n_cr), in_specs=[pl.BlockS...  8.4 us
    unnamed x44, local copies, waits for them, and re-layouts  7.94 us
    ppermute x2, starting transfers between devices, neighbours(): lax.ppermute(value_high, axis, ahead)  5.85 us
    pallas_call x1, Pallas kernels, pack_columns(): pl.pallas_call(pack_columns_kernel, in_specs=[hbm] * 4, out_specs=[pl.Blo...  3.83 us
  transfers between devices with their start and end apart: 4, of which 0 were waited for; matrix products, arithmetic and copies ran while one was open for 0% of the time, Pallas kernels for 9%

profile of v4, /device:TPU:0, one launch (start us, length us, event | category | flops | bytes accessed | tf_op | source)
XLA Modules:
  0.0 103.0 jit_solution(1248863512334218641)
XLA Ops:
  0.6 3.8 %pack_columns.1 = (bf16[256,128]{1,0:T(8,128)(2,1)S(1)}, bf16[256,128]{1,0:T(8,128)(2,1)S(1)}, bf16[16,256,1024]{2,1,0:T(8,128)(2,1)S(1)}) custom-call(bf16[16,256,1024]{2,1,0:T(8,128)(2,1)} %amp.1, f32[256,1024]{1,0:T(8,128)} %v_in.5, s32[256,1024]{1,0:T(8,128)} %mask.3, s32[256,1024]{1,0:T(8,128)} %depth.1), custom_call_target="tpu_custom_call" | custom-call | flops 10000000 | bytes 3000000 | tf_op jit(solution)/shard_map/pack_columns/pallas_call | solution.py:182
  4.5 1.3 %collective-permute-start = (bf16[256,128]{1,0:T(8,128)(2,1)S(1)}, bf16[256,128]{1,0:T(8,128)(2,1)S(1)}, u32[]{:S(2)}, u32[]{:S(2)}) collective-permute-start(bf16[256,128]{1,0:T(8,128)(2,1)S(1)} %get-tuple-element.36), channel_id=1, source_target_pairs={{0,1},{1,2},{2,3},{3,4},{4,5},{5,6},{6,7},{8,9},{9,10},{10,11},{11... | collective-permute-start | bytes 196616 | tf_op jit(solution)/shard_map/ppermute | solution.py:701
  5.8 1.3 %collective-permute-start.1 = (bf16[256,128]{1,0:T(8,128)(2,1)S(1)}, bf16[256,128]{1,0:T(8,128)(2,1)S(1)}, u32[]{:S(2)}, u32[]{:S(2)}) collective-permute-start(bf16[256,128]{1,0:T(8,128)(2,1)S(1)} %get-tuple-element.37), channel_id=1, source_target_pairs={{1,0},{2,1},{3,2},{4,3},{5,4},{6,5},{7,6},{9,8},{10,9},{11,10},{12... | collective-permute-start | bytes 196616 | tf_op jit(solution)/shard_map/ppermute | solution.py:701
  7.1 5.0 %inner_stage.2 = (f32[112,1024]{1,0:T(8,128)S(1)}, f32[112,1024]{1,0:T(8,128)S(1)}, f32[112,1024]{1,0:T(8,128)S(1)}, bf16[16,128,128]{2,1,0:T(8,128)(2,1)S(1)}, bf16[2,64,1024]{2,1,0:T(8,128)(2,1)S(1)}) custom-call(bf16[16,256,1024]{2,1,0:T(8,128)(2,1)S(1)} %get-tuple-element.35.amp, f32[256,1024]{1,0:T(8,128)} %v_in.5, s32[256,1024]{1,0:T(8,128)} %mask.3, ...), custom_call_target="tpu_custom_call" | custom-call | flops 100000000 | bytes 6000000 | tf_op jit(solution)/shard_map/inner_stage/pallas_call | solution.py:313
  12.2 0.8 copy-done.12
  12.9 0.8 copy-done.14
  13.7 1.0 pack_rows.1
  14.7 4.6 %collective-permute-start.2 = (bf16[64,1152]{1,0:T(8,128)(2,1)}, bf16[64,1152]{1,0:T(8,128)(2,1)}, u32[]{:S(2)}, u32[]{:S(2)}) collective-permute-start(bf16[64,1152]{1,0:T(8,128)(2,1)} %get-tuple-element.42), channel_id=1, source_target_pairs={{0,8},{8,16},{16,24},{24,32},{32,40},{40,48},{48,56},{56,64},{64,7... | collective-permute-start | bytes 442376 | tf_op jit(solution)/shard_map/ppermute | solution.py:701
  19.3 1.3 %collective-permute-start.3 = (bf16[64,1152]{1,0:T(8,128)(2,1)}, bf16[64,1152]{1,0:T(8,128)(2,1)}, u32[]{:S(2)}, u32[]{:S(2)}) collective-permute-start(bf16[64,1152]{1,0:T(8,128)(2,1)} %get-tuple-element.43), channel_id=1, source_target_pairs={{8,0},{16,8},{24,16},{32,24},{40,32},{48,40},{56,48},{64,56},{72,6... | collective-permute-start | bytes 442376 | tf_op jit(solution)/shard_map/ppermute | solution.py:701
  20.6 3.4 %copy-done.1 = bf16[16,256,1024]{2,1,0:T(8,128)(2,1)S(1)} copy-done((bf16[16,256,1024]{2,1,0:T(8,128)(2,1)S(1)}, bf16[16,256,1024]{2,1,0:T(8,128)(2,1)}, u32[]{:S(2)}) %copy-start.1) | copy-done | bytes 8388632
  23.9 4.6 %inner_stage.3 = (f32[112,1024]{1,0:T(8,128)S(1)}, f32[112,1024]{1,0:T(8,128)S(1)}, f32[112,1024]{1,0:T(8,128)S(1)}, bf16[16,128,128]{2,1,0:T(8,128)(2,1)S(1)}) custom-call(bf16[16,256,1024]{2,1,0:T(8,128)(2,1)S(1)} %copy-done.1), custom_call_target="tpu_custom_call" | custom-call | flops 100000000 | bytes 6000000 | tf_op jit(solution)/shard_map/inner_stage/pallas_call | solution.py:313
  28.5 0.1 pad_add_fusion.pos
  28.7 1.0 copy-done.13
  29.7 1.0 copy-done.15
  30.7 0.9 copy-done.16
  31.6 11.0 %tensor_stage.1 = (f32[288,1152]{1,0:T(8,128)S(1)}, f32[288,1152]{1,0:T(8,128)S(1)}, f32[288,1152]{1,0:T(8,128)S(1)}, f32[288,1152]{1,0:T(8,128)S(1)}, f32[256,1...) custom-call(s32[2]{0:T(128)S(1)} %pad_add_fusion.pos, ...), custom_call_target="tpu_custom_call" | custom-call | flops 100000000 | bytes 20000000 | tf_op jit(solution)/shard_map/tensor_stage/pallas_call | solution.py:491
  42.6 12.9 %all_to_all.20.blocks = f32[8,32,128]{2,1,0:T(8,128)S(1)} all-to-all(f32[8,32,128]{2,1,0:T(8,128)S(1)} %get-tuple-element.52.first_blocks), channel_id=1, replica_groups=mesh['inline'=16,'crosslin'=8] {'crosslin'}, dimensions={0} | all-to-all | bytes 262144 | tf_op jit(solution)/shard_map/all_to_all | solution.py:722
  55.6 1.0 moments_stage.2
  56.6 16.6 %all_to_all.21.moments = f32[16,16,128]{2,1,0:T(8,128)S(1)} all-to-all(f32[16,16,128]{2,1,0:T(8,128)S(1)} %get-tuple-element.53), channel_id=1, replica_groups=mesh['inline'=16,'crosslin'=8] {'inline'}, dimensions={0} | all-to-all | bytes 262144 | tf_op jit(solution)/shard_map/all_to_all | solution.py:724
  73.2 4.6 %image_stage.1 = (f32[256,1024]{1,0:T(8,128)S(1)}, f32[256,1024]{1,0:T(8,128)S(1)}, f32[8,40,128]{2,1,0:T(8,128)S(1)}) custom-call(s32[2]{0:T(128)S(1)} %pad_add_fusion.pos, f32[16,16,128]{2,1,0:T(8,128)S(1)} %all_to_all.21.moments, f32[40,1024]{1,0:T(8,128)S(1)} %get-tuple-element.54.own, f32[40,1024]{1,0:T(8,128)S(1)} %copy-done.11, ...), custom_call_target="tpu_custom_call" | custom-call | flops 100000000 | bytes 10000000 | tf_op jit(solution)/shard_map/image_stage/pallas_call | solution.py:688
  77.9 8.9 %all_to_all.22.blocks = f32[8,40,128]{2,1,0:T(8,128)S(1)} all-to-all(f32[8,40,128]{2,1,0:T(8,128)S(1)} %get-tuple-element.61), channel_id=1, replica_groups=mesh['inline'=16,'crosslin'=8] {'crosslin'}, dimensions={0} | all-to-all | bytes 327680 | tf_op jit(solution)/shard_map/all_to_all | solution.py:722
  86.7 1.0 %moments_stage.3 = (f32[16,24,128]{2,1,0:T(8,128)S(1)}, f32[40,1024]{1,0:T(8,128)S(1)}) custom-call(f32[8,40,128]{2,1,0:T(8,128)S(1)} %all_to_all.22.blocks, bf16[1152,1024]{1,0:T(8,128)(2,1)S(1)} %copy-done.4, bf16[1152,1024]{1,0:T(8,128)(2,1)S(1)} %copy-done.3, f32[8,1024]{1,0:T(8,128)S(1)} %copy-done.17), custom_call_target="tpu_custom_call" | custom-call | flops 200000000 | bytes 5000000 | tf_op jit(solution)/shard_map/moments_stage/pallas_call | solution.py:550
  87.8 11.4 %all_to_all.23.moments = f32[16,24,128]{2,1,0:T(8,128)S(1)} all-to-all(f32[16,24,128]{2,1,0:T(8,128)S(1)} %get-tuple-element.62), channel_id=1, replica_groups=mesh['inline'=16,'crosslin'=8] {'inline'}, dimensions={0} | all-to-all | bytes 393216 | tf_op jit(solution)/shard_map/all_to_all | solution.py:724
  99.2 3.8 %final_stage.1 = (f32[256,1024]{1,0:T(8,128)}, f32[256,1024]{1,0:T(8,128)}, f32[256,1024]{1,0:T(8,128)}) custom-call(s32[2]{0:T(128)S(1)} %pad_add_fusion.pos, f32[16,24,128]{2,1,0:T(8,128)S(1)} %all_to_all.23.moments, f32[40,1024]{1,0:T(8,128)S(1)} %get-tuple-element.63.own, f32[40,1024]{1,0:T(8,128)S(1)} %copy-done.11, f32[40,1024]{1,0:T(8,128)S(1)} %copy-done.10, ...), custom_call_target="tpu_custom_call" | custom-call | flops 100000000 | bytes 10000000 | tf_op jit(solution)/shard_map/final_stage/pallas_call | solution.py:688
  (42 shorter events, 0.1 us)
Async XLA Ops:
  0.6 6.5 %copy-start.19 = (bf16[2,64,256]{2,1,0:T(8,128)(2,1)S(1)}, bf16[2,64,256]{2,1,0:T(8,128)(2,1)}, u32[]{:S(2)}) copy-start(bf16[2,64,256]{2,1,0:T(8,128)(2,1)} %constant.33.clone.rest_3_) | copy-start | bytes 196612
  4.5 7.7 %copy-start = (bf16[16,256,1024]{2,1,0:T(8,128)(2,1)}, bf16[16,256,1024]{2,1,0:T(8,128)(2,1)S(1)}, u32[]{:S(2)}) copy-start(bf16[16,256,1024]{2,1,0:T(8,128)(2,1)S(1)} %get-tuple-element.35.amp) | copy-start | bytes 25165828
  4.5 9.2 %collective-permute-start = (bf16[256,128]{1,0:T(8,128)(2,1)S(1)}, bf16[256,128]{1,0:T(8,128)(2,1)S(1)}, u32[]{:S(2)}, u32[]{:S(2)}) collective-permute-start(bf16[256,128]{1,0:T(8,128)(2,1)S(1)} %get-tuple-element.36), channel_id=1, source_target_pairs={{0,1},{1,2},{2,3},{3,4},{4,5},{5,6},{6,7},{8,9},{9,10},{10,11},{11... | collective-permute-start | bytes 196616 | tf_op jit(solution)/shard_map/ppermute | solution.py:701
  5.8 7.9 %collective-permute-start.1 = (bf16[256,128]{1,0:T(8,128)(2,1)S(1)}, bf16[256,128]{1,0:T(8,128)(2,1)S(1)}, u32[]{:S(2)}, u32[]{:S(2)}) collective-permute-start(bf16[256,128]{1,0:T(8,128)(2,1)S(1)} %get-tuple-element.37), channel_id=1, source_target_pairs={{1,0},{2,1},{3,2},{4,3},{5,4},{6,5},{7,6},{9,8},{10,9},{11,10},{12... | collective-permute-start | bytes 196616 | tf_op jit(solution)/shard_map/ppermute | solution.py:701
  7.1 6.6 %copy-start.18 = (bf16[2,3,64,128]{3,2,1,0:T(8,128)(2,1)S(1)}, bf16[2,3,64,128]{3,2,1,0:T(8,128)(2,1)}, u32[]{:S(2)}) copy-start(bf16[2,3,64,128]{3,2,1,0:T(8,128)(2,1)} %constant.35.clone.mix) | copy-start | bytes 294916
  7.1 6.6 %copy-start.21 = (bf16[2,128,128]{2,1,0:T(8,128)(2,1)S(1)}, bf16[2,128,128]{2,1,0:T(8,128)(2,1)}, u32[]{:S(2)}) copy-start(bf16[2,128,128]{2,1,0:T(8,128)(2,1)} %constant.36.clone.lanes) | copy-start | bytes 196612
  7.1 21.5 %copy-start.5 = (s32[256,1024]{1,0:T(8,128)S(1)}, s32[256,1024]{1,0:T(8,128)}, u32[]{:S(2)}) copy-start(s32[256,1024]{1,0:T(8,128)} %mask.3) | copy-start | bytes 3145732
  7.1 21.5 %copy-start.7 = (s32[256,1024]{1,0:T(8,128)S(1)}, s32[256,1024]{1,0:T(8,128)}, u32[]{:S(2)}) copy-start(s32[256,1024]{1,0:T(8,128)} %depth.1) | copy-start | bytes 3145732
  13.7 14.9 %copy-start.9 = (bf16[1024,128]{1,0:T(8,128)(2,1)S(1)}, bf16[1024,128]{1,0:T(8,128)(2,1)}, u32[]{:S(2)}) copy-start(bf16[1024,128]{1,0:T(8,128)(2,1)} %constant.37.clone.group) | copy-start | bytes 786436
  14.7 13.9 %collective-permute-start.2 = (bf16[64,1152]{1,0:T(8,128)(2,1)}, bf16[64,1152]{1,0:T(8,128)(2,1)}, u32[]{:S(2)}, u32[]{:S(2)}) collective-permute-start(bf16[64,1152]{1,0:T(8,128)(2,1)} %get-tuple-element.42), channel_id=1, source_target_pairs={{0,8},{8,16},{16,24},{24,32},{32,40},{40,48},{48,56},{56,64},{64,7... | collective-permute-start | bytes 442376 | tf_op jit(solution)/shard_map/ppermute | solution.py:701
  19.3 9.4 %collective-permute-start.3 = (bf16[64,1152]{1,0:T(8,128)(2,1)}, bf16[64,1152]{1,0:T(8,128)(2,1)}, u32[]{:S(2)}, u32[]{:S(2)}) collective-permute-start(bf16[64,1152]{1,0:T(8,128)(2,1)} %get-tuple-element.43), channel_id=1, source_target_pairs={{8,0},{16,8},{24,16},{32,24},{40,32},{48,40},{56,48},{64,56},{72,6... | collective-permute-start | bytes 442376 | tf_op jit(solution)/shard_map/ppermute | solution.py:701
  20.6 3.4 %copy-start.1 = (bf16[16,256,1024]{2,1,0:T(8,128)(2,1)S(1)}, bf16[16,256,1024]{2,1,0:T(8,128)(2,1)}, u32[]{:S(2)}) copy-start(bf16[16,256,1024]{2,1,0:T(8,128)(2,1)} %copy-done) | copy-start | bytes 25165828
  23.9 4.7 %copy-start.2 = (bf16[16,256,1024]{2,1,0:T(8,128)(2,1)S(1)}, bf16[16,256,1024]{2,1,0:T(8,128)(2,1)}, u32[]{:S(2)}) copy-start(bf16[16,256,1024]{2,1,0:T(8,128)(2,1)} %copy-done) | copy-start | bytes 25165828
  28.7 1.0 copy-start.13
  29.7 1.0 copy-start.15
  30.7 0.9 copy-start.16
  31.6 23.9 %copy-start.3 = (bf16[1152,1024]{1,0:T(8,128)(2,1)S(1)}, bf16[1152,1024]{1,0:T(8,128)(2,1)}, u32[]{:S(2)}) copy-start(bf16[1152,1024]{1,0:T(8,128)(2,1)} %constant.39.clone.fwd_lo) | copy-start | bytes 7077892
  31.6 23.9 %copy-start.4 = (bf16[1152,1024]{1,0:T(8,128)(2,1)S(1)}, bf16[1152,1024]{1,0:T(8,128)(2,1)}, u32[]{:S(2)}) copy-start(bf16[1152,1024]{1,0:T(8,128)(2,1)} %constant.38.clone.fwd_hi) | copy-start | bytes 7077892
  31.6 23.9 %copy-start.17 = (f32[8,1024]{1,0:T(8,128)S(1)}, f32[8,1024]{1,0:T(8,128)}, u32[]{:S(2)}) copy-start(f32[8,1024]{1,0:T(8,128)} %constant.40.clone.steps) | copy-start | bytes 98308
  55.6 17.7 %copy-start.8 = (bf16[256,1152]{1,0:T(8,128)(2,1)S(1)}, bf16[256,1152]{1,0:T(8,128)(2,1)}, u32[]{:S(2)}) copy-start(bf16[256,1152]{1,0:T(8,128)(2,1)} %constant.44.clone.spread) | copy-start | bytes 1769476
  55.6 17.6 %copy-start.10 = (f32[40,1024]{1,0:T(8,128)S(1)}, f32[40,1024]{1,0:T(8,128)}, u32[]{:S(2)}) copy-start(f32[40,1024]{1,0:T(8,128)} %constant.42.clone.fall) | copy-start | bytes 491524
  55.6 17.6 %copy-start.11 = (f32[40,1024]{1,0:T(8,128)S(1)}, f32[40,1024]{1,0:T(8,128)}, u32[]{:S(2)}) copy-start(f32[40,1024]{1,0:T(8,128)} %constant.41.clone.grow) | copy-start | bytes 491524
  55.6 17.6 %copy-start.20 = (f32[4,8,128]{2,1,0:T(8,128)S(1)}, f32[4,8,128]{2,1,0:T(8,128)}, u32[]{:S(2)}) copy-start(f32[4,8,128]{2,1,0:T(8,128)} %constant.43.clone.blocks) | copy-start | bytes 49156
  86.7 12.5 %copy-start.6 = (f32[256,1024]{1,0:T(8,128)S(1)}, f32[256,1024]{1,0:T(8,128)}, u32[]{:S(2)}) copy-start(f32[256,1024]{1,0:T(8,128)} %v_in.5) | copy-start | bytes 3145732
  (2 other events, 1.5 us)

commit v5 on v4

--- a/solution.py
+++ b/solution.py
@@ -254,8 +254,18 @@
     if edge:
         v_in, m_in, d_in, rows_t, sii_o, sic_o, scc_o, edge_o, lines_o, v, m, d, end_sems = rest
     else:
-        sii_o, sic_o, scc_o, edge_o = rest
+        sii_o, sic_o, scc_o, edge_o, local, sems = rest
     base = 16 * (first - 1)
+    skip = 0 if edge else 128 - base
+    bounds = [] if edge else [(0, 48), (48, 48), (96, 16 * (steps + 2) - 96)]
+    copies = [
+        pltpu.make_async_copy(amp.at[:, pl.ds(base + r, n)], local.at[:, pl.ds(r, n)], sems.at[i])
+        for i, (r, n) in enumerate(bounds)
+    ]
+    for c in copies:
+        c.start()
+    if not edge:
+        amp, base = local, 0
     if edge:
         more = []
         for side in range(2):
@@ -280,7 +290,7 @@
 
     def edges(t, carry):
         at = pl.ds(pl.multiple_of(16 * t, 16), 16)
-        source = pl.ds(pl.multiple_of(16 * t + 128 * (base > 0), 16), 16)
+        source = pl.ds(pl.multiple_of(16 * t + skip, 16), 16)
         for s in range(K):
             low = moved(amp[s, source, 0:128].astype(F32), 0, 35)
             high = moved(amp[s, source, CD - 128 : CD].astype(F32), 125, 64)
@@ -288,8 +298,14 @@
             edge_o[s, at, :] = tile.astype(BF16)
         return carry
 
-    lax.fori_loop(0, steps, step, 0)
-    lax.fori_loop(0, 8, edges, 0)
+    done = 0
+    for i, (r, n) in enumerate(bounds):
+        copies[i].wait()
+        until = min(steps, (r + n) // 16 - 2)
+        lax.fori_loop(done, until, step, 0)
+        done = until
+    lax.fori_loop(done, steps, step, 0)
+    lax.fori_loop(0, 8, edges, 0, unroll=4)
     if edge:
         for c in more:
             c.wait()
@@ -301,8 +317,8 @@
     hbm, vmem = pl.BlockSpec(memory_space=pltpu.HBM), pl.BlockSpec(memory_space=VMEM)
     flat = jax.ShapeDtypeStruct((16 * steps, CD), F32)
     out_shape = [flat, flat, flat, jax.ShapeDtypeStruct((K, 128, 128), BF16)]
-    scratch = []
-    in_specs = [vmem]
+    scratch = [] if more else [VMEM((K, 16 * (steps + 2), CD), BF16), pltpu.SemaphoreType.DMA((3,))]
+    in_specs = [vmem if more else hbm]
     if more:
         out_shape += [jax.ShapeDtypeStruct((2, MSG, CD), BF16)]
         scratch += [
@@ -316,7 +332,7 @@
         compiler_params=pltpu.CompilerParams(vmem_limit_bytes=14 * 1024 * 1024),
         cost_estimate=pl.CostEstimate(flops=10**8, bytes_accessed=6 * 10**6, transcendentals=0),
         name="inner_stage",
-    )(amplitudes, *(in_hbm(x) for x in more[:3]), *more[3:])
+    )(amplitudes if more else in_hbm(amplitudes), *(in_hbm(x) for x in more[:3]), *more[3:])
 
 
 def block_sums(rows, group):
@@ -422,7 +438,7 @@
             rim_sums[i, pl.ds(pl.multiple_of(at + 16, 16), 32), :] = e
         return carry
 
-    lax.fori_loop(0, RD // 32 - 1, rim_step, 0)
+    lax.fori_loop(0, RD // 32 - 1, rim_step, 0, unroll=7)
 
     for c, (first, steps) in enumerate(cuts):
         sii, sic, scc = inner_refs[4 * c : 4 * c + 3]
@@ -448,7 +464,7 @@
             finish(pl.multiple_of(16 * t + 16, 16), sums)
             return carry
 
-        lax.fori_loop(first, first + steps, step, 0)
+        lax.fori_loop(first, first + steps, step, 0, unroll=7)
 
     def residuals(at, n):
         before = pl.ds(pl.multiple_of(at - 8, 8), n + 8)
@@ -477,7 +493,7 @@
 
     residuals(8, 8)
     residuals(16 + RD, 8)
-    sums_o[...] = lax.fori_loop(0, RD // 16, own, jnp.zeros((8, 128), F32))
+    sums_o[...] = lax.fori_loop(0, RD // 16, own, jnp.zeros((8, 128), F32), unroll=4)
     sums = block_sums(rowsum[...], group[...])
     for j in range(n_cr):
         blocks_o[j] = sums
@@ -490,7 +506,7 @@
     flat = jax.ShapeDtypeStruct((RD, CD), F32)
     return pl.pallas_call(
         functools.partial(tensor_kernel, n_in, n_cr, cuts),
-        in_specs=[pl.BlockSpec(memory_space=pltpu.SMEM), pl.BlockSpec(memory_space=pl.ANY), hbm] + [vmem] * (8 + len(sums)),
+        in_specs=[pl.BlockSpec(memory_space=pltpu.SMEM), hbm, hbm] + [vmem] * (8 + len(sums)),
         out_specs=[vmem] * 8,
         out_shape=[
             ext, ext, ext, ext, flat, flat,
@@ -505,7 +521,7 @@
         compiler_params=pltpu.CompilerParams(vmem_limit_bytes=28 * 1024 * 1024),
         cost_estimate=pl.CostEstimate(flops=10**8, bytes_accessed=2 * 10**7, transcendentals=0),
         name="tensor_stage",
-    )(pos, amp, in_hbm(v), mask, depth, up, down, left, right, put, group, *sums)
+    )(pos, in_hbm(amp), in_hbm(v), mask, depth, up, down, left, right, put, group, *sums)
 
 
 def moments_kernel(n_in, n_cr, extra, blocks, fwd_hi, fwd_lo, steps, pay_o, own_o):
@@ -637,7 +653,7 @@
     strip = field(1)
     above, _ = fluxes(8, 8, jnp.concatenate([field(0), strip], axis=0))
     zero = jnp.zeros((8, 128), F32)
-    pq, qq, _, _ = lax.fori_loop(0, RD // 16, images, (zero, zero, strip, above))
+    pq, qq, _, _ = lax.fori_loop(0, RD // 16, images, (zero, zero, strip, above), unroll=4)
 
     def lanes(x):
         return jnp.sum(x, axis=0, keepdims=True)
@@ -678,7 +694,7 @@
         d_o[at, :] = more * p - step * (q * rd[at, :] + coarse)
         return carry
 
-    lax.fori_loop(0, RD // 16, body, 0)
+    lax.fori_loop(0, RD // 16, body, 0, unroll=4)
 
 
 def coarse_call(kernel, n_in, n_cr, name, out_shape, scratch, pos, moments, own, tables, rest, group=None):
@@ -712,10 +728,10 @@
     (left, right), lines = lax.optimization_barrier(((left, right), lines))
     row_first, row_last = pack_rows(lines, left, right, mix, lanes)
     up, down = neighbours(row_first, row_last, "inline", n_in)
-    inner += inner_stage(*cuts[1], local)
+    inner += inner_stage(*cuts[1], amplitudes)
     group = jnp.asarray(tables["group"])
     ta, tb, tc, z, r, rd, blocks, sums = tensor_stage(
-        n_in, n_cr, cuts, pos, local, iterate, mask, depth, up, down, left, right, put, group, inner
+        n_in, n_cr, cuts, pos, amplitudes, iterate, mask, depth, up, down, left, right, put, group, inner
     )
 
     def moments_of(payload, extra):

time: 103 us -> 91.8 us (0.89)
  local copies, waits for them, and re-layouts: 7.94 us -> 0.1 us
  Pallas kernels: 35.8 us -> 32 us
    unnamed x44 -> x30, local copies, waits for them, and re-layouts: 7.94 us -> 0.1 us
    pallas_call x1, Pallas kernels: 11 us -> 9.06 us  [tensor_stage(): pl.pallas_call(functools.partial(tensor_kernel, n_in, n_cr, cuts), in_spe...]
    pallas_call x2, Pallas kernels: 8.4 us -> 6.62 us  [coarse_call(): pl.pallas_call(functools.partial(kernel, n_in, n_cr), in_specs=[pl.BlockS...]
  transfers between devices with their start and end apart: 4 -> 4, of which waited for: 0 -> 1; matrix products, arithmetic and copies ran while one was open for 0% -> 0% of each run, Pallas kernels for 9% -> 11%
where the time goes in v5:
time: 91.8 us; the launch traced here: 91.5 us
  blocking collectives  50.3 us (55%)
  Pallas kernels  32 us (35%)
  starting transfers between devices  7.81 us (9%)
    all_to_all x2, blocking collectives, moments_of(): return (lax.all_to_all(pay, 'inline', 0, 0, tiled=True), own)  28.7 us
    all_to_all x2, blocking collectives, moments_of(): gathered = lax.all_to_all(payload, 'crosslin', 0, 0, tiled=True)  21.6 us
    pallas_call x2, Pallas kernels, inner_stage(): pl.pallas_call(functools.partial(inner_kernel, first, steps, bool(more)),...  10.2 us
    pallas_call x1, Pallas kernels, tensor_stage(): pl.pallas_call(functools.partial(tensor_kernel, n_in, n_cr, cuts), in_spe...  9.06 us
    pallas_call x2, Pallas kernels, coarse_call(): pl.pallas_call(functools.partial(kernel, n_in, n_cr), in_specs=[pl.BlockS...  6.62 us
    ppermute x2, starting transfers between devices, neighbours(): lax.ppermute(value_high, axis, ahead)  5.23 us
    pallas_call x1, Pallas kernels, pack_columns(): pl.pallas_call(pack_columns_kernel, in_specs=[hbm] * 4, out_specs=[pl.Blo...  3.83 us
    ppermute x2, starting transfers between devices, neighbours(): lax.ppermute(value_low, axis, behind)  2.58 us
  transfers between devices with their start and end apart: 4, of which 1 were waited for; matrix products, arithmetic and copies ran while one was open for 0% of the time, Pallas kernels for 11%

profile of v5, /device:TPU:0, one launch (start us, length us, event | category | flops | bytes accessed | tf_op | source)
XLA Modules:
  0.0 91.5 jit_solution(10546849715373595965)
XLA Ops:
  0.6 0.0 copy-start.12
  0.6 3.8 %pack_columns.1 = (bf16[256,128]{1,0:T(8,128)(2,1)S(1)}, bf16[256,128]{1,0:T(8,128)(2,1)S(1)}, bf16[16,256,1024]{2,1,0:T(8,128)(2,1)S(1)}) custom-call(bf16[16,256,1024]{2,1,0:T(8,128)(2,1)} %amp.5, f32[256,1024]{1,0:T(8,128)} %v_in.5, s32[256,1024]{1,0:T(8,128)} %mask.3, s32[256,1024]{1,0:T(8,128)} %depth.1), custom_call_target="tpu_custom_call" | custom-call | flops 10000000 | bytes 3000000 | tf_op jit(solution)/shard_map/pack_columns/pallas_call | solution.py:182
  4.5 1.3 %collective-permute-start = (bf16[256,128]{1,0:T(8,128)(2,1)S(1)}, bf16[256,128]{1,0:T(8,128)(2,1)S(1)}, u32[]{:S(2)}, u32[]{:S(2)}) collective-permute-start(bf16[256,128]{1,0:T(8,128)(2,1)S(1)} %get-tuple-element.35), channel_id=1, source_target_pairs={{0,1},{1,2},{2,3},{3,4},{4,5},{5,6},{6,7},{8,9},{9,10},{10,11},{11... | collective-permute-start | bytes 196616 | tf_op jit(solution)/shard_map/ppermute | solution.py:717
  5.8 1.3 %collective-permute-start.1 = (bf16[256,128]{1,0:T(8,128)(2,1)S(1)}, bf16[256,128]{1,0:T(8,128)(2,1)S(1)}, u32[]{:S(2)}, u32[]{:S(2)}) collective-permute-start(bf16[256,128]{1,0:T(8,128)(2,1)S(1)} %get-tuple-element.36), channel_id=1, source_target_pairs={{1,0},{2,1},{3,2},{4,3},{5,4},{6,5},{7,6},{9,8},{10,9},{11,10},{12... | collective-permute-start | bytes 196616 | tf_op jit(solution)/shard_map/ppermute | solution.py:717
  7.1 0.0 copy-start.14
  7.1 4.6 %inner_stage.2 = (f32[112,1024]{1,0:T(8,128)S(1)}, f32[112,1024]{1,0:T(8,128)S(1)}, f32[112,1024]{1,0:T(8,128)S(1)}, bf16[16,128,128]{2,1,0:T(8,128)(2,1)S(1)}, bf16[2,64,1024]{2,1,0:T(8,128)(2,1)S(1)}) custom-call(bf16[16,256,1024]{2,1,0:T(8,128)(2,1)S(1)} %get-tuple-element.37.amp, f32[256,1024]{1,0:T(8,128)} %v_in.5, s32[256,1024]{1,0:T(8,128)} %mask.3, ...), custom_call_target="tpu_custom_call" | custom-call | flops 100000000 | bytes 6000000 | tf_op jit(solution)/shard_map/inner_stage/pallas_call | solution.py:329
  11.7 0.2 pack_rows.1
  12.0 3.9 %collective-permute-start.2 = (bf16[64,1152]{1,0:T(8,128)(2,1)S(1)}, bf16[64,1152]{1,0:T(8,128)(2,1)S(1)}, u32[]{:S(2)}, u32[]{:S(2)}) collective-permute-start(bf16[64,1152]{1,0:T(8,128)(2,1)S(1)} %get-tuple-element.42), channel_id=1, source_target_pairs={{0,8},{8,16},{16,24},{24,32},{32,40},{40,48},{48,56},{56,64},{64,7... | collective-permute-start | bytes 442376 | tf_op jit(solution)/shard_map/ppermute | solution.py:717
  15.9 1.3 %collective-permute-start.3 = (bf16[64,1152]{1,0:T(8,128)(2,1)S(1)}, bf16[64,1152]{1,0:T(8,128)(2,1)S(1)}, u32[]{:S(2)}, u32[]{:S(2)}) collective-permute-start(bf16[64,1152]{1,0:T(8,128)(2,1)S(1)} %get-tuple-element.43), channel_id=1, source_target_pairs={{8,0},{16,8},{24,16},{32,24},{40,32},{48,40},{56,48},{64,56},{72,6... | collective-permute-start | bytes 442376 | tf_op jit(solution)/shard_map/ppermute | solution.py:717
  17.2 0.0 copy-start.6
  17.3 0.0 copy-start.9
  17.3 5.7 %inner_stage.3 = (f32[112,1024]{1,0:T(8,128)S(1)}, f32[112,1024]{1,0:T(8,128)S(1)}, f32[112,1024]{1,0:T(8,128)S(1)}, bf16[16,128,128]{2,1,0:T(8,128)(2,1)S(1)}) custom-call(bf16[16,256,1024]{2,1,0:T(8,128)(2,1)} %amp.5), custom_call_target="tpu_custom_call" | custom-call | flops 100000000 | bytes 6000000 | tf_op jit(solution)/shard_map/inner_stage/pallas_call | solution.py:329
  22.9 0.1 pad_add_fusion.pos
  23.0 0.2 collective-permute-done.3.down
  23.3 0.0 copy-start
  23.3 9.1 %tensor_stage.1 = (f32[288,1152]{1,0:T(8,128)S(1)}, f32[288,1152]{1,0:T(8,128)S(1)}, f32[288,1152]{1,0:T(8,128)S(1)}, f32[288,1152]{1,0:T(8,128)S(1)}, f32[256,1...) custom-call(s32[2]{0:T(128)S(1)} %pad_add_fusion.pos, ...), custom_call_target="tpu_custom_call" | custom-call | flops 100000000 | bytes 20000000 | tf_op jit(solution)/shard_map/tensor_stage/pallas_call | solution.py:507
  32.4 12.7 %all_to_all.20.blocks = f32[8,32,128]{2,1,0:T(8,128)S(1)} all-to-all(f32[8,32,128]{2,1,0:T(8,128)S(1)} %get-tuple-element.52.first_blocks), channel_id=1, replica_groups=mesh['inline'=16,'crosslin'=8] {'crosslin'}, dimensions={0} | all-to-all | bytes 262144 | tf_op jit(solution)/shard_map/all_to_all | solution.py:738
  45.2 1.0 %moments_stage.2 = (f32[16,16,128]{2,1,0:T(8,128)S(1)}, f32[40,1024]{1,0:T(8,128)S(1)}) custom-call(f32[8,32,128]{2,1,0:T(8,128)S(1)} %all_to_all.20.blocks, bf16[1152,1024]{1,0:T(8,128)(2,1)S(1)} %copy-done, bf16[1152,1024]{1,0:T(8,128)(2,1)S(1)} %copy-done.1, f32[8,1024]{1,0:T(8,128)S(1)} %copy-done.10), custom_call_target="tpu_custom_call" | custom-call | flops 200000000 | bytes 5000000 | tf_op jit(solution)/shard_map/moments_stage/pallas_call | solution.py:566
  46.2 17.3 %all_to_all.21.moments = f32[16,16,128]{2,1,0:T(8,128)S(1)} all-to-all(f32[16,16,128]{2,1,0:T(8,128)S(1)} %get-tuple-element.53), channel_id=1, replica_groups=mesh['inline'=16,'crosslin'=8] {'inline'}, dimensions={0} | all-to-all | bytes 262144 | tf_op jit(solution)/shard_map/all_to_all | solution.py:740
  63.5 3.2 %image_stage.1 = (f32[256,1024]{1,0:T(8,128)S(1)}, f32[256,1024]{1,0:T(8,128)S(1)}, f32[8,40,128]{2,1,0:T(8,128)S(1)}) custom-call(s32[2]{0:T(128)S(1)} %pad_add_fusion.pos, f32[16,16,128]{2,1,0:T(8,128)S(1)} %all_to_all.21.moments, f32[40,1024]{1,0:T(8,128)S(1)} %get-tuple-element.54.own, f32[40,1024]{1,0:T(8,128)S(1)} %copy-done.7, ...), custom_call_target="tpu_custom_call" | custom-call | flops 100000000 | bytes 10000000 | tf_op jit(solution)/shard_map/image_stage/pallas_call | solution.py:704
  66.7 8.9 %all_to_all.22.blocks = f32[8,40,128]{2,1,0:T(8,128)S(1)} all-to-all(f32[8,40,128]{2,1,0:T(8,128)S(1)} %get-tuple-element.61), channel_id=1, replica_groups=mesh['inline'=16,'crosslin'=8] {'crosslin'}, dimensions={0} | all-to-all | bytes 327680 | tf_op jit(solution)/shard_map/all_to_all | solution.py:738
  75.6 1.0 %moments_stage.3 = (f32[16,24,128]{2,1,0:T(8,128)S(1)}, f32[40,1024]{1,0:T(8,128)S(1)}) custom-call(f32[8,40,128]{2,1,0:T(8,128)S(1)} %all_to_all.22.blocks, bf16[1152,1024]{1,0:T(8,128)(2,1)S(1)} %copy-done, bf16[1152,1024]{1,0:T(8,128)(2,1)S(1)} %copy-done.1, f32[8,1024]{1,0:T(8,128)S(1)} %copy-done.10), custom_call_target="tpu_custom_call" | custom-call | flops 200000000 | bytes 5000000 | tf_op jit(solution)/shard_map/moments_stage/pallas_call | solution.py:566
  76.6 11.4 %all_to_all.23.moments = f32[16,24,128]{2,1,0:T(8,128)S(1)} all-to-all(f32[16,24,128]{2,1,0:T(8,128)S(1)} %get-tuple-element.62), channel_id=1, replica_groups=mesh['inline'=16,'crosslin'=8] {'inline'}, dimensions={0} | all-to-all | bytes 393216 | tf_op jit(solution)/shard_map/all_to_all | solution.py:740
  88.0 3.5 %final_stage.1 = (f32[256,1024]{1,0:T(8,128)}, f32[256,1024]{1,0:T(8,128)}, f32[256,1024]{1,0:T(8,128)}) custom-call(s32[2]{0:T(128)S(1)} %pad_add_fusion.pos, f32[16,24,128]{2,1,0:T(8,128)S(1)} %all_to_all.23.moments, f32[40,1024]{1,0:T(8,128)S(1)} %get-tuple-element.63.own, f32[40,1024]{1,0:T(8,128)S(1)} %copy-done.7, f32[40,1024]{1,0:T(8,128)S(1)} %copy-done.8, ...), custom_call_target="tpu_custom_call" | custom-call | flops 100000000 | bytes 10000000 | tf_op jit(solution)/shard_map/final_stage/pallas_call | solution.py:704
  (28 shorter events, 0.1 us)
Async XLA Ops:
  0.6 6.5 %copy-start.12 = (bf16[2,64,256]{2,1,0:T(8,128)(2,1)S(1)}, bf16[2,64,256]{2,1,0:T(8,128)(2,1)}, u32[]{:S(2)}) copy-start(bf16[2,64,256]{2,1,0:T(8,128)(2,1)} %constant.33.clone.rest_3_) | copy-start | bytes 196612
  4.5 7.2 %collective-permute-start = (bf16[256,128]{1,0:T(8,128)(2,1)S(1)}, bf16[256,128]{1,0:T(8,128)(2,1)S(1)}, u32[]{:S(2)}, u32[]{:S(2)}) collective-permute-start(bf16[256,128]{1,0:T(8,128)(2,1)S(1)} %get-tuple-element.35), channel_id=1, source_target_pairs={{0,1},{1,2},{2,3},{3,4},{4,5},{5,6},{6,7},{8,9},{9,10},{10,11},{11... | collective-permute-start | bytes 196616 | tf_op jit(solution)/shard_map/ppermute | solution.py:717
  5.8 5.9 %collective-permute-start.1 = (bf16[256,128]{1,0:T(8,128)(2,1)S(1)}, bf16[256,128]{1,0:T(8,128)(2,1)S(1)}, u32[]{:S(2)}, u32[]{:S(2)}) collective-permute-start(bf16[256,128]{1,0:T(8,128)(2,1)S(1)} %get-tuple-element.36), channel_id=1, source_target_pairs={{1,0},{2,1},{3,2},{4,3},{5,4},{6,5},{7,6},{9,8},{10,9},{11,10},{12... | collective-permute-start | bytes 196616 | tf_op jit(solution)/shard_map/ppermute | solution.py:717
  7.1 4.6 %copy-start.11 = (bf16[2,3,64,128]{3,2,1,0:T(8,128)(2,1)S(1)}, bf16[2,3,64,128]{3,2,1,0:T(8,128)(2,1)}, u32[]{:S(2)}) copy-start(bf16[2,3,64,128]{3,2,1,0:T(8,128)(2,1)} %constant.35.clone.mix) | copy-start | bytes 294916
  7.1 4.6 %copy-start.14 = (bf16[2,128,128]{2,1,0:T(8,128)(2,1)S(1)}, bf16[2,128,128]{2,1,0:T(8,128)(2,1)}, u32[]{:S(2)}) copy-start(bf16[2,128,128]{2,1,0:T(8,128)(2,1)} %constant.36.clone.lanes) | copy-start | bytes 196612
  12.0 11.1 %collective-permute-start.2 = (bf16[64,1152]{1,0:T(8,128)(2,1)S(1)}, bf16[64,1152]{1,0:T(8,128)(2,1)S(1)}, u32[]{:S(2)}, u32[]{:S(2)}) collective-permute-start(bf16[64,1152]{1,0:T(8,128)(2,1)S(1)} %get-tuple-element.42), channel_id=1, source_target_pairs={{0,8},{8,16},{16,24},{24,32},{32,40},{40,48},{48,56},{56,64},{64,7... | collective-permute-start | bytes 442376 | tf_op jit(solution)/shard_map/ppermute | solution.py:717
  15.9 7.3 %collective-permute-start.3 = (bf16[64,1152]{1,0:T(8,128)(2,1)S(1)}, bf16[64,1152]{1,0:T(8,128)(2,1)S(1)}, u32[]{:S(2)}, u32[]{:S(2)}) collective-permute-start(bf16[64,1152]{1,0:T(8,128)(2,1)S(1)} %get-tuple-element.43), channel_id=1, source_target_pairs={{8,0},{16,8},{24,16},{32,24},{40,32},{48,40},{56,48},{64,56},{72,6... | collective-permute-start | bytes 442376 | tf_op jit(solution)/shard_map/ppermute | solution.py:717
  17.2 6.0 %copy-start.2 = (s32[256,1024]{1,0:T(8,128)S(1)}, s32[256,1024]{1,0:T(8,128)}, u32[]{:S(2)}) copy-start(s32[256,1024]{1,0:T(8,128)} %mask.3) | copy-start | bytes 3145732
  17.2 6.0 %copy-start.4 = (s32[256,1024]{1,0:T(8,128)S(1)}, s32[256,1024]{1,0:T(8,128)}, u32[]{:S(2)}) copy-start(s32[256,1024]{1,0:T(8,128)} %depth.1) | copy-start | bytes 3145732
  17.2 6.0 %copy-start.6 = (bf16[1024,128]{1,0:T(8,128)(2,1)S(1)}, bf16[1024,128]{1,0:T(8,128)(2,1)}, u32[]{:S(2)}) copy-start(bf16[1024,128]{1,0:T(8,128)(2,1)} %constant.37.clone.group) | copy-start | bytes 786436
  17.3 6.0 %copy-start.9 = (bf16[2,304,64]{2,1,0:T(8,128)(2,1)S(1)}, bf16[2,304,64]{2,1,0:T(8,128)(2,1)}, u32[]{:S(2)}) copy-start(bf16[2,304,64]{2,1,0:T(8,128)(2,1)} %constant.34.clone.put) | copy-start | bytes 233476
  23.3 21.8 %copy-start = (bf16[1152,1024]{1,0:T(8,128)(2,1)S(1)}, bf16[1152,1024]{1,0:T(8,128)(2,1)}, u32[]{:S(2)}) copy-start(bf16[1152,1024]{1,0:T(8,128)(2,1)} %constant.38.clone.fwd_hi) | copy-start | bytes 7077892
  23.3 21.8 %copy-start.1 = (bf16[1152,1024]{1,0:T(8,128)(2,1)S(1)}, bf16[1152,1024]{1,0:T(8,128)(2,1)}, u32[]{:S(2)}) copy-start(bf16[1152,1024]{1,0:T(8,128)(2,1)} %constant.39.clone.fwd_lo) | copy-start | bytes 7077892
  23.3 21.8 %copy-start.10 = (f32[8,1024]{1,0:T(8,128)S(1)}, f32[8,1024]{1,0:T(8,128)}, u32[]{:S(2)}) copy-start(f32[8,1024]{1,0:T(8,128)} %constant.40.clone.steps) | copy-start | bytes 98308
  45.1 18.4 %copy-start.5 = (bf16[256,1152]{1,0:T(8,128)(2,1)S(1)}, bf16[256,1152]{1,0:T(8,128)(2,1)}, u32[]{:S(2)}) copy-start(bf16[256,1152]{1,0:T(8,128)(2,1)} %constant.44.clone.spread) | copy-start | bytes 1769476
  45.1 18.3 %copy-start.7 = (f32[40,1024]{1,0:T(8,128)S(1)}, f32[40,1024]{1,0:T(8,128)}, u32[]{:S(2)}) copy-start(f32[40,1024]{1,0:T(8,128)} %constant.41.clone.grow) | copy-start | bytes 491524
  45.1 18.3 %copy-start.8 = (f32[40,1024]{1,0:T(8,128)S(1)}, f32[40,1024]{1,0:T(8,128)}, u32[]{:S(2)}) copy-start(f32[40,1024]{1,0:T(8,128)} %constant.42.clone.fall) | copy-start | bytes 491524
  45.2 18.3 %copy-start.13 = (f32[4,8,128]{2,1,0:T(8,128)S(1)}, f32[4,8,128]{2,1,0:T(8,128)}, u32[]{:S(2)}) copy-start(f32[4,8,128]{2,1,0:T(8,128)} %constant.43.clone.blocks) | copy-start | bytes 49156
  75.5 12.5 %copy-start.3 = (f32[256,1024]{1,0:T(8,128)S(1)}, f32[256,1024]{1,0:T(8,128)}, u32[]{:S(2)}) copy-start(f32[256,1024]{1,0:T(8,128)} %v_in.5) | copy-start | bytes 3145732

commit v6 on v5

--- a/solution.py
+++ b/solution.py
@@ -148,10 +148,14 @@
         copies.append(pltpu.make_async_copy(m_in.at[:, span], m.at[side], sems.at[side, 2]))
         copies.append(pltpu.make_async_copy(d_in.at[:, span], d.at[side], sems.at[side, 3]))
     middle = pl.ds(128, CD - 256)
-    rest = pltpu.make_async_copy(amp.at[:, :, middle], amp_o.at[:, :, middle], rest_sem)
+    rest = [
+        pltpu.make_async_copy(amp.at[:, span, middle], amp_o.at[:, span, middle], rest_sem.at[i])
+        for i, span in enumerate((pl.ds(0, 144), pl.ds(RD - 16, 16)))
+    ]
     for c in copies:
         c.start()
-    rest.start()
+    for c in rest:
+        c.start()
     lane = lax.broadcasted_iota(jnp.int32, (RD, 128), 1)
     for c in copies:
         c.wait()
@@ -173,7 +177,8 @@
         for s in range(K):
             total = jnp.where((lane >= 3 * s) & (lane < 3 * s + 3), moved(edge(s).astype(F32), low, 3 * s), total)
         out[...] = jnp.where(lane < 56, total, 0.0).astype(BF16)
-    rest.wait()
+    for c in rest:
+        c.wait()
 
 
 def pack_columns(amplitudes, iterate, mask, depth):
@@ -185,7 +190,7 @@
         out_shape=[out, out, jax.ShapeDtypeStruct((K, RD, CD), BF16)],
         scratch_shapes=[
             VMEM((2, RD, 128), F32), VMEM((2, RD, 128), jnp.int32),
-            VMEM((2, RD, 128), jnp.int32), pltpu.SemaphoreType.DMA((2, 4)), pltpu.SemaphoreType.DMA,
+            VMEM((2, RD, 128), jnp.int32), pltpu.SemaphoreType.DMA((2, 4)), pltpu.SemaphoreType.DMA((2,)),
         ],
         compiler_params=pltpu.CompilerParams(vmem_limit_bytes=12 * 1024 * 1024),
         cost_estimate=pl.CostEstimate(flops=10**7, bytes_accessed=3 * 10**6, transcendentals=0),
@@ -222,14 +227,14 @@
     return jnp.where(to == at + 1, 1.0, jnp.where(to == at - 1, -1.0, 0.0)).astype(BF16)
 
 
-def gradient_sums(window, band, span, off, take):
+def gradient_sums(window, band, span, off, take, keep=slice(None)):
     total = None
     for s in range(K):
         x = window(s)
         n = x.shape[1]
         middle = x[span]
         gc = pltpu.roll(middle, n - 1, 1).astype(F32) - pltpu.roll(middle, 1, 1).astype(F32)
-        gc = gc[:, off : off + take]
+        gc = gc[keep, off : off + take]
         gi = dot(band, x[:, off : off + take])
         terms = (gi * gi, gi * gc, gc * gc)
         total = terms if total is None else tuple(t + u for t, u in zip(total, terms))
@@ -402,19 +407,19 @@
     def right_of(x):
         return pltpu.roll(x, EC - 1, 1)
 
-    def finish(at, sums):
+    def finish(at, sums, n=16):
         sii, sic, scc = (0.25 * x for x in sums)
         inv = 1.0 / (sii + scc + 2.0)
-        row = pos[0] * RD - 16 + at + row_iota
+        row = pos[0] * RD - 16 + at + row_iota[0:n]
         valid_down = ((row >= 0) & (row < n_in * RD - 1)).astype(F32)
         ta = valid_down * ((scc + 1.0) * inv)
         tb = (valid_down * valid_right) * (-sic * inv)
         tc = valid_right * ((sii + 1.0) * inv)
-        value = v_ext[pl.ds(at, 24), :]
-        here = value[0:16]
-        dd = value[1:17] - here
+        value = v_ext[pl.ds(at, n + 8), :]
+        here = value[0:n]
+        dd = value[1 : n + 1] - here
         dr = right_of(here) - here
-        to = pl.ds(at, 16)
+        to = pl.ds(at, n)
         ta_o[to, :] = ta
         tb_o[to, :] = tb
         tc_o[to, :] = tc
@@ -422,12 +427,13 @@
         fr[to, :] = tb * dd + tc * dr
 
     for side in range(2):
-        for half in range(2):
-            lead = 16 * (side + half)
+        for lead, n in ((8, 8), (16, 16)) if side == 0 else ((16, 16), (32, 8)):
+            tile = slice(lead // 16 * 16, lead // 16 * 16 + 16)
+            keep = slice(lead % 16, lead % 16 + n)
             sums = gradient_sums(
-                lambda s, side=side: tops[side, s], row_band(16, 48, lead), slice(lead, lead + 16), 0, EC
+                lambda s, side=side: tops[side, s], row_band(n, 48, lead), tile, 0, EC, keep
             )
-            finish((RD if side else 0) + 16 * half, sums)
+            finish(lead + side * (RD - 16), sums, n)
 
     wide = row_band(32, 64, 16)
 

time: 91.8 us -> 90.5 us (0.986)
  Pallas kernels: 32 us -> 30.8 us
where the time goes in v6:
time: 90.5 us; the launch traced here: 90.2 us
  blocking collectives  50.3 us (56%)
  Pallas kernels  30.8 us (34%)
  starting transfers between devices  7.81 us (9%)
    all_to_all x2, blocking collectives, moments_of(): return (lax.all_to_all(pay, 'inline', 0, 0, tiled=True), own)  28.7 us
    all_to_all x2, blocking collectives, moments_of(): gathered = lax.all_to_all(payload, 'crosslin', 0, 0, tiled=True)  21.6 us
    pallas_call x2, Pallas kernels, inner_stage(): pl.pallas_call(functools.partial(inner_kernel, first, steps, bool(more)),...  10.2 us
    pallas_call x1, Pallas kernels, tensor_stage(): pl.pallas_call(functools.partial(tensor_kernel, n_in, n_cr, cuts), in_spe...  8.56 us
    pallas_call x2, Pallas kernels, coarse_call(): pl.pallas_call(functools.partial(kernel, n_in, n_cr), in_specs=[pl.BlockS...  6.62 us
    ppermute x2, starting transfers between devices, neighbours(): lax.ppermute(value_high, axis, ahead)  5.22 us
    pallas_call x1, Pallas kernels, pack_columns(): pl.pallas_call(pack_columns_kernel, in_specs=[hbm] * 4, out_specs=[pl.Blo...  3.09 us
    ppermute x2, starting transfers between devices, neighbours(): lax.ppermute(value_low, axis, behind)  2.58 us
  transfers between devices with their start and end apart: 4, of which 1 were waited for; matrix products, arithmetic and copies ran while one was open for 0% of the time, Pallas kernels for 11%

profile of v6, /device:TPU:0, one launch (start us, length us, event | category | flops | bytes accessed | tf_op | source)
XLA Modules:
  0.0 90.2 jit_solution(9622523603033637206)
XLA Ops:
  0.6 0.0 copy-start.12
  0.6 3.1 %pack_columns.1 = (bf16[256,128]{1,0:T(8,128)(2,1)S(1)}, bf16[256,128]{1,0:T(8,128)(2,1)S(1)}, bf16[16,256,1024]{2,1,0:T(8,128)(2,1)S(1)}) custom-call(bf16[16,256,1024]{2,1,0:T(8,128)(2,1)} %amp.5, f32[256,1024]{1,0:T(8,128)} %v_in.5, s32[256,1024]{1,0:T(8,128)} %mask.3, s32[256,1024]{1,0:T(8,128)} %depth.1), custom_call_target="tpu_custom_call" | custom-call | flops 10000000 | bytes 3000000 | tf_op jit(solution)/shard_map/pack_columns/pallas_call | solution.py:187
  3.7 1.3 %collective-permute-start = (bf16[256,128]{1,0:T(8,128)(2,1)S(1)}, bf16[256,128]{1,0:T(8,128)(2,1)S(1)}, u32[]{:S(2)}, u32[]{:S(2)}) collective-permute-start(bf16[256,128]{1,0:T(8,128)(2,1)S(1)} %get-tuple-element.35), channel_id=1, source_target_pairs={{0,1},{1,2},{2,3},{3,4},{4,5},{5,6},{6,7},{8,9},{9,10},{10,11},{11... | collective-permute-start | bytes 196616 | tf_op jit(solution)/shard_map/ppermute | solution.py:723
  5.0 1.3 %collective-permute-start.1 = (bf16[256,128]{1,0:T(8,128)(2,1)S(1)}, bf16[256,128]{1,0:T(8,128)(2,1)S(1)}, u32[]{:S(2)}, u32[]{:S(2)}) collective-permute-start(bf16[256,128]{1,0:T(8,128)(2,1)S(1)} %get-tuple-element.36), channel_id=1, source_target_pairs={{1,0},{2,1},{3,2},{4,3},{5,4},{6,5},{7,6},{9,8},{10,9},{11,10},{12... | collective-permute-start | bytes 196616 | tf_op jit(solution)/shard_map/ppermute | solution.py:723
  6.4 0.0 copy-start.11
  6.4 0.0 copy-start.14
  6.4 4.6 %inner_stage.2 = (f32[112,1024]{1,0:T(8,128)S(1)}, f32[112,1024]{1,0:T(8,128)S(1)}, f32[112,1024]{1,0:T(8,128)S(1)}, bf16[16,128,128]{2,1,0:T(8,128)(2,1)S(1)}, bf16[2,64,1024]{2,1,0:T(8,128)(2,1)S(1)}) custom-call(bf16[16,256,1024]{2,1,0:T(8,128)(2,1)S(1)} %get-tuple-element.37.amp, f32[256,1024]{1,0:T(8,128)} %v_in.5, s32[256,1024]{1,0:T(8,128)} %mask.3, ...), custom_call_target="tpu_custom_call" | custom-call | flops 100000000 | bytes 6000000 | tf_op jit(solution)/shard_map/inner_stage/pallas_call | solution.py:334
  11.0 0.2 pack_rows.1
  11.2 3.9 %collective-permute-start.2 = (bf16[64,1152]{1,0:T(8,128)(2,1)S(1)}, bf16[64,1152]{1,0:T(8,128)(2,1)S(1)}, u32[]{:S(2)}, u32[]{:S(2)}) collective-permute-start(bf16[64,1152]{1,0:T(8,128)(2,1)S(1)} %get-tuple-element.42), channel_id=1, source_target_pairs={{0,8},{8,16},{16,24},{24,32},{32,40},{40,48},{48,56},{56,64},{64,7... | collective-permute-start | bytes 442376 | tf_op jit(solution)/shard_map/ppermute | solution.py:723
  15.2 1.3 %collective-permute-start.3 = (bf16[64,1152]{1,0:T(8,128)(2,1)S(1)}, bf16[64,1152]{1,0:T(8,128)(2,1)S(1)}, u32[]{:S(2)}, u32[]{:S(2)}) collective-permute-start(bf16[64,1152]{1,0:T(8,128)(2,1)S(1)} %get-tuple-element.43), channel_id=1, source_target_pairs={{8,0},{16,8},{24,16},{32,24},{40,32},{48,40},{56,48},{64,56},{72,6... | collective-permute-start | bytes 442376 | tf_op jit(solution)/shard_map/ppermute | solution.py:723
  16.5 0.0 copy-start.6
  16.5 5.7 %inner_stage.3 = (f32[112,1024]{1,0:T(8,128)S(1)}, f32[112,1024]{1,0:T(8,128)S(1)}, f32[112,1024]{1,0:T(8,128)S(1)}, bf16[16,128,128]{2,1,0:T(8,128)(2,1)S(1)}) custom-call(bf16[16,256,1024]{2,1,0:T(8,128)(2,1)} %amp.5), custom_call_target="tpu_custom_call" | custom-call | flops 100000000 | bytes 6000000 | tf_op jit(solution)/shard_map/inner_stage/pallas_call | solution.py:334
  22.2 0.1 pad_add_fusion.pos
  22.3 0.2 collective-permute-done.3.down
  22.6 0.0 copy-start.1
  22.6 8.6 %tensor_stage.1 = (f32[288,1152]{1,0:T(8,128)S(1)}, f32[288,1152]{1,0:T(8,128)S(1)}, f32[288,1152]{1,0:T(8,128)S(1)}, f32[288,1152]{1,0:T(8,128)S(1)}, f32[256,1...) custom-call(s32[2]{0:T(128)S(1)} %pad_add_fusion.pos, ...), custom_call_target="tpu_custom_call" | custom-call | flops 100000000 | bytes 20000000 | tf_op jit(solution)/shard_map/tensor_stage/pallas_call | solution.py:513
  31.1 12.7 %all_to_all.20.blocks = f32[8,32,128]{2,1,0:T(8,128)S(1)} all-to-all(f32[8,32,128]{2,1,0:T(8,128)S(1)} %get-tuple-element.52.first_blocks), channel_id=1, replica_groups=mesh['inline'=16,'crosslin'=8] {'crosslin'}, dimensions={0} | all-to-all | bytes 262144 | tf_op jit(solution)/shard_map/all_to_all | solution.py:744
  43.9 1.0 %moments_stage.2 = (f32[16,16,128]{2,1,0:T(8,128)S(1)}, f32[40,1024]{1,0:T(8,128)S(1)}) custom-call(f32[8,32,128]{2,1,0:T(8,128)S(1)} %all_to_all.20.blocks, bf16[1152,1024]{1,0:T(8,128)(2,1)S(1)} %copy-done, bf16[1152,1024]{1,0:T(8,128)(2,1)S(1)} %copy-done.1, f32[8,1024]{1,0:T(8,128)S(1)} %copy-done.10), custom_call_target="tpu_custom_call" | custom-call | flops 200000000 | bytes 5000000 | tf_op jit(solution)/shard_map/moments_stage/pallas_call | solution.py:572
  44.9 17.3 %all_to_all.21.moments = f32[16,16,128]{2,1,0:T(8,128)S(1)} all-to-all(f32[16,16,128]{2,1,0:T(8,128)S(1)} %get-tuple-element.53), channel_id=1, replica_groups=mesh['inline'=16,'crosslin'=8] {'inline'}, dimensions={0} | all-to-all | bytes 262144 | tf_op jit(solution)/shard_map/all_to_all | solution.py:746
  62.3 3.2 %image_stage.1 = (f32[256,1024]{1,0:T(8,128)S(1)}, f32[256,1024]{1,0:T(8,128)S(1)}, f32[8,40,128]{2,1,0:T(8,128)S(1)}) custom-call(s32[2]{0:T(128)S(1)} %pad_add_fusion.pos, f32[16,16,128]{2,1,0:T(8,128)S(1)} %all_to_all.21.moments, f32[40,1024]{1,0:T(8,128)S(1)} %get-tuple-element.54.own, f32[40,1024]{1,0:T(8,128)S(1)} %copy-done.7, ...), custom_call_target="tpu_custom_call" | custom-call | flops 100000000 | bytes 10000000 | tf_op jit(solution)/shard_map/image_stage/pallas_call | solution.py:710
  65.4 8.9 %all_to_all.22.blocks = f32[8,40,128]{2,1,0:T(8,128)S(1)} all-to-all(f32[8,40,128]{2,1,0:T(8,128)S(1)} %get-tuple-element.61), channel_id=1, replica_groups=mesh['inline'=16,'crosslin'=8] {'crosslin'}, dimensions={0} | all-to-all | bytes 327680 | tf_op jit(solution)/shard_map/all_to_all | solution.py:744
  74.3 1.0 %moments_stage.3 = (f32[16,24,128]{2,1,0:T(8,128)S(1)}, f32[40,1024]{1,0:T(8,128)S(1)}) custom-call(f32[8,40,128]{2,1,0:T(8,128)S(1)} %all_to_all.22.blocks, bf16[1152,1024]{1,0:T(8,128)(2,1)S(1)} %copy-done, bf16[1152,1024]{1,0:T(8,128)(2,1)S(1)} %copy-done.1, f32[8,1024]{1,0:T(8,128)S(1)} %copy-done.10), custom_call_target="tpu_custom_call" | custom-call | flops 200000000 | bytes 5000000 | tf_op jit(solution)/shard_map/moments_stage/pallas_call | solution.py:572
  75.4 11.4 %all_to_all.23.moments = f32[16,24,128]{2,1,0:T(8,128)S(1)} all-to-all(f32[16,24,128]{2,1,0:T(8,128)S(1)} %get-tuple-element.62), channel_id=1, replica_groups=mesh['inline'=16,'crosslin'=8] {'inline'}, dimensions={0} | all-to-all | bytes 393216 | tf_op jit(solution)/shard_map/all_to_all | solution.py:746
  86.8 3.5 %final_stage.1 = (f32[256,1024]{1,0:T(8,128)}, f32[256,1024]{1,0:T(8,128)}, f32[256,1024]{1,0:T(8,128)}) custom-call(s32[2]{0:T(128)S(1)} %pad_add_fusion.pos, f32[16,24,128]{2,1,0:T(8,128)S(1)} %all_to_all.23.moments, f32[40,1024]{1,0:T(8,128)S(1)} %get-tuple-element.63.own, f32[40,1024]{1,0:T(8,128)S(1)} %copy-done.7, f32[40,1024]{1,0:T(8,128)S(1)} %copy-done.8, ...), custom_call_target="tpu_custom_call" | custom-call | flops 100000000 | bytes 10000000 | tf_op jit(solution)/shard_map/final_stage/pallas_call | solution.py:710
  (28 shorter events, 0.1 us)
Async XLA Ops:
  0.6 5.7 %copy-start.12 = (bf16[2,64,256]{2,1,0:T(8,128)(2,1)S(1)}, bf16[2,64,256]{2,1,0:T(8,128)(2,1)}, u32[]{:S(2)}) copy-start(bf16[2,64,256]{2,1,0:T(8,128)(2,1)} %constant.33.clone.rest_3_) | copy-start | bytes 196612
  3.7 7.2 %collective-permute-start = (bf16[256,128]{1,0:T(8,128)(2,1)S(1)}, bf16[256,128]{1,0:T(8,128)(2,1)S(1)}, u32[]{:S(2)}, u32[]{:S(2)}) collective-permute-start(bf16[256,128]{1,0:T(8,128)(2,1)S(1)} %get-tuple-element.35), channel_id=1, source_target_pairs={{0,1},{1,2},{2,3},{3,4},{4,5},{5,6},{6,7},{8,9},{9,10},{10,11},{11... | collective-permute-start | bytes 196616 | tf_op jit(solution)/shard_map/ppermute | solution.py:723
  5.0 5.9 %collective-permute-start.1 = (bf16[256,128]{1,0:T(8,128)(2,1)S(1)}, bf16[256,128]{1,0:T(8,128)(2,1)S(1)}, u32[]{:S(2)}, u32[]{:S(2)}) collective-permute-start(bf16[256,128]{1,0:T(8,128)(2,1)S(1)} %get-tuple-element.36), channel_id=1, source_target_pairs={{1,0},{2,1},{3,2},{4,3},{5,4},{6,5},{7,6},{9,8},{10,9},{11,10},{12... | collective-permute-start | bytes 196616 | tf_op jit(solution)/shard_map/ppermute | solution.py:723
  6.4 4.6 %copy-start.11 = (bf16[2,3,64,128]{3,2,1,0:T(8,128)(2,1)S(1)}, bf16[2,3,64,128]{3,2,1,0:T(8,128)(2,1)}, u32[]{:S(2)}) copy-start(bf16[2,3,64,128]{3,2,1,0:T(8,128)(2,1)} %constant.35.clone.mix) | copy-start | bytes 294916
  6.4 4.6 %copy-start.14 = (bf16[2,128,128]{2,1,0:T(8,128)(2,1)S(1)}, bf16[2,128,128]{2,1,0:T(8,128)(2,1)}, u32[]{:S(2)}) copy-start(bf16[2,128,128]{2,1,0:T(8,128)(2,1)} %constant.36.clone.lanes) | copy-start | bytes 196612
  11.2 11.1 %collective-permute-start.2 = (bf16[64,1152]{1,0:T(8,128)(2,1)S(1)}, bf16[64,1152]{1,0:T(8,128)(2,1)S(1)}, u32[]{:S(2)}, u32[]{:S(2)}) collective-permute-start(bf16[64,1152]{1,0:T(8,128)(2,1)S(1)} %get-tuple-element.42), channel_id=1, source_target_pairs={{0,8},{8,16},{16,24},{24,32},{32,40},{40,48},{48,56},{56,64},{64,7... | collective-permute-start | bytes 442376 | tf_op jit(solution)/shard_map/ppermute | solution.py:723
  15.2 7.3 %collective-permute-start.3 = (bf16[64,1152]{1,0:T(8,128)(2,1)S(1)}, bf16[64,1152]{1,0:T(8,128)(2,1)S(1)}, u32[]{:S(2)}, u32[]{:S(2)}) collective-permute-start(bf16[64,1152]{1,0:T(8,128)(2,1)S(1)} %get-tuple-element.43), channel_id=1, source_target_pairs={{8,0},{16,8},{24,16},{32,24},{40,32},{48,40},{56,48},{64,56},{72,6... | collective-permute-start | bytes 442376 | tf_op jit(solution)/shard_map/ppermute | solution.py:723
  16.5 6.0 %copy-start.2 = (s32[256,1024]{1,0:T(8,128)S(1)}, s32[256,1024]{1,0:T(8,128)}, u32[]{:S(2)}) copy-start(s32[256,1024]{1,0:T(8,128)} %mask.3) | copy-start | bytes 3145732
  16.5 6.0 %copy-start.4 = (s32[256,1024]{1,0:T(8,128)S(1)}, s32[256,1024]{1,0:T(8,128)}, u32[]{:S(2)}) copy-start(s32[256,1024]{1,0:T(8,128)} %depth.1) | copy-start | bytes 3145732
  16.5 6.0 %copy-start.6 = (bf16[1024,128]{1,0:T(8,128)(2,1)S(1)}, bf16[1024,128]{1,0:T(8,128)(2,1)}, u32[]{:S(2)}) copy-start(bf16[1024,128]{1,0:T(8,128)(2,1)} %constant.37.clone.group) | copy-start | bytes 786436
  16.5 6.0 %copy-start.9 = (bf16[2,304,64]{2,1,0:T(8,128)(2,1)S(1)}, bf16[2,304,64]{2,1,0:T(8,128)(2,1)}, u32[]{:S(2)}) copy-start(bf16[2,304,64]{2,1,0:T(8,128)(2,1)} %constant.34.clone.put) | copy-start | bytes 233476
  22.5 21.3 %copy-start = (bf16[1152,1024]{1,0:T(8,128)(2,1)S(1)}, bf16[1152,1024]{1,0:T(8,128)(2,1)}, u32[]{:S(2)}) copy-start(bf16[1152,1024]{1,0:T(8,128)(2,1)} %constant.38.clone.fwd_hi) | copy-start | bytes 7077892
  22.6 21.3 %copy-start.1 = (bf16[1152,1024]{1,0:T(8,128)(2,1)S(1)}, bf16[1152,1024]{1,0:T(8,128)(2,1)}, u32[]{:S(2)}) copy-start(bf16[1152,1024]{1,0:T(8,128)(2,1)} %constant.39.clone.fwd_lo) | copy-start | bytes 7077892
  22.6 21.3 %copy-start.10 = (f32[8,1024]{1,0:T(8,128)S(1)}, f32[8,1024]{1,0:T(8,128)}, u32[]{:S(2)}) copy-start(f32[8,1024]{1,0:T(8,128)} %constant.40.clone.steps) | copy-start | bytes 98308
  43.9 18.4 %copy-start.5 = (bf16[256,1152]{1,0:T(8,128)(2,1)S(1)}, bf16[256,1152]{1,0:T(8,128)(2,1)}, u32[]{:S(2)}) copy-start(bf16[256,1152]{1,0:T(8,128)(2,1)} %constant.44.clone.spread) | copy-start | bytes 1769476
  43.9 18.4 %copy-start.7 = (f32[40,1024]{1,0:T(8,128)S(1)}, f32[40,1024]{1,0:T(8,128)}, u32[]{:S(2)}) copy-start(f32[40,1024]{1,0:T(8,128)} %constant.41.clone.grow) | copy-start | bytes 491524
  43.9 18.3 %copy-start.8 = (f32[40,1024]{1,0:T(8,128)S(1)}, f32[40,1024]{1,0:T(8,128)}, u32[]{:S(2)}) copy-start(f32[40,1024]{1,0:T(8,128)} %constant.42.clone.fall) | copy-start | bytes 491524
  43.9 18.3 %copy-start.13 = (f32[4,8,128]{2,1,0:T(8,128)S(1)}, f32[4,8,128]{2,1,0:T(8,128)}, u32[]{:S(2)}) copy-start(f32[4,8,128]{2,1,0:T(8,128)} %constant.43.clone.blocks) | copy-start | bytes 49156
  74.3 12.5 %copy-start.3 = (f32[256,1024]{1,0:T(8,128)S(1)}, f32[256,1024]{1,0:T(8,128)}, u32[]{:S(2)}) copy-start(f32[256,1024]{1,0:T(8,128)} %v_in.5) | copy-start | bytes 3145732

commit v7 on v6

--- a/solution.py
+++ b/solution.py
@@ -307,9 +307,9 @@
     for i, (r, n) in enumerate(bounds):
         copies[i].wait()
         until = min(steps, (r + n) // 16 - 2)
-        lax.fori_loop(done, until, step, 0)
+        lax.fori_loop(done, until, step, 0, unroll=until - done)
         done = until
-    lax.fori_loop(done, steps, step, 0)
+    lax.fori_loop(done, steps, step, 0, unroll=max(1, steps - done))
     lax.fori_loop(0, 8, edges, 0, unroll=4)
     if edge:
         for c in more:

time: 90.5 us -> 90.2 us (level)
  transfers between devices with their start and end apart: 4 -> 4, of which waited for: 1 -> 1; matrix products, arithmetic and copies ran while one was open for 0% -> 0% of each run, Pallas kernels for 11% -> 10%
where the time goes in v7:
time: 90.2 us; the launch traced here: 89.8 us
  blocking collectives  50.3 us (56%)
  Pallas kernels  29.9 us (33%)
  starting transfers between devices  7.99 us (9%)
    all_to_all x2, blocking collectives, moments_of(): return (lax.all_to_all(pay, 'inline', 0, 0, tiled=True), own)  28.8 us
    all_to_all x2, blocking collectives, moments_of(): gathered = lax.all_to_all(payload, 'crosslin', 0, 0, tiled=True)  21.5 us
    pallas_call x2, Pallas kernels, inner_stage(): pl.pallas_call(functools.partial(inner_kernel, first, steps, bool(more)),...  9.4 us
    pallas_call x1, Pallas kernels, tensor_stage(): pl.pallas_call(functools.partial(tensor_kernel, n_in, n_cr, cuts), in_spe...  8.56 us
    pallas_call x2, Pallas kernels, coarse_call(): pl.pallas_call(functools.partial(kernel, n_in, n_cr), in_specs=[pl.BlockS...  6.62 us
    ppermute x2, starting transfers between devices, neighbours(): lax.ppermute(value_high, axis, ahead)  5.22 us
    pallas_call x1, Pallas kernels, pack_columns(): pl.pallas_call(pack_columns_kernel, in_specs=[hbm] * 4, out_specs=[pl.Blo...  3.09 us
    ppermute x2, starting transfers between devices, neighbours(): lax.ppermute(value_low, axis, behind)  2.76 us
  transfers between devices with their start and end apart: 4, of which 1 were waited for; matrix products, arithmetic and copies ran while one was open for 0% of the time, Pallas kernels for 10%

profile of v7, /device:TPU:0, one launch (start us, length us, event | category | flops | bytes accessed | tf_op | source)
XLA Modules:
  0.0 89.8 jit_solution(9016816779486432093)
XLA Ops:
  0.6 0.0 copy-start.12
  0.6 3.1 %pack_columns.1 = (bf16[256,128]{1,0:T(8,128)(2,1)S(1)}, bf16[256,128]{1,0:T(8,128)(2,1)S(1)}, bf16[16,256,1024]{2,1,0:T(8,128)(2,1)S(1)}) custom-call(bf16[16,256,1024]{2,1,0:T(8,128)(2,1)} %amp.5, f32[256,1024]{1,0:T(8,128)} %v_in.5, s32[256,1024]{1,0:T(8,128)} %mask.3, s32[256,1024]{1,0:T(8,128)} %depth.1), custom_call_target="tpu_custom_call" | custom-call | flops 10000000 | bytes 3000000 | tf_op jit(solution)/shard_map/pack_columns/pallas_call | solution.py:187
  3.7 1.3 %collective-permute-start = (bf16[256,128]{1,0:T(8,128)(2,1)S(1)}, bf16[256,128]{1,0:T(8,128)(2,1)S(1)}, u32[]{:S(2)}, u32[]{:S(2)}) collective-permute-start(bf16[256,128]{1,0:T(8,128)(2,1)S(1)} %get-tuple-element.35), channel_id=1, source_target_pairs={{0,1},{1,2},{2,3},{3,4},{4,5},{5,6},{6,7},{8,9},{9,10},{10,11},{11... | collective-permute-start | bytes 196616 | tf_op jit(solution)/shard_map/ppermute | solution.py:723
  5.0 1.3 %collective-permute-start.1 = (bf16[256,128]{1,0:T(8,128)(2,1)S(1)}, bf16[256,128]{1,0:T(8,128)(2,1)S(1)}, u32[]{:S(2)}, u32[]{:S(2)}) collective-permute-start(bf16[256,128]{1,0:T(8,128)(2,1)S(1)} %get-tuple-element.36), channel_id=1, source_target_pairs={{1,0},{2,1},{3,2},{4,3},{5,4},{6,5},{7,6},{9,8},{10,9},{11,10},{12... | collective-permute-start | bytes 196616 | tf_op jit(solution)/shard_map/ppermute | solution.py:723
  6.4 0.0 copy-start.11
  6.4 0.0 copy-start.14
  6.4 4.2 %inner_stage.2 = (f32[112,1024]{1,0:T(8,128)S(1)}, f32[112,1024]{1,0:T(8,128)S(1)}, f32[112,1024]{1,0:T(8,128)S(1)}, bf16[16,128,128]{2,1,0:T(8,128)(2,1)S(1)}, bf16[2,64,1024]{2,1,0:T(8,128)(2,1)S(1)}) custom-call(bf16[16,256,1024]{2,1,0:T(8,128)(2,1)S(1)} %get-tuple-element.37.amp, f32[256,1024]{1,0:T(8,128)} %v_in.5, s32[256,1024]{1,0:T(8,128)} %mask.3, ...), custom_call_target="tpu_custom_call" | custom-call | flops 100000000 | bytes 6000000 | tf_op jit(solution)/shard_map/inner_stage/pallas_call | solution.py:334
  10.6 0.2 pack_rows.1
  10.8 3.9 %collective-permute-start.2 = (bf16[64,1152]{1,0:T(8,128)(2,1)S(1)}, bf16[64,1152]{1,0:T(8,128)(2,1)S(1)}, u32[]{:S(2)}, u32[]{:S(2)}) collective-permute-start(bf16[64,1152]{1,0:T(8,128)(2,1)S(1)} %get-tuple-element.42), channel_id=1, source_target_pairs={{0,8},{8,16},{16,24},{24,32},{32,40},{40,48},{48,56},{56,64},{64,7... | collective-permute-start | bytes 442376 | tf_op jit(solution)/shard_map/ppermute | solution.py:723
  14.8 1.5 %collective-permute-start.3 = (bf16[64,1152]{1,0:T(8,128)(2,1)S(1)}, bf16[64,1152]{1,0:T(8,128)(2,1)S(1)}, u32[]{:S(2)}, u32[]{:S(2)}) collective-permute-start(bf16[64,1152]{1,0:T(8,128)(2,1)S(1)} %get-tuple-element.43), channel_id=1, source_target_pairs={{8,0},{16,8},{24,16},{32,24},{40,32},{48,40},{56,48},{64,56},{72,6... | collective-permute-start | bytes 442376 | tf_op jit(solution)/shard_map/ppermute | solution.py:723
  16.3 0.0 copy-start.9
  16.3 5.2 %inner_stage.3 = (f32[112,1024]{1,0:T(8,128)S(1)}, f32[112,1024]{1,0:T(8,128)S(1)}, f32[112,1024]{1,0:T(8,128)S(1)}, bf16[16,128,128]{2,1,0:T(8,128)(2,1)S(1)}) custom-call(bf16[16,256,1024]{2,1,0:T(8,128)(2,1)} %amp.5), custom_call_target="tpu_custom_call" | custom-call | flops 100000000 | bytes 6000000 | tf_op jit(solution)/shard_map/inner_stage/pallas_call | solution.py:334
  21.5 0.1 pad_add_fusion.pos
  21.6 0.5 collective-permute-done.3.down
  22.1 0.0 copy-start
  22.2 8.6 %tensor_stage.1 = (f32[288,1152]{1,0:T(8,128)S(1)}, f32[288,1152]{1,0:T(8,128)S(1)}, f32[288,1152]{1,0:T(8,128)S(1)}, f32[288,1152]{1,0:T(8,128)S(1)}, f32[256,1...) custom-call(s32[2]{0:T(128)S(1)} %pad_add_fusion.pos, ...), custom_call_target="tpu_custom_call" | custom-call | flops 100000000 | bytes 20000000 | tf_op jit(solution)/shard_map/tensor_stage/pallas_call | solution.py:513
  30.7 12.6 %all_to_all.20.blocks = f32[8,32,128]{2,1,0:T(8,128)S(1)} all-to-all(f32[8,32,128]{2,1,0:T(8,128)S(1)} %get-tuple-element.52.first_blocks), channel_id=1, replica_groups=mesh['inline'=16,'crosslin'=8] {'crosslin'}, dimensions={0} | all-to-all | bytes 262144 | tf_op jit(solution)/shard_map/all_to_all | solution.py:744
  43.4 1.0 %moments_stage.2 = (f32[16,16,128]{2,1,0:T(8,128)S(1)}, f32[40,1024]{1,0:T(8,128)S(1)}) custom-call(f32[8,32,128]{2,1,0:T(8,128)S(1)} %all_to_all.20.blocks, bf16[1152,1024]{1,0:T(8,128)(2,1)S(1)} %copy-done, bf16[1152,1024]{1,0:T(8,128)(2,1)S(1)} %copy-done.1, f32[8,1024]{1,0:T(8,128)S(1)} %copy-done.10), custom_call_target="tpu_custom_call" | custom-call | flops 200000000 | bytes 5000000 | tf_op jit(solution)/shard_map/moments_stage/pallas_call | solution.py:572
  44.4 17.4 %all_to_all.21.moments = f32[16,16,128]{2,1,0:T(8,128)S(1)} all-to-all(f32[16,16,128]{2,1,0:T(8,128)S(1)} %get-tuple-element.53), channel_id=1, replica_groups=mesh['inline'=16,'crosslin'=8] {'inline'}, dimensions={0} | all-to-all | bytes 262144 | tf_op jit(solution)/shard_map/all_to_all | solution.py:746
  61.9 3.2 %image_stage.1 = (f32[256,1024]{1,0:T(8,128)S(1)}, f32[256,1024]{1,0:T(8,128)S(1)}, f32[8,40,128]{2,1,0:T(8,128)S(1)}) custom-call(s32[2]{0:T(128)S(1)} %pad_add_fusion.pos, f32[16,16,128]{2,1,0:T(8,128)S(1)} %all_to_all.21.moments, f32[40,1024]{1,0:T(8,128)S(1)} %get-tuple-element.54.own, f32[40,1024]{1,0:T(8,128)S(1)} %copy-done.7, ...), custom_call_target="tpu_custom_call" | custom-call | flops 100000000 | bytes 10000000 | tf_op jit(solution)/shard_map/image_stage/pallas_call | solution.py:710
  65.0 8.9 %all_to_all.22.blocks = f32[8,40,128]{2,1,0:T(8,128)S(1)} all-to-all(f32[8,40,128]{2,1,0:T(8,128)S(1)} %get-tuple-element.61), channel_id=1, replica_groups=mesh['inline'=16,'crosslin'=8] {'crosslin'}, dimensions={0} | all-to-all | bytes 327680 | tf_op jit(solution)/shard_map/all_to_all | solution.py:744
  73.9 1.0 %moments_stage.3 = (f32[16,24,128]{2,1,0:T(8,128)S(1)}, f32[40,1024]{1,0:T(8,128)S(1)}) custom-call(f32[8,40,128]{2,1,0:T(8,128)S(1)} %all_to_all.22.blocks, bf16[1152,1024]{1,0:T(8,128)(2,1)S(1)} %copy-done, bf16[1152,1024]{1,0:T(8,128)(2,1)S(1)} %copy-done.1, f32[8,1024]{1,0:T(8,128)S(1)} %copy-done.10), custom_call_target="tpu_custom_call" | custom-call | flops 200000000 | bytes 5000000 | tf_op jit(solution)/shard_map/moments_stage/pallas_call | solution.py:572
  74.9 11.4 %all_to_all.23.moments = f32[16,24,128]{2,1,0:T(8,128)S(1)} all-to-all(f32[16,24,128]{2,1,0:T(8,128)S(1)} %get-tuple-element.62), channel_id=1, replica_groups=mesh['inline'=16,'crosslin'=8] {'inline'}, dimensions={0} | all-to-all | bytes 393216 | tf_op jit(solution)/shard_map/all_to_all | solution.py:746
  86.4 3.5 %final_stage.1 = (f32[256,1024]{1,0:T(8,128)}, f32[256,1024]{1,0:T(8,128)}, f32[256,1024]{1,0:T(8,128)}) custom-call(s32[2]{0:T(128)S(1)} %pad_add_fusion.pos, f32[16,24,128]{2,1,0:T(8,128)S(1)} %all_to_all.23.moments, f32[40,1024]{1,0:T(8,128)S(1)} %get-tuple-element.63.own, f32[40,1024]{1,0:T(8,128)S(1)} %copy-done.7, f32[40,1024]{1,0:T(8,128)S(1)} %copy-done.8, ...), custom_call_target="tpu_custom_call" | custom-call | flops 100000000 | bytes 10000000 | tf_op jit(solution)/shard_map/final_stage/pallas_call | solution.py:710
  (28 shorter events, 0.1 us)
Async XLA Ops:
  0.6 5.7 %copy-start.12 = (bf16[2,64,256]{2,1,0:T(8,128)(2,1)S(1)}, bf16[2,64,256]{2,1,0:T(8,128)(2,1)}, u32[]{:S(2)}) copy-start(bf16[2,64,256]{2,1,0:T(8,128)(2,1)} %constant.33.clone.rest_3_) | copy-start | bytes 196612
  3.7 6.8 %collective-permute-start = (bf16[256,128]{1,0:T(8,128)(2,1)S(1)}, bf16[256,128]{1,0:T(8,128)(2,1)S(1)}, u32[]{:S(2)}, u32[]{:S(2)}) collective-permute-start(bf16[256,128]{1,0:T(8,128)(2,1)S(1)} %get-tuple-element.35), channel_id=1, source_target_pairs={{0,1},{1,2},{2,3},{3,4},{4,5},{5,6},{6,7},{8,9},{9,10},{10,11},{11... | collective-permute-start | bytes 196616 | tf_op jit(solution)/shard_map/ppermute | solution.py:723
  5.0 5.5 %collective-permute-start.1 = (bf16[256,128]{1,0:T(8,128)(2,1)S(1)}, bf16[256,128]{1,0:T(8,128)(2,1)S(1)}, u32[]{:S(2)}, u32[]{:S(2)}) collective-permute-start(bf16[256,128]{1,0:T(8,128)(2,1)S(1)} %get-tuple-element.36), channel_id=1, source_target_pairs={{1,0},{2,1},{3,2},{4,3},{5,4},{6,5},{7,6},{9,8},{10,9},{11,10},{12... | collective-permute-start | bytes 196616 | tf_op jit(solution)/shard_map/ppermute | solution.py:723
  6.4 4.2 %copy-start.11 = (bf16[2,3,64,128]{3,2,1,0:T(8,128)(2,1)S(1)}, bf16[2,3,64,128]{3,2,1,0:T(8,128)(2,1)}, u32[]{:S(2)}) copy-start(bf16[2,3,64,128]{3,2,1,0:T(8,128)(2,1)} %constant.35.clone.mix) | copy-start | bytes 294916
  6.4 4.2 %copy-start.14 = (bf16[2,128,128]{2,1,0:T(8,128)(2,1)S(1)}, bf16[2,128,128]{2,1,0:T(8,128)(2,1)}, u32[]{:S(2)}) copy-start(bf16[2,128,128]{2,1,0:T(8,128)(2,1)} %constant.36.clone.lanes) | copy-start | bytes 196612
  10.8 10.8 %collective-permute-start.2 = (bf16[64,1152]{1,0:T(8,128)(2,1)S(1)}, bf16[64,1152]{1,0:T(8,128)(2,1)S(1)}, u32[]{:S(2)}, u32[]{:S(2)}) collective-permute-start(bf16[64,1152]{1,0:T(8,128)(2,1)S(1)} %get-tuple-element.42), channel_id=1, source_target_pairs={{0,8},{8,16},{16,24},{24,32},{32,40},{40,48},{48,56},{56,64},{64,7... | collective-permute-start | bytes 442376 | tf_op jit(solution)/shard_map/ppermute | solution.py:723
  14.8 7.3 %collective-permute-start.3 = (bf16[64,1152]{1,0:T(8,128)(2,1)S(1)}, bf16[64,1152]{1,0:T(8,128)(2,1)S(1)}, u32[]{:S(2)}, u32[]{:S(2)}) collective-permute-start(bf16[64,1152]{1,0:T(8,128)(2,1)S(1)} %get-tuple-element.43), channel_id=1, source_target_pairs={{8,0},{16,8},{24,16},{32,24},{40,32},{48,40},{56,48},{64,56},{72,6... | collective-permute-start | bytes 442376 | tf_op jit(solution)/shard_map/ppermute | solution.py:723
  16.3 5.9 %copy-start.2 = (s32[256,1024]{1,0:T(8,128)S(1)}, s32[256,1024]{1,0:T(8,128)}, u32[]{:S(2)}) copy-start(s32[256,1024]{1,0:T(8,128)} %mask.3) | copy-start | bytes 3145732
  16.3 5.9 %copy-start.4 = (s32[256,1024]{1,0:T(8,128)S(1)}, s32[256,1024]{1,0:T(8,128)}, u32[]{:S(2)}) copy-start(s32[256,1024]{1,0:T(8,128)} %depth.1) | copy-start | bytes 3145732
  16.3 5.8 %copy-start.6 = (bf16[1024,128]{1,0:T(8,128)(2,1)S(1)}, bf16[1024,128]{1,0:T(8,128)(2,1)}, u32[]{:S(2)}) copy-start(bf16[1024,128]{1,0:T(8,128)(2,1)} %constant.37.clone.group) | copy-start | bytes 786436
  16.3 5.8 %copy-start.9 = (bf16[2,304,64]{2,1,0:T(8,128)(2,1)S(1)}, bf16[2,304,64]{2,1,0:T(8,128)(2,1)}, u32[]{:S(2)}) copy-start(bf16[2,304,64]{2,1,0:T(8,128)(2,1)} %constant.34.clone.put) | copy-start | bytes 233476
  22.1 21.2 %copy-start = (bf16[1152,1024]{1,0:T(8,128)(2,1)S(1)}, bf16[1152,1024]{1,0:T(8,128)(2,1)}, u32[]{:S(2)}) copy-start(bf16[1152,1024]{1,0:T(8,128)(2,1)} %constant.38.clone.fwd_hi) | copy-start | bytes 7077892
  22.1 21.2 %copy-start.1 = (bf16[1152,1024]{1,0:T(8,128)(2,1)S(1)}, bf16[1152,1024]{1,0:T(8,128)(2,1)}, u32[]{:S(2)}) copy-start(bf16[1152,1024]{1,0:T(8,128)(2,1)} %constant.39.clone.fwd_lo) | copy-start | bytes 7077892
  22.2 21.2 %copy-start.10 = (f32[8,1024]{1,0:T(8,128)S(1)}, f32[8,1024]{1,0:T(8,128)}, u32[]{:S(2)}) copy-start(f32[8,1024]{1,0:T(8,128)} %constant.40.clone.steps) | copy-start | bytes 98308
  43.4 18.5 %copy-start.5 = (bf16[256,1152]{1,0:T(8,128)(2,1)S(1)}, bf16[256,1152]{1,0:T(8,128)(2,1)}, u32[]{:S(2)}) copy-start(bf16[256,1152]{1,0:T(8,128)(2,1)} %constant.44.clone.spread) | copy-start | bytes 1769476
  43.4 18.5 %copy-start.7 = (f32[40,1024]{1,0:T(8,128)S(1)}, f32[40,1024]{1,0:T(8,128)}, u32[]{:S(2)}) copy-start(f32[40,1024]{1,0:T(8,128)} %constant.41.clone.grow) | copy-start | bytes 491524
  43.4 18.4 %copy-start.8 = (f32[40,1024]{1,0:T(8,128)S(1)}, f32[40,1024]{1,0:T(8,128)}, u32[]{:S(2)}) copy-start(f32[40,1024]{1,0:T(8,128)} %constant.42.clone.fall) | copy-start | bytes 491524
  43.4 18.4 %copy-start.13 = (f32[4,8,128]{2,1,0:T(8,128)S(1)}, f32[4,8,128]{2,1,0:T(8,128)}, u32[]{:S(2)}) copy-start(f32[4,8,128]{2,1,0:T(8,128)} %constant.43.clone.blocks) | copy-start | bytes 49156
  73.9 12.5 %copy-start.3 = (f32[256,1024]{1,0:T(8,128)S(1)}, f32[256,1024]{1,0:T(8,128)}, u32[]{:S(2)}) copy-start(f32[256,1024]{1,0:T(8,128)} %v_in.5) | copy-start | bytes 3145732
